TPU v7x, 32 devices: a whole 2x2x4 slice. The times are simulated.
32 devices in a mesh: seq: 8 (over z, x), tp: 4 (over y, core).
Axes of the slice: x: 2, y: 2, z: 4, core: 2. Of those that a mesh axis runs over, the one named last changes fastest.
Arguments:
- queries: bfloat16 [2048, 1024], P('seq', 'tp'), may hold values from -6 to 6
- keys: bfloat16 [2048, 1024], P('seq', 'tp'), may hold values from -6 to 6
- values: bfloat16 [2048, 1024], P('seq', 'tp'), may hold values from -6 to 6
- out_weight: bfloat16 [1024, 5120], P('tp'), may hold values from -0.375 to 0.375
- residual: bfloat16 [2048, 5120], P(('seq', 'tp')), may hold values from -3 to 3
- gate: float32 [5120], replicated, may hold values from 0.5 to 1.5
- block_mask: int32 [16, 16], replicated, may hold values from 0 to 1, as said below
Outputs:
- updated: bfloat16 [2048, 5120], P(('seq', 'tp'))
Inputs may be any that keep to these rules, and one draw needn't show every extreme that they name: block_mask[i, j] is 1 wherever |i - j| <= 4. Group the blocks by index of seq, 2 consecutive blocks to an index; where two indices lie more than 2 apart, the rows of one index's query blocks name at most one key block of the other index, and for indices exactly 3 apart this most is always reached.
All inputs are finite; a program needn't handle non-finite values.
Results may differ from a plain program's by a relative error of at most 0.012.
Values may be sent and summed in bfloat16 or wider, within the bound.
No kernel may reach another device: no remote copies, remote signals or barrier semaphores. Data moves between devices by JAX's collectives and lax.ppermute only.
A program may use at most 128 MiB of HBM per device.

v0:
```python
import jax
import jax.numpy as jnp
from jax import lax
from jax.sharding import PartitionSpec as P

HD = 128
BLOCK = 128


NEGATIVE = -1e30


def attend(carry, query_heads, key_piece, value_piece, tile_mask, score_scale):
    old_top, old_total, old_summed = carry
    key_rows = key_piece.shape[0]
    query_rows = query_heads.shape[0]
    local_heads = query_heads.shape[1]
    head_size = query_heads.shape[2]
    key_heads = key_piece.reshape(key_rows, local_heads, head_size)
    value_heads = value_piece.reshape(key_rows, local_heads, head_size)
    scores = (
        jnp.einsum("qhd,khd->hqk", query_heads, key_heads, preferred_element_type=jnp.float32)
        * score_scale
    )
    query_tiles = tile_mask.shape[0]
    key_tiles = tile_mask.shape[1]
    allowed = jnp.broadcast_to(
        (tile_mask > 0)[:, None, :, None],
        (query_tiles, query_rows // query_tiles, key_tiles, key_rows // key_tiles),
    )
    allowed = allowed.reshape(query_rows, key_rows)[None, :, :]
    scores = jnp.where(allowed, scores, NEGATIVE)
    new_top = jnp.maximum(old_top, jnp.max(scores, axis=-1))
    weights = jnp.where(allowed, jnp.exp(scores - new_top[:, :, None]), 0.0)
    new_total = jnp.sum(weights, axis=-1)
    added = jnp.einsum(
        "hqk,khd->qhd",
        weights.astype(jnp.bfloat16),
        value_heads,
        preferred_element_type=jnp.float32,
    )
    return (new_top, new_total, added)


def shards(queries, keys, values, out_weight, residual, gate, block_mask):
    tok_rows = queries.shape[0]
    width = queries.shape[1]
    local_heads = width // HD
    my_blocks = tok_rows // BLOCK
    all_blocks = block_mask.shape[0]
    score_scale = 1.0 / HD**0.5
    seq_place = lax.axis_index("seq")
    query_heads = queries.reshape(tok_rows, local_heads, HD)
    start_carry = (
        jnp.full((local_heads, tok_rows), NEGATIVE, jnp.float32),
        jnp.zeros((local_heads, tok_rows), jnp.float32),
        jnp.zeros((tok_rows, local_heads, HD), jnp.float32),
    )
    mask_rows = lax.dynamic_slice(
        block_mask, (seq_place * my_blocks, jnp.int32(0)), (my_blocks, all_blocks)
    )
    key_piece = lax.all_gather(keys, "seq", axis=0, tiled=True)
    value_piece = lax.all_gather(values, "seq", axis=0, tiled=True)
    row_top, totals, summed = attend(
        start_carry, query_heads, key_piece, value_piece, mask_rows, score_scale
    )
    attended = (
        (summed / jnp.transpose(totals)[:, :, None]).reshape(tok_rows, width).astype(jnp.bfloat16)
    )
    branch = lax.psum_scatter(
        jnp.dot(attended, out_weight, preferred_element_type=jnp.float32).astype(jnp.bfloat16),
        "tp",
        scatter_dimension=0,
        tiled=True,
    ).astype(jnp.float32)
    return (residual.astype(jnp.float32) + gate[None, :] * branch).astype(jnp.bfloat16)


def solution(mesh):
    return jax.shard_map(
        shards,
        mesh=mesh,
        in_specs=(
            P("seq", "tp"),
            P("seq", "tp"),
            P("seq", "tp"),
            P("tp", None),
            P(("seq", "tp"), None),
            P(),
            P(),
        ),
        out_specs=P(("seq", "tp"), None),
        check_vma=False,
    )
```

profile of v0, /device:TPU:0, one launch (start us, length us, event | category | flops | bytes accessed | tf_op | source)
XLA Modules:
  0.0 143.5 jit_solution(10287776268414306620)
XLA Ops:
  6.5 0.0 copy-start
  6.5 0.0 all-gather.3.cloned.1.call-start
  6.5 1.8 %copy.10 = bf16[256,256]{0,1:T(8,128)(2,1)} copy(bf16[256,256]{1,0:T(8,128)(2,1)} %param.8) | data formatting | bytes 262144 | tf_op args[1]
  8.4 0.0 all-gather.3.cloned.1.call-update
  8.4 0.0 all-gather.5.cloned.1.call-start
  8.4 0.7 all-gather.5.cloned.1.call-update
  9.1 0.0 reduce-scatter.2.cloned.1.call-start
  9.2 0.7 dynamic-slice_compare_fusion
  9.9 0.2 broadcast_in_dim.32
  10.1 0.3 copy.24
  10.4 41.3 %all-gather.3.cloned.1.call-done = bf16[2048,256]{0,1:T(8,128)(2,1)} async-done(((bf16[256,256]{0,1:T(8,128)(2,1)}), bf16[2048,256]{0,1:T(8,128)(2,1)}) %all-gather.3.cloned.1.call-update) | async-done | bytes 1048592 | tf_op jit(solution)/shard_map/all_gather | solution.py:62
  51.7 2.4 %fusion = (f32[2,256]{1,0:T(2,128)S(1)}, f32[2,256,2048]{2,1,0:T(8,128)S(1)}) fusion(pred[256,2048]{1,0:T(8,128)(4,1)S(1)} %bitcast.28, bf16[2048,2,128]{0,2,1:T(8,128)(2,1)} %bitcast.33, bf16[256,256]{1,0:T(8,128)(2,1)} %param.7), kind=kOutput, calls=%fused_computation.3 | convolution fusion | flops 271580672 | bytes 5900288 | tf_op jit(solution)/shard_map/qhd,khd->hqk/dot_general | solution.py:22
  54.1 0.0 copy-start.1
  54.1 1.9 %copy-done.1 = f32[2,256,2048]{2,1,0:T(8,128)} copy-done((f32[2,256,2048]{2,1,0:T(8,128)}, f32[2,256,2048]{2,1,0:T(8,128)S(1)}, u32[]{:S(2)}) %copy-start.1) | copy-done | bytes 4194328
  56.1 1.4 fusion.1
  57.5 35.4 %all-gather.5.cloned.1.call-done = bf16[2048,256]{1,0:T(8,128)(2,1)} async-done(((bf16[256,256]{1,0:T(8,128)(2,1)}), bf16[2048,256]{1,0:T(8,128)(2,1)}) %all-gather.5.cloned.1.call-update) | async-done | bytes 1048592 | tf_op jit(solution)/shard_map/all_gather | solution.py:63
  92.9 2.3 %copy.13 = bf16[2048,256]{0,1:T(8,128)(2,1)} copy(bf16[2048,256]{1,0:T(8,128)(2,1)} %all-gather.5.cloned.1.call-done) | data formatting | bytes 2097152 | tf_op jit(solution)/shard_map/all_gather | solution.py:63
  95.1 3.7 %fusion.12 = bf16[256,2,128]{0,2,1:T(8,128)(2,1)S(1)} fusion(bf16[2048,2,128]{0,2,1:T(8,128)(2,1)} %bitcast.32, f32[2,256,2048]{2,1,0:T(8,128)} %copy-done.1, f32[2,256]{1,0:T(2,128)S(1)} %broadcast_maximum_fusion, pred[256,2048]{1,0:T(8,128)(4,1)S(1)} %bitcast.30, f32[256,2]{0,1:T(2,128)S(1)} %bitcast.35), kind=kOutput, calls=%fused_computation.12 | convolution fusion | flops 273809408 | bytes 5902336 | tf_op jit(solution)/shard_map/hqk,khd->qhd/dot_general | solution.py:36
  98.8 0.0 copy-start.2
  98.8 0.0 copy-start.3
  98.8 0.0 copy-done
  98.8 2.4 %convolution_convert_fusion = bf16[256,5120]{1,0:T(8,128)(2,1)} fusion(bf16[256,256]{0,1:T(8,128)(2,1)S(1)} %bitcast.34, bf16[256,5120]{1,0:T(8,128)(2,1)S(1)} %copy-done), kind=kOutput, calls=%fused_computation | convolution fusion | flops 672399360 | bytes 5373952 | tf_op jit(solution)/shard_map/dot_general | solution.py:71
  101.2 0.0 reduce-scatter.2.cloned.1.call-update
  101.2 33.6 %reduce-scatter.2.cloned.1.call-done = bf16[64,5120]{1,0:T(8,128)(2,1)} async-done(((bf16[256,5120]{1,0:T(8,128)(2,1)}), bf16[64,5120]{1,0:T(8,128)(2,1)}) %reduce-scatter.2.cloned.1.call-update) | async-done | bytes 655376 | tf_op jit(solution)/shard_map/reduce_scatter | solution.py:70
  134.8 0.0 copy-done.2
  134.9 0.0 copy-done.3
  134.9 2.1 %add_convert_fusion = bf16[64,5120]{1,0:T(8,128)(2,1)} fusion(bf16[64,5120]{1,0:T(8,128)(2,1)} %reduce-scatter.2.cloned.1.call-done, bf16[64,5120]{1,0:T(8,128)(2,1)S(1)} %copy-done.2, f32[5120]{0:T(1024)S(1)} %copy-done.3), kind=kLoop, calls=%fused_computation.9 | loop fusion | flops 1638400 | bytes 1986560 | tf_op jit(solution)/shard_map/convert_element_type | solution.py:76
  (1 shorter events, 0.0 us)
Async XLA Ops:
  6.5 92.3 %copy-start = (bf16[256,5120]{1,0:T(8,128)(2,1)S(1)}, bf16[256,5120]{1,0:T(8,128)(2,1)}, u32[]{:S(2)}) copy-start(bf16[256,5120]{1,0:T(8,128)(2,1)} %param.10) | copy-start | bytes 7864324
  6.5 45.1 %all-gather.3.cloned.1.call-start = ((), (), s32[]{:S(2)}) async-start(), calls=%async_computation.1 | async-start | bytes 1179648 | tf_op jit(solution)/shard_map/all_gather | solution.py:62
  8.4 84.5 %all-gather.5.cloned.1.call-start = ((), (), s32[]{:S(2)}) async-start(), calls=%async_computation.2 | async-start | bytes 1179648 | tf_op jit(solution)/shard_map/all_gather | solution.py:63
  9.1 125.7 %reduce-scatter.2.cloned.1.call-start = ((), (), s32[]{:S(2)}) async-start(), calls=%async_computation.3 | async-start | bytes 3276800 | tf_op jit(solution)/shard_map/reduce_scatter | solution.py:70
  54.1 1.9 %copy-start.1 = (f32[2,256,2048]{2,1,0:T(8,128)}, f32[2,256,2048]{2,1,0:T(8,128)S(1)}, u32[]{:S(2)}) copy-start(f32[2,256,2048]{2,1,0:T(8,128)S(1)} %get-tuple-element.6) | copy-start | bytes 12582916
  98.8 36.1 %copy-start.2 = (bf16[64,5120]{1,0:T(8,128)(2,1)S(1)}, bf16[64,5120]{1,0:T(8,128)(2,1)}, u32[]{:S(2)}) copy-start(bf16[64,5120]{1,0:T(8,128)(2,1)} %param.11) | copy-start | bytes 1966084
  98.8 36.0 %copy-start.3 = (f32[5120]{0:T(1024)S(1)}, f32[5120]{0:T(1024)}, u32[]{:S(2)}) copy-start(f32[5120]{0:T(1024)} %param.12) | copy-start | bytes 61444
Sparse Core Ops, SparseCore 0:
  9.4 42.2 all-gather.2
  53.8 39.0 all-gather.4
  101.4 33.4 reduce-scatter.1
where the time goes:
time: 144 us
  waiting for transfers between devices  111 us (77%)
  between operations  13.2 us (9%)
  matrix products  8.49 us (6%)
  local copies, waits for them, and re-layouts  6.52 us (5%)
  other arithmetic  4.23 us (3%)
    all_gather x1, waiting for transfers between devices, shards(): key_piece = lax.all_gather(keys, 'seq', axis=0, tiled=True)  41.3 us
    all_gather x1, waiting for transfers between devices, shards(): value_piece = lax.all_gather(values, 'seq', axis=0, tiled=True)  35.4 us
    reduce_scatter x1, waiting for transfers between devices, shards(): lax.psum_scatter(jnp.dot(attended, out_weight, preferred_element_type=jnp...  33.6 us
    unnamed x10, local copies, waits for them, and re-layouts  4.06 us
    dot_general x1, matrix products, attend(): jnp.einsum('hqk,khd->qhd', weights.astype(jnp.bfloat16), value_heads, pre...  3.67 us
  transfers between devices with their start and end apart: 3, of which 3 were waited for; matrix products, arithmetic and copies ran while one was open for 4% of the time, Pallas kernels for 0%

commit v1 on v0

v1 whole, which is shorter than its diff:
```python
import functools
import math

import jax
import jax.numpy as jnp
from jax import lax
from jax.experimental import pallas as pl
from jax.experimental.pallas import tpu as pltpu
from jax.sharding import PartitionSpec as P

HD = 128
BLOCK = 128
NEGATIVE = -1e30
LOG2E = math.log2(math.e)
SCORE_SCALE = LOG2E / HD**0.5
BATCH = 4

VMEM = pltpu.MemorySpace.VMEM
SMEM = pltpu.MemorySpace.SMEM


def in_vmem(count):
    return [pl.BlockSpec(memory_space=VMEM)] * count


def bf16(*shape):
    return jax.ShapeDtypeStruct(shape, jnp.bfloat16)


def f32(*shape):
    return jax.ShapeDtypeStruct(shape, jnp.float32)


def dot(left, right, contract=((1,), (0,))):
    return lax.dot_general(
        left, right, (contract, ((), ())), preferred_element_type=jnp.float32
    )


def pack(half, q, k, v, kv_keep, kv_send, q_keep, q_send):
    rows, width = q.shape
    part = width // 2
    mine = (lax.axis_index("seq") >= half).astype(jnp.int32)
    keep = pl.ds(pl.multiple_of(mine * part, part), part)
    send = pl.ds(pl.multiple_of((1 - mine) * part, part), part)
    for columns, kv, queries in ((keep, kv_keep, q_keep), (send, kv_send, q_send)):
        kv[:rows] = k[:, columns]
        kv[rows:] = v[:, columns]
        queries[...] = q[:, columns]


def attend(half, cores, places, first, last, *refs):
    mask, q_own, q_far = refs[:3]
    pieces = refs[3 : 3 + len(places)]
    rest = refs[3 + len(places) :]
    if not first:
        old_top, old_total, old_summed = rest[:3]
        rest = rest[3:]
    me = lax.axis_index("seq")
    rows = q_own.shape[0]
    blocks = rows // BLOCK
    heads = q_own.shape[1] // HD
    partner = me ^ half
    query_blocks = [me * blocks + a for a in range(blocks)]
    query_blocks += [partner * blocks + a for a in range(blocks)]
    bias = [
        [
            [
                jnp.where(mask[row, (me ^ place) * blocks + b] > 0, 0.0, NEGATIVE)
                for b in range(blocks)
            ]
            for row in query_blocks
        ]
        for place in places
    ]
    outs = []
    for head in range(heads):
        at = slice(head * HD, (head + 1) * HD)
        queries = jnp.concatenate([q_own[:, at], q_far[:, at]], axis=0)
        scores = []
        for n, piece in enumerate(pieces):
            raw = dot(queries, piece[:rows, at], ((1,), (1,)))
            scores.append(
                [
                    [
                        raw[a * BLOCK : (a + 1) * BLOCK, b * BLOCK : (b + 1) * BLOCK]
                        * SCORE_SCALE
                        + bias[n][a][b]
                        for b in range(blocks)
                    ]
                    for a in range(2 * blocks)
                ]
            )
        for a in range(2 * blocks):
            band = slice(a * BLOCK, (a + 1) * BLOCK)
            tiles = [piece[a][b] for piece in scores for b in range(blocks)]
            high = functools.reduce(jnp.maximum, tiles)
            top = jnp.max(high, axis=1, keepdims=True)
            if not first:
                before = old_top[band, at][:, :1]
                top = jnp.maximum(top, before)
                fade = jnp.exp2(before - top)
            weights = [jnp.exp2(tile - top) for tile in tiles]
            total = functools.reduce(jnp.add, weights)
            summed = None
            for n, piece in enumerate(pieces):
                mine = jnp.concatenate(weights[n * blocks : (n + 1) * blocks], axis=1)
                part = dot(mine.astype(jnp.bfloat16), piece[rows:, at])
                summed = part if summed is None else summed + part
            if not first:
                total = total + old_total[band, at] * fade
                summed = summed + old_summed[band, at] * fade
            if last:
                whole = jnp.sum(total, axis=1, keepdims=True)
                outs.append((summed / whole).astype(jnp.bfloat16))
            else:
                new_top, new_total, new_summed = rest
                new_top[band, at] = jnp.broadcast_to(top, (BLOCK, HD))
                new_total[band, at] = total
                new_summed[band, at] = summed
    if not last:
        return
    own_mine, own_other, far_mine, far_other = rest
    core = lax.rem(lax.axis_index("tp"), cores)
    chips = lax.axis_size("tp") // cores
    share = rows // (chips * cores)
    for head in range(heads):
        at = slice(head * HD, (head + 1) * HD)
        whole = jnp.concatenate(outs[head * 2 * blocks : (head + 1) * 2 * blocks], axis=0)
        for base, mine, other in ((0, own_mine, own_other), (rows, far_mine, far_other)):
            for chip in range(chips):
                start = base + chip * cores * share
                one = whole[start : start + share]
                two = whole[start + share : start + 2 * share]
                to = slice(chip * share, (chip + 1) * share)
                mine[to, at] = jnp.where(core == 0, one, two)
                other[to, at] = jnp.where(core == 0, two, one)


def gather_heads(half, own, far, other, far_other, mine_ref, core_ref):
    low = lax.axis_index("seq") < half
    part = own.shape[1]
    own, far, other, far_other = own[...], far[...], other[...], far_other[...]
    mine_ref[:, :part] = jnp.where(low, own, far)
    mine_ref[:, part:] = jnp.where(low, far, own)
    core_ref[:, :part] = jnp.where(low, other, far_other)
    core_ref[:, part:] = jnp.where(low, far_other, other)


def project_peers(half, cores, own, far, other, far_other, weight, core_weight, *rest):
    outs, (mine, core) = rest[:-2], rest[-2:]
    gather_heads(half, own, far, other, far_other, mine, core)
    chips = lax.axis_size("tp") // cores
    chip = lax.axis_index("tp") // cores
    share = own.shape[0] // chips
    for step, out in enumerate(outs, 1):
        place = lax.rem(chip + step, chips)
        rows = pl.ds(pl.multiple_of(place * share, share), share)
        branch = dot(mine[rows], weight[...]) + dot(core[rows], core_weight[...])
        out[...] = branch.astype(jnp.bfloat16)


def project_own(half, cores, own, far, other, far_other, weight, core_weight, out, mine, core):
    gather_heads(half, own, far, other, far_other, mine, core)
    chips = lax.axis_size("tp") // cores
    chip = lax.axis_index("tp") // cores
    share = own.shape[0] // chips
    rows = pl.ds(pl.multiple_of(chip * share, share), share)
    out[...] = dot(mine[rows], weight[...]) + dot(core[rows], core_weight[...])


def finish(residual, gate, own, *rest):
    peers, out = rest[:-1], rest[-1]
    branch = own[...]
    for peer in peers:
        branch = branch + peer[...].astype(jnp.float32)
    out[...] = (residual[...].astype(jnp.float32) + gate[...] * branch).astype(jnp.bfloat16)


def params(mib):
    return pltpu.CompilerParams(vmem_limit_bytes=mib * 2**20)


def shards(queries, keys, values, out_weight, residual, gate, block_mask):
    rows, width = queries.shape
    columns = out_weight.shape[1]
    seq, tp = lax.axis_size("seq"), lax.axis_size("tp")
    half = seq // 2
    cores = 2
    chips = tp // cores
    share = rows // tp
    part = width // 2

    def swap(array, place):
        return lax.ppermute(array, "seq", [(i, i ^ place) for i in range(seq)])

    def across(array, place, core):
        return lax.ppermute(
            array,
            ("seq", "tp"),
            [
                (i * tp + t, (i ^ place) * tp + (t ^ core))
                for i in range(seq)
                for t in range(tp)
            ],
        )

    kv_keep, kv_send, q_keep, q_send = pl.pallas_call(
        functools.partial(pack, half),
        out_shape=[bf16(2 * rows, part)] * 2 + [bf16(rows, part)] * 2,
        in_specs=in_vmem(3),
        out_specs=in_vmem(4),
        compiler_params=params(16),
        name="pack",
    )(queries, keys, values)
    kv_far = swap(kv_send, half)
    order = list(range(half - 1, 0, -1))
    near = {m: swap(kv_keep, m) for m in order}
    q_far = swap(q_send, half)
    far = {m: swap(kv_far, m) for m in order}
    core_weight = lax.ppermute(out_weight, "tp", [(t, t ^ 1) for t in range(tp)])
    pieces = [(0, kv_keep)] + [(m, near[m]) for m in order]
    pieces += [(half, kv_far)] + [(m ^ half, far[m]) for m in order]
    state = []
    for at in range(0, len(pieces), BATCH):
        batch = pieces[at : at + BATCH]
        first, last = at == 0, at + BATCH >= len(pieces)
        if last:
            out_shape = [bf16(rows // cores, part)] * 4
        else:
            out_shape = [f32(2 * rows, part)] * 3
        state = pl.pallas_call(
            functools.partial(attend, half, cores, [m for m, _ in batch], first, last),
            out_shape=out_shape,
            in_specs=[pl.BlockSpec(memory_space=SMEM)] + in_vmem(2 + len(batch) + len(state)),
            out_specs=in_vmem(len(out_shape)),
            compiler_params=params(32),
            name="attend",
        )(block_mask, q_keep, q_far, *[piece for _, piece in batch], *state)
    own_mine, own_other, far_mine, far_other = state
    from_far = across(far_mine, half, 0)
    from_far_core = across(far_other, half, 1)
    from_core = across(own_other, 0, 1)
    heads = (own_mine, from_far, from_core, from_far_core)
    scratch = [pltpu.VMEM((rows // cores, width), jnp.bfloat16)] * 2
    sums = pl.pallas_call(
        functools.partial(project_peers, half, cores),
        out_shape=[bf16(share, columns)] * (chips - 1),
        in_specs=in_vmem(6),
        out_specs=in_vmem(chips - 1),
        scratch_shapes=scratch,
        compiler_params=params(32),
        name="project_peers",
    )(*heads, out_weight, core_weight)
    arrived = [
        lax.ppermute(
            array,
            "tp",
            [(t, (t // cores + step) % chips * cores + t % cores) for t in range(tp)],
        )
        for step, array in enumerate(sums, 1)
    ]
    own = pl.pallas_call(
        functools.partial(project_own, half, cores),
        out_shape=f32(share, columns),
        in_specs=in_vmem(6),
        out_specs=pl.BlockSpec(memory_space=VMEM),
        scratch_shapes=scratch,
        compiler_params=params(32),
        name="project_own",
    )(*heads, out_weight, core_weight)
    return pl.pallas_call(
        finish,
        out_shape=bf16(share, columns),
        in_specs=in_vmem(3 + len(arrived)),
        out_specs=pl.BlockSpec(memory_space=VMEM),
        compiler_params=params(16),
        name="finish",
    )(residual, gate[None, :], own, *arrived)


def solution(mesh):
    return jax.shard_map(
        shards,
        mesh=mesh,
        in_specs=(
            P("seq", "tp"),
            P("seq", "tp"),
            P("seq", "tp"),
            P("tp", None),
            P(("seq", "tp"), None),
            P(),
            P(),
        ),
        out_specs=P(("seq", "tp"), None),
        check_vma=False,
    )
```

time: 144 us -> 59 us (0.41)
  waiting for transfers between devices: 111 us -> 29.1 us
  starting transfers between devices: 0.08 us -> 17.3 us
  between operations: 13.2 us -> 0.06 us
  matrix products: 8.49 us -> 0 us
  Pallas kernels: 0 us -> 7.14 us
  other arithmetic: 4.23 us -> 0 us
    all_gather x2 -> x0, waiting for transfers between devices: 76.7 us -> none  [the longest x1 41.3 us: shards(): key_piece = lax.all_gather(keys, 'seq', axis=0, tiled=True)]
    reduce_scatter x1 -> x0, waiting for transfers between devices: 33.6 us -> none  [shards(): lax.psum_scatter(jnp.dot(attended, out_weight, preferred_element_type=jnp...]
    ppermute x0 -> x13, waiting for transfers between devices: none -> 29.1 us  [the longest x1 14.6 us: shards(): lax.ppermute(array, 'tp', [(t, (t // cores + step) % chips * cores + t %...]
    ppermute x0 -> x13, starting transfers between devices: none -> 17.3 us  [the longest x8 12.1 us: swap(): return lax.ppermute(array, 'seq', [(i, i ^ place) for i in range(seq)])]
    dot_general x3 -> x0, matrix products: 8.49 us -> none  [the longest x1 3.67 us: attend(): jnp.einsum('hqk,khd->qhd', weights.astype(jnp.bfloat16), value_heads, pre...]
    pallas_call x0 -> x6, Pallas kernels: none -> 7.14 us  [the longest x2 3.96 us: shards(): pl.pallas_call(functools.partial(attend, half, cores, [m for m, _ in batc...]
    all_gather x1 -> x0, local copies, waits for them, and re-layouts: 2.26 us -> none  [shards(): value_piece = lax.all_gather(values, 'seq', axis=0, tiled=True)]
    convert_element_type x1 -> x0, other arithmetic: 2.12 us -> none  [shards(): (residual.astype(jnp.float32) + gate[None, :] * branch).astype(jnp.bfloat16)]
  transfers between devices with their start and end apart: 3 -> 13, of which waited for: 3 -> 7; matrix products, arithmetic and copies ran while one was open for 4% -> 0% of each run, Pallas kernels for 0% -> 9%
where the time goes in v1:
time: 59 us; the launch traced here: 58.7 us
  waiting for transfers between devices  29.1 us (49%)
  starting transfers between devices  17.3 us (29%)
  Pallas kernels  7.14 us (12%)
  local copies, waits for them, and re-layouts  5.16 us (9%)
    ppermute x1, waiting for transfers between devices, shards(): lax.ppermute(array, 'tp', [(t, (t // cores + step) % chips * cores + t %...  14.6 us
    ppermute x8, starting transfers between devices, swap(): return lax.ppermute(array, 'seq', [(i, i ^ place) for i in range(seq)])  12.1 us
    ppermute x8, waiting for transfers between devices, swap(): return lax.ppermute(array, 'seq', [(i, i ^ place) for i in range(seq)])  10.5 us
    unnamed x14, local copies, waits for them, and re-layouts  5.16 us
    ppermute x3, waiting for transfers between devices, across(): lax.ppermute(array, ('seq', 'tp'), [(i * tp + t, (i ^ place) * tp + (t ^...  3.99 us
    pallas_call x2, Pallas kernels, shards(): pl.pallas_call(functools.partial(attend, half, cores, [m for m, _ in batc...  3.96 us
    ppermute x3, starting transfers between devices, across(): lax.ppermute(array, ('seq', 'tp'), [(i * tp + t, (i ^ place) * tp + (t ^...  3.1 us
    ppermute x1, starting transfers between devices, shards(): lax.ppermute(array, 'tp', [(t, (t // cores + step) % chips * cores + t %...  1.58 us
  transfers between devices with their start and end apart: 13, of which 7 were waited for; matrix products, arithmetic and copies ran while one was open for 0% of the time, Pallas kernels for 9%

profile of v1, /device:TPU:0, one launch (start us, length us, event | category | flops | bytes accessed | tf_op | source)
XLA Modules:
  0.0 58.7 jit_solution(1416544665554935815)
XLA Ops:
  0.0 0.5 collective-permute-start.11
  0.5 0.0 copy-start.2
  0.5 0.9 %copy-done.2 = bf16[256,256]{1,0:T(8,128)(2,1)S(1)} copy-done((bf16[256,256]{1,0:T(8,128)(2,1)S(1)}, bf16[256,256]{1,0:T(8,128)(2,1)}, u32[]{:S(2)}) %copy-start.2) | copy-done | bytes 131096
  1.4 0.0 copy-start.3
  1.4 0.9 %copy-done.3 = bf16[256,256]{1,0:T(8,128)(2,1)S(1)} copy-done((bf16[256,256]{1,0:T(8,128)(2,1)S(1)}, bf16[256,256]{1,0:T(8,128)(2,1)}, u32[]{:S(2)}) %copy-start.3) | copy-done | bytes 131096
  2.3 0.0 copy-start.4
  2.3 0.9 %copy-done.4 = bf16[256,256]{1,0:T(8,128)(2,1)S(1)} copy-done((bf16[256,256]{1,0:T(8,128)(2,1)S(1)}, bf16[256,256]{1,0:T(8,128)(2,1)}, u32[]{:S(2)}) %copy-start.4) | copy-done | bytes 131096
  3.2 0.1 pack.1
  3.2 3.7 %collective-permute-start.1 = (bf16[512,128]{1,0:T(8,128)(2,1)S(1)}, bf16[512,128]{1,0:T(8,128)(2,1)S(1)}, u32[]{:S(2)}, u32[]{:S(2)}) collective-permute-start(bf16[512,128]{1,0:T(8,128)(2,1)S(1)} %get-tuple-element.18), channel_id=1, source_target_pairs={{0,16},{4,20},{8,24},{12,28},{16,0},{20,4},{24,8},{28,12},{1,17},{... | collective-permute-start | bytes 393224 | tf_op jit(solution)/shard_map/ppermute | solution.py:195
  6.9 1.5 %collective-permute-start.7 = (bf16[512,128]{1,0:T(8,128)(2,1)S(1)}, bf16[512,128]{1,0:T(8,128)(2,1)S(1)}, u32[]{:S(2)}, u32[]{:S(2)}) collective-permute-start(bf16[512,128]{1,0:T(8,128)(2,1)S(1)} %get-tuple-element.19.refs_3_), channel_id=1, source_target_pairs={{0,4},{4,0},{8,12},{12,8},{16,20},{20,16},{24,28},{28,24},{1,5},{5... | collective-permute-start | bytes 393224 | tf_op jit(solution)/shard_map/ppermute | solution.py:195
  8.4 1.6 %collective-permute-start.6 = (bf16[512,128]{1,0:T(8,128)(2,1)S(1)}, bf16[512,128]{1,0:T(8,128)(2,1)S(1)}, u32[]{:S(2)}, u32[]{:S(2)}) collective-permute-start(bf16[512,128]{1,0:T(8,128)(2,1)S(1)} %get-tuple-element.19.refs_3_), channel_id=1, source_target_pairs={{0,8},{4,12},{8,0},{12,4},{16,24},{20,28},{24,16},{28,20},{1,9},{5... | collective-permute-start | bytes 393224 | tf_op jit(solution)/shard_map/ppermute | solution.py:195
  10.0 0.3 collective-permute-start
  10.3 6.5 %collective-permute-done.refs_2_ = bf16[256,128]{1,0:T(8,128)(2,1)S(1)} collective-permute-done((bf16[256,128]{1,0:T(8,128)(2,1)S(1)}, bf16[256,128]{1,0:T(8,128)(2,1)S(1)}, u32[]{:S(2)}, u32[]{:S(2)}) %collective-permute-start) | collective-permute-done | bytes 65568 | tf_op jit(solution)/shard_map/ppermute | solution.py:195
  16.8 1.6 %collective-permute-start.5 = (bf16[512,128]{1,0:T(8,128)(2,1)S(1)}, bf16[512,128]{1,0:T(8,128)(2,1)S(1)}, u32[]{:S(2)}, u32[]{:S(2)}) collective-permute-start(bf16[512,128]{1,0:T(8,128)(2,1)S(1)} %get-tuple-element.19.refs_3_), channel_id=1, source_target_pairs={{0,12},{4,8},{8,4},{12,0},{16,28},{20,24},{24,20},{28,16},{1,13},{... | collective-permute-start | bytes 393224 | tf_op jit(solution)/shard_map/ppermute | solution.py:195
  18.4 0.0 collective-permute-done.1.refs_3_
  18.4 0.6 collective-permute-start.4
  18.9 0.0 collective-permute-done.7.refs_6_
  18.9 1.3 %collective-permute-start.3 = (bf16[512,128]{1,0:T(8,128)(2,1)S(1)}, bf16[512,128]{1,0:T(8,128)(2,1)S(1)}, u32[]{:S(2)}, u32[]{:S(2)}) collective-permute-start(bf16[512,128]{1,0:T(8,128)(2,1)S(1)} %collective-permute-done.1.refs_3_), channel_id=1, source_target_pairs={{0,8},{4,12},{8,0},{12,4},{16,24},{20,28},{24,16},{28,20},{1,9},{5... | collective-permute-start | bytes 393224 | tf_op jit(solution)/shard_map/ppermute | solution.py:195
  20.3 0.0 collective-permute-done.6.refs_5_
  20.3 1.6 %collective-permute-start.2 = (bf16[512,128]{1,0:T(8,128)(2,1)S(1)}, bf16[512,128]{1,0:T(8,128)(2,1)S(1)}, u32[]{:S(2)}, u32[]{:S(2)}) collective-permute-start(bf16[512,128]{1,0:T(8,128)(2,1)S(1)} %collective-permute-done.1.refs_3_), channel_id=1, source_target_pairs={{0,12},{4,8},{8,4},{12,0},{16,28},{20,24},{24,20},{28,16},{1,13},{... | collective-permute-start | bytes 393224 | tf_op jit(solution)/shard_map/ppermute | solution.py:195
  21.9 1.6 %collective-permute-done.5.refs_4_ = bf16[512,128]{1,0:T(8,128)(2,1)S(1)} collective-permute-done((bf16[512,128]{1,0:T(8,128)(2,1)S(1)}, bf16[512,128]{1,0:T(8,128)(2,1)S(1)}, u32[]{:S(2)}, u32[]{:S(2)}) %collective-permute-start.5) | collective-permute-done | bytes 131104 | tf_op jit(solution)/shard_map/ppermute | solution.py:195
  23.4 0.0 copy-start.5
  23.4 0.7 %copy-done.5 = s32[16,16]{1,0:T(8,128)S(1)} copy-done((s32[16,16]{1,0:T(8,128)S(1)}, s32[16,16]{1,0:T(8,128)}, u32[]{:S(2)}) %copy-start.5) | copy-done | bytes 1048
  24.1 1.7 %attend.2 = (f32[512,128]{1,0:T(8,128)S(1)}, f32[512,128]{1,0:T(8,128)S(1)}, f32[512,128]{1,0:T(8,128)S(1)}) custom-call(s32[16,16]{1,0:T(8,128)S(1)} %copy-done.5, bf16[256,128]{1,0:T(8,128)(2,1)S(1)} %get-tuple-element.16.refs_1_, bf16[256,128]{1,0:T(8,128)(2,1)S(1)} %collective-permute-done.refs_2_, bf16[512,128]{1,0:T(8,128)(2,1)S(1)} %get-tuple-element.19.refs_3_, ...), custom_call_target="tpu_custom_call" | custom-call | tf_op jit(solution)/shard_map/attend/pallas_call | solution.py:232
  25.8 0.0 collective-permute-done.4.refs_6_
  25.8 0.8 %collective-permute-done.3.refs_5_ = bf16[512,128]{1,0:T(8,128)(2,1)S(1)} collective-permute-done((bf16[512,128]{1,0:T(8,128)(2,1)S(1)}, bf16[512,128]{1,0:T(8,128)(2,1)S(1)}, u32[]{:S(2)}, u32[]{:S(2)}) %collective-permute-start.3) | collective-permute-done | bytes 131104 | tf_op jit(solution)/shard_map/ppermute | solution.py:195
  26.6 1.6 %collective-permute-done.2.refs_4_ = bf16[512,128]{1,0:T(8,128)(2,1)S(1)} collective-permute-done((bf16[512,128]{1,0:T(8,128)(2,1)S(1)}, bf16[512,128]{1,0:T(8,128)(2,1)S(1)}, u32[]{:S(2)}, u32[]{:S(2)}) %collective-permute-start.2) | collective-permute-done | bytes 131104 | tf_op jit(solution)/shard_map/ppermute | solution.py:195
  28.3 2.3 %attend.3 = (bf16[128,128]{1,0:T(8,128)(2,1)S(1)}, bf16[128,128]{1,0:T(8,128)(2,1)S(1)}, bf16[128,128]{1,0:T(8,128)(2,1)S(1)}, bf16[128,128]{1,0:T(8,128)(2,1)S(1)}) custom-call(s32[16,16]{1,0:T(8,128)S(1)} %copy-done.5, bf16[256,128]{1,0:T(8,128)(2,1)S(1)} %get-tuple-element.16.refs_1_, bf16[256,128]{1,0:T(8,128)(2,1)S(1)} %collective-permute-done.refs_2_, ...), custom_call_target="tpu_custom_call" | custom-call | tf_op jit(solution)/shard_map/attend/pallas_call | solution.py:232
  30.5 2.9 %collective-permute-start.8 = (bf16[128,128]{1,0:T(8,128)(2,1)S(1)}, bf16[128,128]{1,0:T(8,128)(2,1)S(1)}, u32[]{:S(2)}, u32[]{:S(2)}) collective-permute-start(bf16[128,128]{1,0:T(8,128)(2,1)S(1)} %get-tuple-element.24), channel_id=1, source_target_pairs={{0,16},{1,17},{2,18},{3,19},{4,20},{5,21},{6,22},{7,23},{8,24},{9,... | collective-permute-start | bytes 98312 | tf_op jit(solution)/shard_map/ppermute | solution.py:198
  33.4 0.0 collective-permute-start.9
  33.4 0.2 collective-permute-start.10
  33.6 1.8 %collective-permute-done.8.far = bf16[128,128]{1,0:T(8,128)(2,1)S(1)} collective-permute-done((bf16[128,128]{1,0:T(8,128)(2,1)S(1)}, bf16[128,128]{1,0:T(8,128)(2,1)S(1)}, u32[]{:S(2)}, u32[]{:S(2)}) %collective-permute-start.8) | collective-permute-done | bytes 32800 | tf_op jit(solution)/shard_map/ppermute | solution.py:198
  35.4 0.0 collective-permute-done.9.other
  35.4 2.2 %collective-permute-done.10.far_other = bf16[128,128]{1,0:T(8,128)(2,1)S(1)} collective-permute-done((bf16[128,128]{1,0:T(8,128)(2,1)S(1)}, bf16[128,128]{1,0:T(8,128)(2,1)S(1)}, u32[]{:S(2)}, u32[]{:S(2)}) %collective-permute-start.10) | collective-permute-done | bytes 32800 | tf_op jit(solution)/shard_map/ppermute | solution.py:198
  37.6 0.0 collective-permute-done.11.core_weight
  37.6 0.0 copy-start
  37.6 1.7 %copy-done = bf16[256,5120]{1,0:T(8,128)(2,1)S(1)} copy-done((bf16[256,5120]{1,0:T(8,128)(2,1)S(1)}, bf16[256,5120]{1,0:T(8,128)(2,1)}, u32[]{:S(2)}) %copy-start) | copy-done | bytes 2621464
  39.4 1.0 %project_peers.1 = bf16[64,5120]{1,0:T(8,128)(2,1)S(1)} custom-call(bf16[128,128]{1,0:T(8,128)(2,1)S(1)} %get-tuple-element.23.own, bf16[128,128]{1,0:T(8,128)(2,1)S(1)} %collective-permute-done.8.far, bf16[128,128]{1,0:T(8,128)(2,1)S(1)} %collective-permute-done.9.other, bf16[128,128]{1,0:T(8,128)(2,1)S(1)} %collective-permute-done.10.far_other, ...), custom_call_target="tpu_custom_call" | custom-call | tf_op jit(solution)/shard_map/project_peers/pallas_call | solution.py:246
  40.4 0.0 copy-start.1
  40.4 0.0 copy-start.6
  40.4 1.6 %collective-permute-start.12 = (bf16[64,5120]{1,0:T(8,128)(2,1)S(1)}, bf16[64,5120]{1,0:T(8,128)(2,1)S(1)}, u32[]{:S(2)}, u32[]{:S(2)}) collective-permute-start(bf16[64,5120]{1,0:T(8,128)(2,1)S(1)} %project_peers.1), channel_id=1, source_target_pairs={{0,2},{1,3},{2,0},{3,1},{4,6},{5,7},{6,4},{7,5},{8,10},{9,11},{10,... | collective-permute-start | bytes 1966088 | tf_op jit(solution)/shard_map/ppermute | solution.py:256
  42.0 1.0 %project_own.1.own = f32[64,5120]{1,0:T(8,128)S(1)} custom-call(bf16[128,128]{1,0:T(8,128)(2,1)S(1)} %get-tuple-element.23.own, bf16[128,128]{1,0:T(8,128)(2,1)S(1)} %collective-permute-done.8.far, bf16[128,128]{1,0:T(8,128)(2,1)S(1)} %collective-permute-done.9.other, bf16[128,128]{1,0:T(8,128)(2,1)S(1)} %collective-permute-done.10.far_other, ...), custom_call_target="tpu_custom_call" | custom-call | tf_op jit(solution)/shard_map/project_own/pallas_call | solution.py:263
  43.0 14.6 %collective-permute-done.12.rest_0_ = bf16[64,5120]{1,0:T(8,128)(2,1)S(1)} collective-permute-done((bf16[64,5120]{1,0:T(8,128)(2,1)S(1)}, bf16[64,5120]{1,0:T(8,128)(2,1)S(1)}, u32[]{:S(2)}, u32[]{:S(2)}) %collective-permute-start.12) | collective-permute-done | bytes 655392 | tf_op jit(solution)/shard_map/ppermute | solution.py:256
  57.6 0.0 copy-done.1
  57.7 0.0 copy-done.6
  57.7 1.1 %finish.1 = bf16[64,5120]{1,0:T(8,128)(2,1)} custom-call(bf16[64,5120]{1,0:T(8,128)(2,1)S(1)} %copy-done.1, f32[1,5120]{1,0:T(1,128)S(1)} %bitcast.1, f32[64,5120]{1,0:T(8,128)S(1)} %project_own.1.own, bf16[64,5120]{1,0:T(8,128)(2,1)S(1)} %collective-permute-done.12.rest_0_), custom_call_target="tpu_custom_call" | custom-call | tf_op jit(solution)/shard_map/finish/pallas_call | solution.py:272
Async XLA Ops:
  0.0 37.6 %collective-permute-start.11 = (bf16[256,5120]{1,0:T(8,128)(2,1)}, bf16[256,5120]{1,0:T(8,128)(2,1)S(1)}, u32[]{:S(2)}, u32[]{:S(2)}) collective-permute-start(bf16[256,5120]{1,0:T(8,128)(2,1)} %weight.3), channel_id=1, source_target_pairs={{0,1},{1,0},{2,3},{3,2},{4,5},{5,4},{6,7},{7,6},{8,9},{9,8},{10,11... | collective-permute-start | bytes 7864328 | tf_op jit(solution)/shard_map/ppermute | solution.py:221
  0.5 0.9 %copy-start.2 = (bf16[256,256]{1,0:T(8,128)(2,1)S(1)}, bf16[256,256]{1,0:T(8,128)(2,1)}, u32[]{:S(2)}) copy-start(bf16[256,256]{1,0:T(8,128)(2,1)} %q.1) | copy-start | bytes 393220
  1.4 0.9 %copy-start.3 = (bf16[256,256]{1,0:T(8,128)(2,1)S(1)}, bf16[256,256]{1,0:T(8,128)(2,1)}, u32[]{:S(2)}) copy-start(bf16[256,256]{1,0:T(8,128)(2,1)} %k.1) | copy-start | bytes 393220
  2.3 0.9 %copy-start.4 = (bf16[256,256]{1,0:T(8,128)(2,1)S(1)}, bf16[256,256]{1,0:T(8,128)(2,1)}, u32[]{:S(2)}) copy-start(bf16[256,256]{1,0:T(8,128)(2,1)} %v.1) | copy-start | bytes 393220
  3.2 15.1 %collective-permute-start.1 = (bf16[512,128]{1,0:T(8,128)(2,1)S(1)}, bf16[512,128]{1,0:T(8,128)(2,1)S(1)}, u32[]{:S(2)}, u32[]{:S(2)}) collective-permute-start(bf16[512,128]{1,0:T(8,128)(2,1)S(1)} %get-tuple-element.18), channel_id=1, source_target_pairs={{0,16},{4,20},{8,24},{12,28},{16,0},{20,4},{24,8},{28,12},{1,17},{... | collective-permute-start | bytes 393224 | tf_op jit(solution)/shard_map/ppermute | solution.py:195
  6.9 12.0 %collective-permute-start.7 = (bf16[512,128]{1,0:T(8,128)(2,1)S(1)}, bf16[512,128]{1,0:T(8,128)(2,1)S(1)}, u32[]{:S(2)}, u32[]{:S(2)}) collective-permute-start(bf16[512,128]{1,0:T(8,128)(2,1)S(1)} %get-tuple-element.19.refs_3_), channel_id=1, source_target_pairs={{0,4},{4,0},{8,12},{12,8},{16,20},{20,16},{24,28},{28,24},{1,5},{5... | collective-permute-start | bytes 393224 | tf_op jit(solution)/shard_map/ppermute | solution.py:195
  8.4 11.9 %collective-permute-start.6 = (bf16[512,128]{1,0:T(8,128)(2,1)S(1)}, bf16[512,128]{1,0:T(8,128)(2,1)S(1)}, u32[]{:S(2)}, u32[]{:S(2)}) collective-permute-start(bf16[512,128]{1,0:T(8,128)(2,1)S(1)} %get-tuple-element.19.refs_3_), channel_id=1, source_target_pairs={{0,8},{4,12},{8,0},{12,4},{16,24},{20,28},{24,16},{28,20},{1,9},{5... | collective-permute-start | bytes 393224 | tf_op jit(solution)/shard_map/ppermute | solution.py:195
  10.0 6.8 %collective-permute-start = (bf16[256,128]{1,0:T(8,128)(2,1)S(1)}, bf16[256,128]{1,0:T(8,128)(2,1)S(1)}, u32[]{:S(2)}, u32[]{:S(2)}) collective-permute-start(bf16[256,128]{1,0:T(8,128)(2,1)S(1)} %get-tuple-element.17), channel_id=1, source_target_pairs={{0,16},{4,20},{8,24},{12,28},{16,0},{20,4},{24,8},{28,12},{1,17},{... | collective-permute-start | bytes 196616 | tf_op jit(solution)/shard_map/ppermute | solution.py:195
  16.8 6.7 %collective-permute-start.5 = (bf16[512,128]{1,0:T(8,128)(2,1)S(1)}, bf16[512,128]{1,0:T(8,128)(2,1)S(1)}, u32[]{:S(2)}, u32[]{:S(2)}) collective-permute-start(bf16[512,128]{1,0:T(8,128)(2,1)S(1)} %get-tuple-element.19.refs_3_), channel_id=1, source_target_pairs={{0,12},{4,8},{8,4},{12,0},{16,28},{20,24},{24,20},{28,16},{1,13},{... | collective-permute-start | bytes 393224 | tf_op jit(solution)/shard_map/ppermute | solution.py:195
  18.4 7.5 %collective-permute-start.4 = (bf16[512,128]{1,0:T(8,128)(2,1)S(1)}, bf16[512,128]{1,0:T(8,128)(2,1)S(1)}, u32[]{:S(2)}, u32[]{:S(2)}) collective-permute-start(bf16[512,128]{1,0:T(8,128)(2,1)S(1)} %collective-permute-done.1.refs_3_), channel_id=1, source_target_pairs={{0,4},{4,0},{8,12},{12,8},{16,20},{20,16},{24,28},{28,24},{1,5},{5... | collective-permute-start | bytes 393224 | tf_op jit(solution)/shard_map/ppermute | solution.py:195
  18.9 7.7 %collective-permute-start.3 = (bf16[512,128]{1,0:T(8,128)(2,1)S(1)}, bf16[512,128]{1,0:T(8,128)(2,1)S(1)}, u32[]{:S(2)}, u32[]{:S(2)}) collective-permute-start(bf16[512,128]{1,0:T(8,128)(2,1)S(1)} %collective-permute-done.1.refs_3_), channel_id=1, source_target_pairs={{0,8},{4,12},{8,0},{12,4},{16,24},{20,28},{24,16},{28,20},{1,9},{5... | collective-permute-start | bytes 393224 | tf_op jit(solution)/shard_map/ppermute | solution.py:195
  20.3 8.0 %collective-permute-start.2 = (bf16[512,128]{1,0:T(8,128)(2,1)S(1)}, bf16[512,128]{1,0:T(8,128)(2,1)S(1)}, u32[]{:S(2)}, u32[]{:S(2)}) collective-permute-start(bf16[512,128]{1,0:T(8,128)(2,1)S(1)} %collective-permute-done.1.refs_3_), channel_id=1, source_target_pairs={{0,12},{4,8},{8,4},{12,0},{16,28},{20,24},{24,20},{28,16},{1,13},{... | collective-permute-start | bytes 393224 | tf_op jit(solution)/shard_map/ppermute | solution.py:195
  23.4 0.7 %copy-start.5 = (s32[16,16]{1,0:T(8,128)S(1)}, s32[16,16]{1,0:T(8,128)}, u32[]{:S(2)}) copy-start(s32[16,16]{1,0:T(8,128)} %refs_0_.3) | copy-start | bytes 3076
  30.5 4.9 %collective-permute-start.8 = (bf16[128,128]{1,0:T(8,128)(2,1)S(1)}, bf16[128,128]{1,0:T(8,128)(2,1)S(1)}, u32[]{:S(2)}, u32[]{:S(2)}) collective-permute-start(bf16[128,128]{1,0:T(8,128)(2,1)S(1)} %get-tuple-element.24), channel_id=1, source_target_pairs={{0,16},{1,17},{2,18},{3,19},{4,20},{5,21},{6,22},{7,23},{8,24},{9,... | collective-permute-start | bytes 98312 | tf_op jit(solution)/shard_map/ppermute | solution.py:198
  33.4 2.0 %collective-permute-start.9 = (bf16[128,128]{1,0:T(8,128)(2,1)S(1)}, bf16[128,128]{1,0:T(8,128)(2,1)S(1)}, u32[]{:S(2)}, u32[]{:S(2)}) collective-permute-start(bf16[128,128]{1,0:T(8,128)(2,1)S(1)} %get-tuple-element.25), channel_id=1, source_target_pairs={{0,1},{1,0},{2,3},{3,2},{4,5},{5,4},{6,7},{7,6},{8,9},{9,8},{10,11... | collective-permute-start | bytes 98312 | tf_op jit(solution)/shard_map/ppermute | solution.py:198
  33.4 4.2 %collective-permute-start.10 = (bf16[128,128]{1,0:T(8,128)(2,1)S(1)}, bf16[128,128]{1,0:T(8,128)(2,1)S(1)}, u32[]{:S(2)}, u32[]{:S(2)}) collective-permute-start(bf16[128,128]{1,0:T(8,128)(2,1)S(1)} %get-tuple-element.26), channel_id=1, source_target_pairs={{0,17},{1,16},{2,19},{3,18},{4,21},{5,20},{6,23},{7,22},{8,25},{9,... | collective-permute-start | bytes 98312 | tf_op jit(solution)/shard_map/ppermute | solution.py:198
  37.6 1.7 %copy-start = (bf16[256,5120]{1,0:T(8,128)(2,1)S(1)}, bf16[256,5120]{1,0:T(8,128)(2,1)}, u32[]{:S(2)}) copy-start(bf16[256,5120]{1,0:T(8,128)(2,1)} %weight.3) | copy-start | bytes 7864324
  40.4 17.2 %copy-start.1 = (bf16[64,5120]{1,0:T(8,128)(2,1)S(1)}, bf16[64,5120]{1,0:T(8,128)(2,1)}, u32[]{:S(2)}) copy-start(bf16[64,5120]{1,0:T(8,128)(2,1)} %residual.1) | copy-start | bytes 1966084
  40.4 17.2 %copy-start.6 = (f32[5120]{0:T(1024)S(1)}, f32[5120]{0:T(1024)}, u32[]{:S(2)}) copy-start(f32[5120]{0:T(1024)} %param.12) | copy-start | bytes 61444
  40.4 17.2 %collective-permute-start.12 = (bf16[64,5120]{1,0:T(8,128)(2,1)S(1)}, bf16[64,5120]{1,0:T(8,128)(2,1)S(1)}, u32[]{:S(2)}, u32[]{:S(2)}) collective-permute-start(bf16[64,5120]{1,0:T(8,128)(2,1)S(1)} %project_peers.1), channel_id=1, source_target_pairs={{0,2},{1,3},{2,0},{3,1},{4,6},{5,7},{6,4},{7,5},{8,10},{9,11},{10,... | collective-permute-start | bytes 1966088 | tf_op jit(solution)/shard_map/ppermute | solution.py:256

commit v2 on v1

--- a/solution.py
+++ b/solution.py
@@ -14,6 +14,8 @@
 LOG2E = math.log2(math.e)
 SCORE_SCALE = LOG2E / HD**0.5
 BATCH = 4
+LANES = 128
+CUT_NUM, CUT_DEN = 1, 2
 
 VMEM = pltpu.MemorySpace.VMEM
 SMEM = pltpu.MemorySpace.SMEM
@@ -37,16 +39,29 @@
     )
 
 
-def pack(half, q, k, v, kv_keep, kv_send, q_keep, q_send):
+def pack(half, q, k, v, weight, kv_keep, kv_send, q_keep, q_send, left, sems):
     rows, width = q.shape
     part = width // 2
     mine = (lax.axis_index("seq") >= half).astype(jnp.int32)
     keep = pl.ds(pl.multiple_of(mine * part, part), part)
     send = pl.ds(pl.multiple_of((1 - mine) * part, part), part)
-    for columns, kv, queries in ((keep, kv_keep, q_keep), (send, kv_send, q_send)):
-        kv[:rows] = k[:, columns]
-        kv[rows:] = v[:, columns]
-        queries[...] = q[:, columns]
+    copies = [
+        (k.at[:, send], kv_send.at[:rows]),
+        (v.at[:, send], kv_send.at[rows:]),
+        (k.at[:, keep], kv_keep.at[:rows]),
+        (v.at[:, keep], kv_keep.at[rows:]),
+        (q.at[:, send], q_send),
+        (q.at[:, keep], q_keep),
+        (weight.at[:, : left.shape[1]], left),
+    ]
+    copies = [
+        pltpu.make_async_copy(source, target, sems.at[n])
+        for n, (source, target) in enumerate(copies)
+    ]
+    for copy in copies:
+        copy.start()
+    for copy in copies:
+        copy.wait()
 
 
 def attend(half, cores, places, first, last, *refs):
@@ -137,44 +152,75 @@
                 other[to, at] = jnp.where(core == 0, two, one)
 
 
-def gather_heads(half, own, far, other, far_other, mine_ref, core_ref):
+def stage(weight, right, sem):
+    copy = pltpu.make_async_copy(weight.at[:, weight.shape[1] - right.shape[1] :], right, sem)
+    copy.start()
+    copy.wait()
+
+
+def line_up(half, cores, own, far, other, far_other, *outs):
     low = lax.axis_index("seq") < half
-    part = own.shape[1]
-    own, far, other, far_other = own[...], far[...], other[...], far_other[...]
-    mine_ref[:, :part] = jnp.where(low, own, far)
-    mine_ref[:, part:] = jnp.where(low, far, own)
-    core_ref[:, :part] = jnp.where(low, other, far_other)
-    core_ref[:, part:] = jnp.where(low, far_other, other)
-
-
-def project_peers(half, cores, own, far, other, far_other, weight, core_weight, *rest):
-    outs, (mine, core) = rest[:-2], rest[-2:]
-    gather_heads(half, own, far, other, far_other, mine, core)
-    chips = lax.axis_size("tp") // cores
+    chips = len(outs)
     chip = lax.axis_index("tp") // cores
     share = own.shape[0] // chips
-    for step, out in enumerate(outs, 1):
+    part = own.shape[1]
+    for step, out in enumerate(outs):
         place = lax.rem(chip + step, chips)
         rows = pl.ds(pl.multiple_of(place * share, share), share)
-        branch = dot(mine[rows], weight[...]) + dot(core[rows], core_weight[...])
-        out[...] = branch.astype(jnp.bfloat16)
-
-
-def project_own(half, cores, own, far, other, far_other, weight, core_weight, out, mine, core):
-    gather_heads(half, own, far, other, far_other, mine, core)
-    chips = lax.axis_size("tp") // cores
-    chip = lax.axis_index("tp") // cores
-    share = own.shape[0] // chips
-    rows = pl.ds(pl.multiple_of(chip * share, share), share)
-    out[...] = dot(mine[rows], weight[...]) + dot(core[rows], core_weight[...])
-
-
-def finish(residual, gate, own, *rest):
-    peers, out = rest[:-1], rest[-1]
+        one, two = own[rows], far[rows]
+        out[:, :part] = jnp.where(low, one, two)
+        out[:, part : 2 * part] = jnp.where(low, two, one)
+        one, two = other[rows], far_other[rows]
+        out[:, 2 * part : 3 * part] = jnp.where(low, one, two)
+        out[:, 3 * part :] = jnp.where(low, two, one)
+
+
+def project(attended, weight, core_weight, cut):
+    rows = weight.shape[0]
+    return dot(attended[:, :rows], weight[...]) + dot(attended[:, rows:], core_weight[:, cut])
+
+
+def project_peers(cut, *refs):
+    peers = len(refs) // 2 - 1
+    right, core_weight = refs[peers : peers + 2]
+    for attended, out in zip(refs[:peers], refs[peers + 2 :]):
+        out[...] = project(attended, right, core_weight, slice(cut, None)).astype(jnp.bfloat16)
+
+
+def project_own(cut, attended, left, right, core_weight, out_left, out_right):
+    out_left[...] = project(attended, left, core_weight, slice(0, cut))
+    out_right[...] = project(attended, right, core_weight, slice(cut, None))
+
+
+def gated(residual, gate, branch):
+    return (residual.astype(jnp.float32) + gate * branch).astype(jnp.bfloat16)
+
+
+def finish_left(peers, cut, residual, gate, own, *refs):
+    attended, weights, core_weights = refs[:peers], refs[peers : 2 * peers], refs[2 * peers : 3 * peers]
+    out, block, sem = refs[3 * peers :]
+    branch = own[...]
+    for one, weight, core_weight in zip(attended, weights, core_weights):
+        branch = branch + project(one, weight, core_weight, slice(None))
+    block[...] = gated(residual[:, :cut], gate[:, :cut], branch)
+    copy = pltpu.make_async_copy(block, out.at[:, :cut], sem)
+    copy.start()
+    copy.wait()
+
+
+def finish_right(cut, residual, gate, own, *refs):
+    peers, (_, out, block, sem) = refs[:-4], refs[-4:]
     branch = own[...]
     for peer in peers:
         branch = branch + peer[...].astype(jnp.float32)
-    out[...] = (residual[...].astype(jnp.float32) + gate[...] * branch).astype(jnp.bfloat16)
+    block[...] = gated(residual[:, cut:], gate[:, cut:], branch)
+    copy = pltpu.make_async_copy(block, out.at[:, cut:], sem)
+    copy.start()
+    copy.wait()
+
+
+def cost(microseconds):
+    return pl.CostEstimate(flops=0, bytes_accessed=microseconds * 3_000_000, transcendentals=0)
 
 
 def params(mib):
@@ -190,6 +236,8 @@
     chips = tp // cores
     share = rows // tp
     part = width // 2
+    peers = chips - 1
+    cut = columns * CUT_NUM // CUT_DEN // LANES * LANES
 
     def swap(array, place):
         return lax.ppermute(array, "seq", [(i, i ^ place) for i in range(seq)])
@@ -205,20 +253,51 @@
             ],
         )
 
-    kv_keep, kv_send, q_keep, q_send = pl.pallas_call(
+    def swap_cores(array):
+        return lax.ppermute(array, "tp", [(t, t ^ 1) for t in range(tp)])
+
+    def to_chip(array, step):
+        return lax.ppermute(
+            array,
+            "tp",
+            [(t, (t // cores + step) % chips * cores + t % cores) for t in range(tp)],
+        )
+
+    def in_hbm(*arrays):
+        return [pltpu.with_memory_space_constraint(array, pltpu.HBM) for array in arrays]
+
+    kv_keep, kv_send, q_keep, q_send, left = pl.pallas_call(
         functools.partial(pack, half),
-        out_shape=[bf16(2 * rows, part)] * 2 + [bf16(rows, part)] * 2,
-        in_specs=in_vmem(3),
-        out_specs=in_vmem(4),
+        out_shape=[bf16(2 * rows, part)] * 2 + [bf16(rows, part)] * 2 + [bf16(width, cut)],
+        in_specs=[pl.BlockSpec(memory_space=pl.ANY)] * 4,
+        out_specs=in_vmem(5),
+        scratch_shapes=[pltpu.SemaphoreType.DMA((7,))],
         compiler_params=params(16),
+        cost_estimate=cost(1),
         name="pack",
-    )(queries, keys, values)
+    )(*in_hbm(queries, keys, values, out_weight))
     kv_far = swap(kv_send, half)
     order = list(range(half - 1, 0, -1))
-    near = {m: swap(kv_keep, m) for m in order}
+    direct = [m for m in order if m % 2 == 0 or m == 1]
+    near = {m: swap(kv_keep, m) for m in direct}
+    core_weight = swap_cores(out_weight)
+    chip_weights = [to_chip(left, step) for step in range(1, chips)]
+    kv_far, weight, q_send = lax.optimization_barrier((kv_far, out_weight, q_send))
     q_far = swap(q_send, half)
     far = {m: swap(kv_far, m) for m in order}
-    core_weight = lax.ppermute(out_weight, "tp", [(t, t ^ 1) for t in range(tp)])
+    for m in order:
+        if m not in direct:
+            near[m] = swap(near[m - 1], 1)
+    right = pl.pallas_call(
+        stage,
+        out_shape=bf16(width, columns - cut),
+        in_specs=[pl.BlockSpec(memory_space=pl.ANY)],
+        out_specs=pl.BlockSpec(memory_space=VMEM),
+        scratch_shapes=[pltpu.SemaphoreType.DMA],
+        compiler_params=params(16),
+        cost_estimate=cost(1),
+        name="stage",
+    )(*in_hbm(weight))
     pieces = [(0, kv_keep)] + [(m, near[m]) for m in order]
     pieces += [(half, kv_far)] + [(m ^ half, far[m]) for m in order]
     state = []
@@ -235,48 +314,70 @@
             in_specs=[pl.BlockSpec(memory_space=SMEM)] + in_vmem(2 + len(batch) + len(state)),
             out_specs=in_vmem(len(out_shape)),
             compiler_params=params(32),
-            name="attend",
+            cost_estimate=cost(2),
+        name="attend",
         )(block_mask, q_keep, q_far, *[piece for _, piece in batch], *state)
     own_mine, own_other, far_mine, far_other = state
     from_far = across(far_mine, half, 0)
     from_far_core = across(far_other, half, 1)
     from_core = across(own_other, 0, 1)
-    heads = (own_mine, from_far, from_core, from_far_core)
-    scratch = [pltpu.VMEM((rows // cores, width), jnp.bfloat16)] * 2
+    lined = pl.pallas_call(
+        functools.partial(line_up, half, cores),
+        out_shape=[bf16(share, cores * width)] * chips,
+        in_specs=in_vmem(4),
+        out_specs=in_vmem(chips),
+        compiler_params=params(16),
+        cost_estimate=cost(1),
+        name="line_up",
+    )(own_mine, from_far, from_core, from_far_core)
+    arrived = [to_chip(array, step) for step, array in enumerate(lined[1:], 1)]
     sums = pl.pallas_call(
-        functools.partial(project_peers, half, cores),
-        out_shape=[bf16(share, columns)] * (chips - 1),
-        in_specs=in_vmem(6),
-        out_specs=in_vmem(chips - 1),
-        scratch_shapes=scratch,
+        functools.partial(project_peers, cut),
+        out_shape=[bf16(share, columns - cut)] * peers,
+        in_specs=in_vmem(peers + 2),
+        out_specs=in_vmem(peers),
         compiler_params=params(32),
+        cost_estimate=cost(1),
         name="project_peers",
-    )(*heads, out_weight, core_weight)
-    arrived = [
-        lax.ppermute(
-            array,
-            "tp",
-            [(t, (t // cores + step) % chips * cores + t % cores) for t in range(tp)],
-        )
-        for step, array in enumerate(sums, 1)
-    ]
-    own = pl.pallas_call(
-        functools.partial(project_own, half, cores),
-        out_shape=f32(share, columns),
-        in_specs=in_vmem(6),
-        out_specs=pl.BlockSpec(memory_space=VMEM),
-        scratch_shapes=scratch,
+    )(*lined[1:], right, core_weight)
+    mine, *sums = lax.optimization_barrier((lined[0], *sums))
+    own_left, own_right = pl.pallas_call(
+        functools.partial(project_own, cut),
+        out_shape=[f32(share, cut), f32(share, columns - cut)],
+        in_specs=in_vmem(4),
+        out_specs=in_vmem(2),
         compiler_params=params(32),
+        cost_estimate=cost(1),
         name="project_own",
-    )(*heads, out_weight, core_weight)
+    )(mine, left, right, core_weight)
+    summed = [to_chip(array, step) for step, array in enumerate(sums, 1)]
+    own_left, *chip_weights = lax.optimization_barrier((own_left, *chip_weights))
+    chip_core_weights = [swap_cores(weight) for weight in chip_weights]
+    gate = gate[None, :]
+    out = pl.pallas_call(
+        functools.partial(finish_left, peers, cut),
+        out_shape=bf16(share, columns),
+        in_specs=in_vmem(3 + 3 * peers),
+        out_specs=pl.BlockSpec(memory_space=pl.ANY),
+        scratch_shapes=[pltpu.VMEM((share, cut), jnp.bfloat16), pltpu.SemaphoreType.DMA],
+        compiler_params=params(32),
+        cost_estimate=cost(2),
+        name="finish_left",
+    )(residual, gate, own_left, *arrived, *chip_weights, *chip_core_weights)
     return pl.pallas_call(
-        finish,
+        functools.partial(finish_right, cut),
         out_shape=bf16(share, columns),
-        in_specs=in_vmem(3 + len(arrived)),
-        out_specs=pl.BlockSpec(memory_space=VMEM),
+        in_specs=in_vmem(3 + peers) + [pl.BlockSpec(memory_space=pl.ANY)],
+        out_specs=pl.BlockSpec(memory_space=pl.ANY),
+        scratch_shapes=[
+            pltpu.VMEM((share, columns - cut), jnp.bfloat16),
+            pltpu.SemaphoreType.DMA,
+        ],
+        input_output_aliases={3 + peers: 0},
         compiler_params=params(16),
-        name="finish",
-    )(residual, gate[None, :], own, *arrived)
+        cost_estimate=cost(1),
+        name="finish_right",
+    )(residual, gate, own_right, *summed, out)
 
 
 def solution(mesh):

time: 59 us -> 50.3 us (0.85)
  waiting for transfers between devices: 29.1 us -> 17.1 us
  local copies, waits for them, and re-layouts: 5.16 us -> 0.02 us
  starting transfers between devices: 17.3 us -> 22.2 us
  Pallas kernels: 7.14 us -> 10.7 us
    ppermute x2 -> x5, waiting for transfers between devices: 14.6 us -> 9.08 us  [the longest x3 9.08 us: to_chip(): lax.ppermute(array, 'tp', [(t, (t // cores + step) % chips * cores + t %...]
    unnamed x14 -> x6, local copies, waits for them, and re-layouts: 5.16 us -> 0.02 us
    ppermute x2 -> x5, starting transfers between devices: 2.04 us -> 6.47 us  [the longest x3 4.62 us: to_chip(): lax.ppermute(array, 'tp', [(t, (t // cores + step) % chips * cores + t %...]
    ppermute x8, waiting for transfers between devices: 10.5 us -> 7.17 us  [swap(): return lax.ppermute(array, 'seq', [(i, i ^ place) for i in range(seq)])]
    ppermute x3, waiting for transfers between devices: 3.99 us -> 0.8 us  [across(): lax.ppermute(array, ('seq', 'tp'), [(i * tp + t, (i ^ place) * tp + (t ^...]
    pallas_call x3 -> x6, Pallas kernels: 3.11 us -> 5.13 us  [the longest x1 1.32 us: shards(): pl.pallas_call(stage, out_shape=bf16(width, columns - cut), in_specs=[pl....]
    pallas_call x1, Pallas kernels: 0.07 us -> 1.59 us  [shards(): pl.pallas_call(functools.partial(pack, half), out_shape=[bf16(2 * rows, p...]
    ppermute x8, starting transfers between devices: 12.1 us -> 13 us  [swap(): return lax.ppermute(array, 'seq', [(i, i ^ place) for i in range(seq)])]
  transfers between devices with their start and end apart: 13 -> 16, of which waited for: 7 -> 8; matrix products, arithmetic and copies ran while one was open for 0% -> 0% of each run, Pallas kernels for 9% -> 20%
where the time goes in v2:
time: 50.3 us; the launch traced here: 50.1 us
  starting transfers between devices  22.2 us (44%)
  waiting for transfers between devices  17.1 us (34%)
  Pallas kernels  10.7 us (21%)
    ppermute x8, starting transfers between devices, swap(): return lax.ppermute(array, 'seq', [(i, i ^ place) for i in range(seq)])  13 us
    ppermute x3, waiting for transfers between devices, to_chip(): lax.ppermute(array, 'tp', [(t, (t // cores + step) % chips * cores + t %...  9.08 us
    ppermute x8, waiting for transfers between devices, swap(): return lax.ppermute(array, 'seq', [(i, i ^ place) for i in range(seq)])  7.17 us
    ppermute x3, starting transfers between devices, to_chip(): lax.ppermute(array, 'tp', [(t, (t // cores + step) % chips * cores + t %...  4.62 us
    pallas_call x2, Pallas kernels, shards(): pl.pallas_call(functools.partial(attend, half, cores, [m for m, _ in batc...  3.97 us
    ppermute x3, starting transfers between devices, across(): lax.ppermute(array, ('seq', 'tp'), [(i * tp + t, (i ^ place) * tp + (t ^...  2.82 us
    ppermute x2, starting transfers between devices, swap_cores(): return lax.ppermute(array, 'tp', [(t, t ^ 1) for t in range(tp)])  1.85 us
    pallas_call x1, Pallas kernels, shards(): pl.pallas_call(functools.partial(pack, half), out_shape=[bf16(2 * rows, p...  1.59 us
  transfers between devices with their start and end apart: 16, of which 8 were waited for; matrix products, arithmetic and copies ran while one was open for 0% of the time, Pallas kernels for 20%

profile of v2, /device:TPU:0, one launch (start us, length us, event | category | flops | bytes accessed | tf_op | source)
XLA Modules:
  0.0 50.1 jit_solution(5982078895912398313)
XLA Ops:
  0.0 0.0 copy-start.2
  0.0 0.5 collective-permute-start.11
  0.5 1.6 %pack.1 = (bf16[512,128]{1,0:T(8,128)(2,1)S(1)}, bf16[512,128]{1,0:T(8,128)(2,1)S(1)}, bf16[256,128]{1,0:T(8,128)(2,1)S(1)}, bf16[256,128]{1,0:T(8,128)(2,1)S(1)}, bf16[256,2560]{1,0:T(8,128)(2,1)S(1)}) custom-call(bf16[256,256]{1,0:T(8,128)(2,1)} %q.1, bf16[256,256]{1,0:T(8,128)(2,1)} %k.1, bf16[256,256]{1,0:T(8,128)(2,1)} %v.1, bf16[256,5120]{1,0:T(8,128)(2,1)} %weight.2), custom_call_target="tpu_custom_call" | custom-call | bytes 3000000 | tf_op jit(solution)/shard_map/pack/pallas_call | solution.py:269
  2.1 2.6 %collective-permute-start.13 = (bf16[256,2560]{1,0:T(8,128)(2,1)S(1)}, bf16[256,2560]{1,0:T(8,128)(2,1)S(1)}, u32[]{:S(2)}, u32[]{:S(2)}) collective-permute-start(bf16[256,2560]{1,0:T(8,128)(2,1)S(1)} %get-tuple-element.45.left), channel_id=1, source_target_pairs={{0,2},{1,3},{2,0},{3,1},{4,6},{5,7},{6,4},{7,5},{8,10},{9,11},{10,... | collective-permute-start | bytes 3932168 | tf_op jit(solution)/shard_map/ppermute | solution.py:260
  4.7 1.6 %collective-permute-start.5 = (bf16[512,128]{1,0:T(8,128)(2,1)S(1)}, bf16[512,128]{1,0:T(8,128)(2,1)S(1)}, u32[]{:S(2)}, u32[]{:S(2)}) collective-permute-start(bf16[512,128]{1,0:T(8,128)(2,1)S(1)} %get-tuple-element.33.refs_3_), channel_id=1, source_target_pairs={{0,8},{4,12},{8,0},{12,4},{16,24},{20,28},{24,16},{28,20},{1,9},{5... | collective-permute-start | bytes 393224 | tf_op jit(solution)/shard_map/ppermute | solution.py:243
  6.2 2.6 %collective-permute-start = (bf16[512,128]{1,0:T(8,128)(2,1)S(1)}, bf16[512,128]{1,0:T(8,128)(2,1)S(1)}, u32[]{:S(2)}, u32[]{:S(2)}) collective-permute-start(bf16[512,128]{1,0:T(8,128)(2,1)S(1)} %get-tuple-element.29), channel_id=1, source_target_pairs={{0,16},{4,20},{8,24},{12,28},{16,0},{20,4},{24,8},{28,12},{1,17},{... | collective-permute-start | bytes 393224 | tf_op jit(solution)/shard_map/ppermute | solution.py:243
  8.8 1.5 %collective-permute-start.7 = (bf16[512,128]{1,0:T(8,128)(2,1)S(1)}, bf16[512,128]{1,0:T(8,128)(2,1)S(1)}, u32[]{:S(2)}, u32[]{:S(2)}) collective-permute-start(bf16[512,128]{1,0:T(8,128)(2,1)S(1)} %get-tuple-element.33.refs_3_), channel_id=1, source_target_pairs={{0,4},{4,0},{8,12},{12,8},{16,20},{20,16},{24,28},{28,24},{1,5},{5... | collective-permute-start | bytes 393224 | tf_op jit(solution)/shard_map/ppermute | solution.py:243
  10.3 2.4 %collective-permute-done.5.refs_5_ = bf16[512,128]{1,0:T(8,128)(2,1)S(1)} collective-permute-done((bf16[512,128]{1,0:T(8,128)(2,1)S(1)}, bf16[512,128]{1,0:T(8,128)(2,1)S(1)}, u32[]{:S(2)}, u32[]{:S(2)}) %collective-permute-start.5) | collective-permute-done | bytes 131104 | tf_op jit(solution)/shard_map/ppermute | solution.py:243
  12.7 1.5 %collective-permute-start.6 = (bf16[512,128]{1,0:T(8,128)(2,1)S(1)}, bf16[512,128]{1,0:T(8,128)(2,1)S(1)}, u32[]{:S(2)}, u32[]{:S(2)}) collective-permute-start(bf16[512,128]{1,0:T(8,128)(2,1)S(1)} %collective-permute-done.5.refs_5_), channel_id=1, source_target_pairs={{0,4},{4,0},{8,12},{12,8},{16,20},{20,16},{24,28},{28,24},{1,5},{5... | collective-permute-start | bytes 393224 | tf_op jit(solution)/shard_map/ppermute | solution.py:243
  14.2 1.1 %collective-permute-done.refs_3_ = bf16[512,128]{1,0:T(8,128)(2,1)S(1)} collective-permute-done((bf16[512,128]{1,0:T(8,128)(2,1)S(1)}, bf16[512,128]{1,0:T(8,128)(2,1)S(1)}, u32[]{:S(2)}, u32[]{:S(2)}) %collective-permute-start) | collective-permute-done | bytes 131104 | tf_op jit(solution)/shard_map/ppermute | solution.py:243
  15.3 0.3 collective-permute-start.1
  15.7 0.0 collective-permute-done.7.refs_6_
  15.7 3.6 %collective-permute-start.2 = (bf16[512,128]{1,0:T(8,128)(2,1)S(1)}, bf16[512,128]{1,0:T(8,128)(2,1)S(1)}, u32[]{:S(2)}, u32[]{:S(2)}) collective-permute-start(bf16[512,128]{1,0:T(8,128)(2,1)S(1)} %collective-permute-done.refs_3_), channel_id=1, source_target_pairs={{0,12},{4,8},{8,4},{12,0},{16,28},{20,24},{24,20},{28,16},{1,13},{... | collective-permute-start | bytes 393224 | tf_op jit(solution)/shard_map/ppermute | solution.py:243
  19.3 1.9 %collective-permute-done.1.refs_2_ = bf16[256,128]{1,0:T(8,128)(2,1)S(1)} collective-permute-done((bf16[256,128]{1,0:T(8,128)(2,1)S(1)}, bf16[256,128]{1,0:T(8,128)(2,1)S(1)}, u32[]{:S(2)}, u32[]{:S(2)}) %collective-permute-start.1) | collective-permute-done | bytes 65568 | tf_op jit(solution)/shard_map/ppermute | solution.py:243
  21.2 0.3 collective-permute-start.3
  21.5 0.0 collective-permute-done.6.refs_4_
  21.5 1.5 %collective-permute-start.4 = (bf16[512,128]{1,0:T(8,128)(2,1)S(1)}, bf16[512,128]{1,0:T(8,128)(2,1)S(1)}, u32[]{:S(2)}, u32[]{:S(2)}) collective-permute-start(bf16[512,128]{1,0:T(8,128)(2,1)S(1)} %collective-permute-done.refs_3_), channel_id=1, source_target_pairs={{0,4},{4,0},{8,12},{12,8},{16,20},{20,16},{24,28},{28,24},{1,5},{5... | collective-permute-start | bytes 393224 | tf_op jit(solution)/shard_map/ppermute | solution.py:243
  23.0 0.0 copy-done.2
  23.0 1.7 %attend.2 = (f32[512,128]{1,0:T(8,128)S(1)}, f32[512,128]{1,0:T(8,128)S(1)}, f32[512,128]{1,0:T(8,128)S(1)}) custom-call(s32[16,16]{1,0:T(8,128)S(1)} %copy-done.2, bf16[256,128]{1,0:T(8,128)(2,1)S(1)} %get-tuple-element.28.refs_1_, bf16[256,128]{1,0:T(8,128)(2,1)S(1)} %collective-permute-done.1.refs_2_, bf16[512,128]{1,0:T(8,128)(2,1)S(1)} %get-tuple-element.33.refs_3_, ...), custom_call_target="tpu_custom_call" | custom-call | bytes 6000000 | tf_op jit(solution)/shard_map/attend/pallas_call | solution.py:311
  24.7 0.0 collective-permute-done.2.refs_4_
  24.7 1.4 %collective-permute-done.3.refs_5_ = bf16[512,128]{1,0:T(8,128)(2,1)S(1)} collective-permute-done((bf16[512,128]{1,0:T(8,128)(2,1)S(1)}, bf16[512,128]{1,0:T(8,128)(2,1)S(1)}, u32[]{:S(2)}, u32[]{:S(2)}) %collective-permute-start.3) | collective-permute-done | bytes 131104 | tf_op jit(solution)/shard_map/ppermute | solution.py:243
  26.1 0.4 collective-permute-done.4.refs_6_
  26.5 2.3 %attend.3 = (bf16[128,128]{1,0:T(8,128)(2,1)S(1)}, bf16[128,128]{1,0:T(8,128)(2,1)S(1)}, bf16[128,128]{1,0:T(8,128)(2,1)S(1)}, bf16[128,128]{1,0:T(8,128)(2,1)S(1)}) custom-call(s32[16,16]{1,0:T(8,128)S(1)} %copy-done.2, bf16[256,128]{1,0:T(8,128)(2,1)S(1)} %get-tuple-element.28.refs_1_, bf16[256,128]{1,0:T(8,128)(2,1)S(1)} %collective-permute-done.1.refs_2_, ...), custom_call_target="tpu_custom_call" | custom-call | bytes 6000000 | tf_op jit(solution)/shard_map/attend/pallas_call | solution.py:311
  28.8 0.1 collective-permute-start.10
  28.8 2.2 %collective-permute-start.8 = (bf16[128,128]{1,0:T(8,128)(2,1)S(1)}, bf16[128,128]{1,0:T(8,128)(2,1)S(1)}, u32[]{:S(2)}, u32[]{:S(2)}) collective-permute-start(bf16[128,128]{1,0:T(8,128)(2,1)S(1)} %get-tuple-element.38), channel_id=1, source_target_pairs={{0,16},{1,17},{2,18},{3,19},{4,20},{5,21},{6,22},{7,23},{8,24},{9,... | collective-permute-start | bytes 98312 | tf_op jit(solution)/shard_map/ppermute | solution.py:246
  31.0 0.6 %collective-permute-start.9 = (bf16[128,128]{1,0:T(8,128)(2,1)S(1)}, bf16[128,128]{1,0:T(8,128)(2,1)S(1)}, u32[]{:S(2)}, u32[]{:S(2)}) collective-permute-start(bf16[128,128]{1,0:T(8,128)(2,1)S(1)} %get-tuple-element.39), channel_id=1, source_target_pairs={{0,1},{1,0},{2,3},{3,2},{4,5},{5,4},{6,7},{7,6},{8,9},{9,8},{10,11... | collective-permute-start | bytes 98312 | tf_op jit(solution)/shard_map/ppermute | solution.py:246
  31.6 1.3 %stage.1.refs_1_.right = bf16[256,2560]{1,0:T(8,128)(2,1)S(1)} custom-call(bf16[256,5120]{1,0:T(8,128)(2,1)} %weight.2), custom_call_target="tpu_custom_call" | custom-call | bytes 3000000 | tf_op jit(solution)/shard_map/stage/pallas_call | solution.py:291
  32.9 0.3 collective-permute-done.10.far_other
  33.2 0.5 %collective-permute-done.8.far = bf16[128,128]{1,0:T(8,128)(2,1)S(1)} collective-permute-done((bf16[128,128]{1,0:T(8,128)(2,1)S(1)}, bf16[128,128]{1,0:T(8,128)(2,1)S(1)}, u32[]{:S(2)}, u32[]{:S(2)}) %collective-permute-start.8) | collective-permute-done | bytes 32800 | tf_op jit(solution)/shard_map/ppermute | solution.py:246
  33.7 0.0 collective-permute-done.9.other
  33.8 0.0 collective-permute-done.11.refs_2_.core_weight
  33.8 0.6 %project_peers.1 = bf16[64,2560]{1,0:T(8,128)(2,1)S(1)} custom-call(bf16[64,512]{1,0:T(8,128)(2,1)S(1)} %get-tuple-element.42.refs_0_, bf16[256,2560]{1,0:T(8,128)(2,1)S(1)} %stage.1.refs_1_.right, bf16[256,5120]{1,0:T(8,128)(2,1)S(1)} %collective-permute-done.11.refs_2_.core_weight), custom_call_target="tpu_custom_call" | custom-call | bytes 3000000 | tf_op jit(solution)/shard_map/project_peers/pallas_call | solution.py:334
  34.3 0.0 copy-start
  34.4 0.0 copy-start.1
  34.4 1.0 %project_own.1 = (f32[64,2560]{1,0:T(8,128)S(1)}, f32[64,2560]{1,0:T(8,128)S(1)}) custom-call(bf16[64,512]{1,0:T(8,128)(2,1)S(1)} %get-tuple-element.44.attended, bf16[256,2560]{1,0:T(8,128)(2,1)S(1)} %get-tuple-element.45.left, bf16[256,2560]{1,0:T(8,128)(2,1)S(1)} %stage.1.refs_1_.right, bf16[256,5120]{1,0:T(8,128)(2,1)S(1)} %collective-permute-done.11.refs_2_.core_weight), custom_call_target="tpu_custom_call" | custom-call | bytes 3000000 | tf_op jit(solution)/shard_map/project_own/pallas_call | solution.py:344
  35.4 0.0 collective-permute-done.13.refs_1_
  35.4 1.4 %collective-permute-start.15 = (bf16[256,2560]{1,0:T(8,128)(2,1)S(1)}, bf16[256,2560]{1,0:T(8,128)(2,1)S(1)}, u32[]{:S(2)}, u32[]{:S(2)}) collective-permute-start(bf16[256,2560]{1,0:T(8,128)(2,1)S(1)} %collective-permute-done.13.refs_1_), channel_id=1, source_target_pairs={{0,1},{1,0},{2,3},{3,2},{4,5},{5,4},{6,7},{7,6},{8,9},{9,8},{10,11... | collective-permute-start | bytes 3932168 | tf_op jit(solution)/shard_map/ppermute | solution.py:257
  36.8 0.5 %collective-permute-start.12 = (bf16[64,2560]{1,0:T(8,128)(2,1)S(1)}, bf16[64,2560]{1,0:T(8,128)(2,1)S(1)}, u32[]{:S(2)}, u32[]{:S(2)}) collective-permute-start(bf16[64,2560]{1,0:T(8,128)(2,1)S(1)} %project_peers.1), channel_id=1, source_target_pairs={{0,2},{1,3},{2,0},{3,1},{4,6},{5,7},{6,4},{7,5},{8,10},{9,11},{10,... | collective-permute-start | bytes 983048 | tf_op jit(solution)/shard_map/ppermute | solution.py:260
  37.3 1.5 %collective-permute-start.14 = (bf16[64,512]{1,0:T(8,128)(2,1)S(1)}, bf16[64,512]{1,0:T(8,128)(2,1)S(1)}, u32[]{:S(2)}, u32[]{:S(2)}) collective-permute-start(bf16[64,512]{1,0:T(8,128)(2,1)S(1)} %get-tuple-element.42.refs_0_), channel_id=1, source_target_pairs={{0,2},{1,3},{2,0},{3,1},{4,6},{5,7},{6,4},{7,5},{8,10},{9,11},{10,... | collective-permute-start | bytes 196616 | tf_op jit(solution)/shard_map/ppermute | solution.py:260
  38.8 9.1 %collective-permute-done.14.refs_0_ = bf16[64,512]{1,0:T(8,128)(2,1)S(1)} collective-permute-done((bf16[64,512]{1,0:T(8,128)(2,1)S(1)}, bf16[64,512]{1,0:T(8,128)(2,1)S(1)}, u32[]{:S(2)}, u32[]{:S(2)}) %collective-permute-start.14) | collective-permute-done | bytes 65568 | tf_op jit(solution)/shard_map/ppermute | solution.py:260
  47.9 0.0 collective-permute-done.15.refs_2_
  47.9 0.0 copy-done
  47.9 0.0 copy-done.1
  47.9 1.3 %finish_left.1.refs_1_ = bf16[64,5120]{1,0:T(8,128)(2,1)} custom-call(bf16[64,5120]{1,0:T(8,128)(2,1)S(1)} %copy-done, f32[1,5120]{1,0:T(1,128)S(1)} %bitcast.1, f32[64,2560]{1,0:T(8,128)S(1)} %get-tuple-element.49.own, bf16[64,512]{1,0:T(8,128)(2,1)S(1)} %collective-permute-done.14.refs_0_, bf16[256,2560]{1,0:T(8,128)(2,1)S(1)} %collective-permute-done.13.refs_1_, ...), custom_call_target="tpu_custom_call" | custom-call | bytes 6000000 | tf_op jit(solution)/shard_map/finish_left/pallas_call | solution.py:357
  49.2 0.0 collective-permute-done.12.refs_0_
  49.2 0.9 %finish_right.1 = bf16[64,5120]{1,0:T(8,128)(2,1)} custom-call(bf16[64,5120]{1,0:T(8,128)(2,1)S(1)} %copy-done, f32[1,5120]{1,0:T(1,128)S(1)} %bitcast.2, f32[64,2560]{1,0:T(8,128)S(1)} %get-tuple-element.46.own, bf16[64,2560]{1,0:T(8,128)(2,1)S(1)} %collective-permute-done.12.refs_0_, ...), custom_call_target="tpu_custom_call", output_to_operand_aliasing={{}: (4, {})} | custom-call | bytes 3000000 | tf_op jit(solution)/shard_map/finish_right/pallas_call | solution.py:367
  (1 shorter events, 0.0 us)
Async XLA Ops:
  0.0 23.0 %copy-start.2 = (s32[16,16]{1,0:T(8,128)S(1)}, s32[16,16]{1,0:T(8,128)}, u32[]{:S(2)}) copy-start(s32[16,16]{1,0:T(8,128)} %refs_0_.3) | copy-start | bytes 3076
  0.0 33.8 %collective-permute-start.11 = (bf16[256,5120]{1,0:T(8,128)(2,1)}, bf16[256,5120]{1,0:T(8,128)(2,1)S(1)}, u32[]{:S(2)}, u32[]{:S(2)}) collective-permute-start(bf16[256,5120]{1,0:T(8,128)(2,1)} %weight.2), channel_id=1, source_target_pairs={{0,1},{1,0},{2,3},{3,2},{4,5},{5,4},{6,7},{7,6},{8,9},{9,8},{10,11... | collective-permute-start | bytes 7864328 | tf_op jit(solution)/shard_map/ppermute | solution.py:257
  2.1 33.3 %collective-permute-start.13 = (bf16[256,2560]{1,0:T(8,128)(2,1)S(1)}, bf16[256,2560]{1,0:T(8,128)(2,1)S(1)}, u32[]{:S(2)}, u32[]{:S(2)}) collective-permute-start(bf16[256,2560]{1,0:T(8,128)(2,1)S(1)} %get-tuple-element.45.left), channel_id=1, source_target_pairs={{0,2},{1,3},{2,0},{3,1},{4,6},{5,7},{6,4},{7,5},{8,10},{9,11},{10,... | collective-permute-start | bytes 3932168 | tf_op jit(solution)/shard_map/ppermute | solution.py:260
  4.7 8.1 %collective-permute-start.5 = (bf16[512,128]{1,0:T(8,128)(2,1)S(1)}, bf16[512,128]{1,0:T(8,128)(2,1)S(1)}, u32[]{:S(2)}, u32[]{:S(2)}) collective-permute-start(bf16[512,128]{1,0:T(8,128)(2,1)S(1)} %get-tuple-element.33.refs_3_), channel_id=1, source_target_pairs={{0,8},{4,12},{8,0},{12,4},{16,24},{20,28},{24,16},{28,20},{1,9},{5... | collective-permute-start | bytes 393224 | tf_op jit(solution)/shard_map/ppermute | solution.py:243
  6.2 9.1 %collective-permute-start = (bf16[512,128]{1,0:T(8,128)(2,1)S(1)}, bf16[512,128]{1,0:T(8,128)(2,1)S(1)}, u32[]{:S(2)}, u32[]{:S(2)}) collective-permute-start(bf16[512,128]{1,0:T(8,128)(2,1)S(1)} %get-tuple-element.29), channel_id=1, source_target_pairs={{0,16},{4,20},{8,24},{12,28},{16,0},{20,4},{24,8},{28,12},{1,17},{... | collective-permute-start | bytes 393224 | tf_op jit(solution)/shard_map/ppermute | solution.py:243
  8.8 6.8 %collective-permute-start.7 = (bf16[512,128]{1,0:T(8,128)(2,1)S(1)}, bf16[512,128]{1,0:T(8,128)(2,1)S(1)}, u32[]{:S(2)}, u32[]{:S(2)}) collective-permute-start(bf16[512,128]{1,0:T(8,128)(2,1)S(1)} %get-tuple-element.33.refs_3_), channel_id=1, source_target_pairs={{0,4},{4,0},{8,12},{12,8},{16,20},{20,16},{24,28},{28,24},{1,5},{5... | collective-permute-start | bytes 393224 | tf_op jit(solution)/shard_map/ppermute | solution.py:243
  12.7 8.8 %collective-permute-start.6 = (bf16[512,128]{1,0:T(8,128)(2,1)S(1)}, bf16[512,128]{1,0:T(8,128)(2,1)S(1)}, u32[]{:S(2)}, u32[]{:S(2)}) collective-permute-start(bf16[512,128]{1,0:T(8,128)(2,1)S(1)} %collective-permute-done.5.refs_5_), channel_id=1, source_target_pairs={{0,4},{4,0},{8,12},{12,8},{16,20},{20,16},{24,28},{28,24},{1,5},{5... | collective-permute-start | bytes 393224 | tf_op jit(solution)/shard_map/ppermute | solution.py:243
  15.3 5.8 %collective-permute-start.1 = (bf16[256,128]{1,0:T(8,128)(2,1)S(1)}, bf16[256,128]{1,0:T(8,128)(2,1)S(1)}, u32[]{:S(2)}, u32[]{:S(2)}) collective-permute-start(bf16[256,128]{1,0:T(8,128)(2,1)S(1)} %get-tuple-element.31), channel_id=1, source_target_pairs={{0,16},{4,20},{8,24},{12,28},{16,0},{20,4},{24,8},{28,12},{1,17},{... | collective-permute-start | bytes 196616 | tf_op jit(solution)/shard_map/ppermute | solution.py:243
  15.7 9.0 %collective-permute-start.2 = (bf16[512,128]{1,0:T(8,128)(2,1)S(1)}, bf16[512,128]{1,0:T(8,128)(2,1)S(1)}, u32[]{:S(2)}, u32[]{:S(2)}) collective-permute-start(bf16[512,128]{1,0:T(8,128)(2,1)S(1)} %collective-permute-done.refs_3_), channel_id=1, source_target_pairs={{0,12},{4,8},{8,4},{12,0},{16,28},{20,24},{24,20},{28,16},{1,13},{... | collective-permute-start | bytes 393224 | tf_op jit(solution)/shard_map/ppermute | solution.py:243
  21.2 5.0 %collective-permute-start.3 = (bf16[512,128]{1,0:T(8,128)(2,1)S(1)}, bf16[512,128]{1,0:T(8,128)(2,1)S(1)}, u32[]{:S(2)}, u32[]{:S(2)}) collective-permute-start(bf16[512,128]{1,0:T(8,128)(2,1)S(1)} %collective-permute-done.refs_3_), channel_id=1, source_target_pairs={{0,8},{4,12},{8,0},{12,4},{16,24},{20,28},{24,16},{28,20},{1,9},{5... | collective-permute-start | bytes 393224 | tf_op jit(solution)/shard_map/ppermute | solution.py:243
  21.5 5.0 %collective-permute-start.4 = (bf16[512,128]{1,0:T(8,128)(2,1)S(1)}, bf16[512,128]{1,0:T(8,128)(2,1)S(1)}, u32[]{:S(2)}, u32[]{:S(2)}) collective-permute-start(bf16[512,128]{1,0:T(8,128)(2,1)S(1)} %collective-permute-done.refs_3_), channel_id=1, source_target_pairs={{0,4},{4,0},{8,12},{12,8},{16,20},{20,16},{24,28},{28,24},{1,5},{5... | collective-permute-start | bytes 393224 | tf_op jit(solution)/shard_map/ppermute | solution.py:243
  28.8 4.4 %collective-permute-start.10 = (bf16[128,128]{1,0:T(8,128)(2,1)S(1)}, bf16[128,128]{1,0:T(8,128)(2,1)S(1)}, u32[]{:S(2)}, u32[]{:S(2)}) collective-permute-start(bf16[128,128]{1,0:T(8,128)(2,1)S(1)} %get-tuple-element.40), channel_id=1, source_target_pairs={{0,17},{1,16},{2,19},{3,18},{4,21},{5,20},{6,23},{7,22},{8,25},{9,... | collective-permute-start | bytes 98312 | tf_op jit(solution)/shard_map/ppermute | solution.py:246
  28.8 4.9 %collective-permute-start.8 = (bf16[128,128]{1,0:T(8,128)(2,1)S(1)}, bf16[128,128]{1,0:T(8,128)(2,1)S(1)}, u32[]{:S(2)}, u32[]{:S(2)}) collective-permute-start(bf16[128,128]{1,0:T(8,128)(2,1)S(1)} %get-tuple-element.38), channel_id=1, source_target_pairs={{0,16},{1,17},{2,18},{3,19},{4,20},{5,21},{6,22},{7,23},{8,24},{9,... | collective-permute-start | bytes 98312 | tf_op jit(solution)/shard_map/ppermute | solution.py:246
  31.0 2.7 %collective-permute-start.9 = (bf16[128,128]{1,0:T(8,128)(2,1)S(1)}, bf16[128,128]{1,0:T(8,128)(2,1)S(1)}, u32[]{:S(2)}, u32[]{:S(2)}) collective-permute-start(bf16[128,128]{1,0:T(8,128)(2,1)S(1)} %get-tuple-element.39), channel_id=1, source_target_pairs={{0,1},{1,0},{2,3},{3,2},{4,5},{5,4},{6,7},{7,6},{8,9},{9,8},{10,11... | collective-permute-start | bytes 98312 | tf_op jit(solution)/shard_map/ppermute | solution.py:246
  34.3 13.6 %copy-start = (bf16[64,5120]{1,0:T(8,128)(2,1)S(1)}, bf16[64,5120]{1,0:T(8,128)(2,1)}, u32[]{:S(2)}) copy-start(bf16[64,5120]{1,0:T(8,128)(2,1)} %residual.3) | copy-start | bytes 1966084
  34.4 13.5 %copy-start.1 = (f32[5120]{0:T(1024)S(1)}, f32[5120]{0:T(1024)}, u32[]{:S(2)}) copy-start(f32[5120]{0:T(1024)} %param.12) | copy-start | bytes 61444
  35.4 12.5 %collective-permute-start.15 = (bf16[256,2560]{1,0:T(8,128)(2,1)S(1)}, bf16[256,2560]{1,0:T(8,128)(2,1)S(1)}, u32[]{:S(2)}, u32[]{:S(2)}) collective-permute-start(bf16[256,2560]{1,0:T(8,128)(2,1)S(1)} %collective-permute-done.13.refs_1_), channel_id=1, source_target_pairs={{0,1},{1,0},{2,3},{3,2},{4,5},{5,4},{6,7},{7,6},{8,9},{9,8},{10,11... | collective-permute-start | bytes 3932168 | tf_op jit(solution)/shard_map/ppermute | solution.py:257
  36.8 12.4 %collective-permute-start.12 = (bf16[64,2560]{1,0:T(8,128)(2,1)S(1)}, bf16[64,2560]{1,0:T(8,128)(2,1)S(1)}, u32[]{:S(2)}, u32[]{:S(2)}) collective-permute-start(bf16[64,2560]{1,0:T(8,128)(2,1)S(1)} %project_peers.1), channel_id=1, source_target_pairs={{0,2},{1,3},{2,0},{3,1},{4,6},{5,7},{6,4},{7,5},{8,10},{9,11},{10,... | collective-permute-start | bytes 983048 | tf_op jit(solution)/shard_map/ppermute | solution.py:260
  37.3 10.6 %collective-permute-start.14 = (bf16[64,512]{1,0:T(8,128)(2,1)S(1)}, bf16[64,512]{1,0:T(8,128)(2,1)S(1)}, u32[]{:S(2)}, u32[]{:S(2)}) collective-permute-start(bf16[64,512]{1,0:T(8,128)(2,1)S(1)} %get-tuple-element.42.refs_0_), channel_id=1, source_target_pairs={{0,2},{1,3},{2,0},{3,1},{4,6},{5,7},{6,4},{7,5},{8,10},{9,11},{10,... | collective-permute-start | bytes 196616 | tf_op jit(solution)/shard_map/ppermute | solution.py:260

commit v3 on v2

--- a/solution.py
+++ b/solution.py
@@ -16,6 +16,7 @@
 BATCH = 4
 LANES = 128
 CUT_NUM, CUT_DEN = 1, 2
+HEAD_NUM, HEAD_DEN = 2, 3
 
 VMEM = pltpu.MemorySpace.VMEM
 SMEM = pltpu.MemorySpace.SMEM
@@ -64,87 +65,99 @@
         copy.wait()
 
 
-def attend(half, cores, places, first, last, *refs):
-    mask, q_own, q_far = refs[:3]
-    pieces = refs[3 : 3 + len(places)]
-    rest = refs[3 + len(places) :]
-    if not first:
-        old_top, old_total, old_summed = rest[:3]
-        rest = rest[3:]
-    me = lax.axis_index("seq")
-    rows = q_own.shape[0]
+def attend(queries, place, mask, pieces, state):
+    rows = queries.shape[0]
     blocks = rows // BLOCK
-    heads = q_own.shape[1] // HD
-    partner = me ^ half
-    query_blocks = [me * blocks + a for a in range(blocks)]
-    query_blocks += [partner * blocks + a for a in range(blocks)]
     bias = [
         [
             [
-                jnp.where(mask[row, (me ^ place) * blocks + b] > 0, 0.0, NEGATIVE)
+                jnp.where(mask[place * blocks + a, owner * blocks + b] > 0, 0.0, NEGATIVE)
                 for b in range(blocks)
             ]
-            for row in query_blocks
+            for a in range(blocks)
         ]
-        for place in places
+        for _, owner in pieces
     ]
-    outs = []
-    for head in range(heads):
+    outs = {}
+    for head in range(queries.shape[1] // HD):
         at = slice(head * HD, (head + 1) * HD)
-        queries = jnp.concatenate([q_own[:, at], q_far[:, at]], axis=0)
-        scores = []
-        for n, piece in enumerate(pieces):
-            raw = dot(queries, piece[:rows, at], ((1,), (1,)))
-            scores.append(
-                [
-                    [
-                        raw[a * BLOCK : (a + 1) * BLOCK, b * BLOCK : (b + 1) * BLOCK]
-                        * SCORE_SCALE
-                        + bias[n][a][b]
-                        for b in range(blocks)
-                    ]
-                    for a in range(2 * blocks)
-                ]
-            )
-        for a in range(2 * blocks):
+        raw = [dot(queries[:, at], piece[:rows, at], ((1,), (1,))) for piece, _ in pieces]
+        for a in range(blocks):
             band = slice(a * BLOCK, (a + 1) * BLOCK)
-            tiles = [piece[a][b] for piece in scores for b in range(blocks)]
-            high = functools.reduce(jnp.maximum, tiles)
-            top = jnp.max(high, axis=1, keepdims=True)
-            if not first:
-                before = old_top[band, at][:, :1]
+            tiles = [
+                raw[n][band, b * BLOCK : (b + 1) * BLOCK] * SCORE_SCALE + bias[n][a][b]
+                for n in range(len(pieces))
+                for b in range(blocks)
+            ]
+            top = jnp.max(functools.reduce(jnp.maximum, tiles), axis=1, keepdims=True)
+            if state is not None:
+                old_top, old_total, old_summed = (ref[band, at] for ref in state)
+                before = old_top[:, :1]
                 top = jnp.maximum(top, before)
                 fade = jnp.exp2(before - top)
             weights = [jnp.exp2(tile - top) for tile in tiles]
             total = functools.reduce(jnp.add, weights)
             summed = None
-            for n, piece in enumerate(pieces):
+            for n, (piece, _) in enumerate(pieces):
                 mine = jnp.concatenate(weights[n * blocks : (n + 1) * blocks], axis=1)
                 part = dot(mine.astype(jnp.bfloat16), piece[rows:, at])
                 summed = part if summed is None else summed + part
-            if not first:
-                total = total + old_total[band, at] * fade
-                summed = summed + old_summed[band, at] * fade
-            if last:
-                whole = jnp.sum(total, axis=1, keepdims=True)
-                outs.append((summed / whole).astype(jnp.bfloat16))
-            else:
-                new_top, new_total, new_summed = rest
-                new_top[band, at] = jnp.broadcast_to(top, (BLOCK, HD))
-                new_total[band, at] = total
-                new_summed[band, at] = summed
+            if state is not None:
+                total = total + old_total * fade
+                summed = summed + old_summed * fade
+            outs[head, a] = top, total, summed
+    return outs
+
+
+def keep_state(outs, refs):
+    new_top, new_total, new_summed = refs
+    for (head, a), (top, total, summed) in outs.items():
+        where = (slice(a * BLOCK, (a + 1) * BLOCK), slice(head * HD, (head + 1) * HD))
+        new_top[where] = jnp.broadcast_to(top, summed.shape)
+        new_total[where] = total
+        new_summed[where] = summed
+
+
+def attend_near(places, first, mask, queries, *refs):
+    me = lax.axis_index("seq")
+    pieces = [(ref, me ^ place) for ref, place in zip(refs, places)]
+    state = None if first else refs[len(places) : -3]
+    keep_state(attend(queries, me, mask, pieces, state), refs[-3:])
+
+
+def attend_rest(half, cores, places, first, last, mask, q_own, q_far, *refs):
+    count = len(places)
+    near, far = refs[:count], refs[count : 2 * count]
+    own_state, rest = refs[2 * count : 2 * count + 3], refs[2 * count + 3 :]
+    far_state = None
+    if not first:
+        far_state, rest = rest[:3], rest[3:]
+    me = lax.axis_index("seq")
+    near = [(ref, me ^ place) for ref, place in zip(near, places)]
+    far = [(ref, me ^ half ^ place) for ref, place in zip(far, places)]
+    for_far = attend(q_far, me ^ half, mask, near + far, far_state)
+    for_own = attend(q_own, me, mask, far, own_state)
     if not last:
+        keep_state(for_own, rest[:3])
+        keep_state(for_far, rest[3:])
         return
     own_mine, own_other, far_mine, far_other = rest
     core = lax.rem(lax.axis_index("tp"), cores)
     chips = lax.axis_size("tp") // cores
+    rows, width = q_own.shape
     share = rows // (chips * cores)
-    for head in range(heads):
-        at = slice(head * HD, (head + 1) * HD)
-        whole = jnp.concatenate(outs[head * 2 * blocks : (head + 1) * 2 * blocks], axis=0)
-        for base, mine, other in ((0, own_mine, own_other), (rows, far_mine, far_other)):
+    for outs, mine, other in ((for_far, far_mine, far_other), (for_own, own_mine, own_other)):
+        for head in range(width // HD):
+            at = slice(head * HD, (head + 1) * HD)
+            whole = []
+            for a in range(rows // BLOCK):
+                _, total, summed = outs[head, a]
+                whole.append(
+                    (summed / jnp.sum(total, axis=1, keepdims=True)).astype(jnp.bfloat16)
+                )
+            whole = jnp.concatenate(whole, axis=0)
             for chip in range(chips):
-                start = base + chip * cores * share
+                start = chip * cores * share
                 one = whole[start : start + share]
                 two = whole[start + share : start + 2 * share]
                 to = slice(chip * share, (chip + 1) * share)
@@ -181,10 +194,20 @@
 
 
 def project_peers(cut, *refs):
-    peers = len(refs) // 2 - 1
+    peers = (len(refs) - 2) // 3
     right, core_weight = refs[peers : peers + 2]
-    for attended, out in zip(refs[:peers], refs[peers + 2 :]):
-        out[...] = project(attended, right, core_weight, slice(cut, None)).astype(jnp.bfloat16)
+    outs = refs[peers + 2 :]
+    for n, attended in enumerate(refs[:peers]):
+        first, second = outs[2 * n : 2 * n + 2]
+        rows = attended.shape[1]
+        head = first.shape[1] - rows
+        first[:, :rows] = attended[...]
+        first[:, rows:] = project(
+            attended, right.at[:, :head], core_weight, slice(cut, cut + head)
+        ).astype(jnp.bfloat16)
+        second[...] = project(
+            attended, right.at[:, head:], core_weight, slice(cut + head, None)
+        ).astype(jnp.bfloat16)
 
 
 def project_own(cut, attended, left, right, core_weight, out_left, out_right):
@@ -196,27 +219,36 @@
     return (residual.astype(jnp.float32) + gate * branch).astype(jnp.bfloat16)
 
 
-def finish_left(peers, cut, residual, gate, own, *refs):
-    attended, weights, core_weights = refs[:peers], refs[peers : 2 * peers], refs[2 * peers : 3 * peers]
-    out, block, sem = refs[3 * peers :]
-    branch = own[...]
-    for one, weight, core_weight in zip(attended, weights, core_weights):
-        branch = branch + project(one, weight, core_weight, slice(None))
-    block[...] = gated(residual[:, :cut], gate[:, :cut], branch)
-    copy = pltpu.make_async_copy(block, out.at[:, :cut], sem)
+def write_out(block, out, columns, sem):
+    copy = pltpu.make_async_copy(block, out.at[:, columns], sem)
     copy.start()
     copy.wait()
 
 
-def finish_right(cut, residual, gate, own, *refs):
-    peers, (_, out, block, sem) = refs[:-4], refs[-4:]
-    branch = own[...]
-    for peer in peers:
-        branch = branch + peer[...].astype(jnp.float32)
-    block[...] = gated(residual[:, cut:], gate[:, cut:], branch)
-    copy = pltpu.make_async_copy(block, out.at[:, cut:], sem)
-    copy.start()
-    copy.wait()
+def finish_left(peers, cut, residual, gate, own_left, own_right, *refs):
+    firsts, weights, core_weights = refs[:peers], refs[peers : 2 * peers], refs[2 * peers : 3 * peers]
+    out, block, sem = refs[3 * peers :]
+    end = block.shape[1]
+    head = end - cut
+    left, right = own_left[...], own_right[:, :head]
+    for first, weight, core_weight in zip(firsts, weights, core_weights):
+        rows = first.shape[1] - head
+        left = left + project(first.at[:, :rows], weight, core_weight, slice(None))
+        right = right + first[:, rows:].astype(jnp.float32)
+    block[:, :cut] = gated(residual[:, :cut], gate[:, :cut], left)
+    block[:, cut:] = gated(residual[:, cut:end], gate[:, cut:end], right)
+    write_out(block, out, slice(0, end), sem)
+
+
+def finish_right(residual, gate, own, *refs):
+    seconds, (_, out, block, sem) = refs[:-4], refs[-4:]
+    tail = block.shape[1]
+    start = out.shape[1] - tail
+    branch = own[:, own.shape[1] - tail :]
+    for second in seconds:
+        branch = branch + second[...].astype(jnp.float32)
+    block[...] = gated(residual[:, start:], gate[:, start:], branch)
+    write_out(block, out, slice(start, None), sem)
 
 
 def cost(microseconds):
@@ -238,6 +270,7 @@
     part = width // 2
     peers = chips - 1
     cut = columns * CUT_NUM // CUT_DEN // LANES * LANES
+    head = (columns - cut) * HEAD_NUM // HEAD_DEN // LANES * LANES
 
     def swap(array, place):
         return lax.ppermute(array, "seq", [(i, i ^ place) for i in range(seq)])
@@ -280,9 +313,9 @@
     order = list(range(half - 1, 0, -1))
     direct = [m for m in order if m % 2 == 0 or m == 1]
     near = {m: swap(kv_keep, m) for m in direct}
+    chip_weights = [to_chip(left, step) for step in range(1, chips)]
     core_weight = swap_cores(out_weight)
-    chip_weights = [to_chip(left, step) for step in range(1, chips)]
-    kv_far, weight, q_send = lax.optimization_barrier((kv_far, out_weight, q_send))
+    kv_far, weight, q_send, core_weight = lax.optimization_barrier((kv_far, out_weight, q_send, core_weight))
     q_far = swap(q_send, half)
     far = {m: swap(kv_far, m) for m in order}
     for m in order:
@@ -298,26 +331,37 @@
         cost_estimate=cost(1),
         name="stage",
     )(*in_hbm(weight))
-    pieces = [(0, kv_keep)] + [(m, near[m]) for m in order]
-    pieces += [(half, kv_far)] + [(m ^ half, far[m]) for m in order]
-    state = []
-    for at in range(0, len(pieces), BATCH):
-        batch = pieces[at : at + BATCH]
-        first, last = at == 0, at + BATCH >= len(pieces)
-        if last:
-            out_shape = [bf16(rows // cores, part)] * 4
-        else:
-            out_shape = [f32(2 * rows, part)] * 3
-        state = pl.pallas_call(
-            functools.partial(attend, half, cores, [m for m, _ in batch], first, last),
+    near[0], far[0] = kv_keep, kv_far
+    places = [0] + order
+    batches = [places[at : at + BATCH] for at in range(0, len(places), BATCH)]
+    smem = pl.BlockSpec(memory_space=SMEM)
+    own_state = []
+    for at, batch in enumerate(batches):
+        own_state = pl.pallas_call(
+            functools.partial(attend_near, batch, at == 0),
+            out_shape=[f32(rows, part)] * 3,
+            in_specs=[smem] + in_vmem(1 + len(batch) + len(own_state)),
+            out_specs=in_vmem(3),
+            compiler_params=params(32),
+            cost_estimate=cost(1),
+            name="attend_near",
+        )(block_mask, q_keep, *[near[m] for m in batch], *own_state)
+    far_state = []
+    for at, batch in enumerate(batches):
+        last = at == len(batches) - 1
+        state = [*own_state, *far_state]
+        out_shape = [bf16(rows // cores, part)] * 4 if last else [f32(rows, part)] * 6
+        outs = pl.pallas_call(
+            functools.partial(attend_rest, half, cores, batch, at == 0, last),
             out_shape=out_shape,
-            in_specs=[pl.BlockSpec(memory_space=SMEM)] + in_vmem(2 + len(batch) + len(state)),
+            in_specs=[smem] + in_vmem(2 + 2 * len(batch) + len(state)),
             out_specs=in_vmem(len(out_shape)),
             compiler_params=params(32),
-            cost_estimate=cost(2),
-        name="attend",
-        )(block_mask, q_keep, q_far, *[piece for _, piece in batch], *state)
-    own_mine, own_other, far_mine, far_other = state
+            cost_estimate=cost(3),
+            name="attend_rest",
+        )(block_mask, q_keep, q_far, *[near[m] for m in batch], *[far[m] for m in batch], *state)
+        own_state, far_state = outs[:3], outs[3:]
+    own_mine, own_other, far_mine, far_other = outs
     from_far = across(far_mine, half, 0)
     from_far_core = across(far_other, half, 1)
     from_core = across(own_other, 0, 1)
@@ -330,12 +374,11 @@
         cost_estimate=cost(1),
         name="line_up",
     )(own_mine, from_far, from_core, from_far_core)
-    arrived = [to_chip(array, step) for step, array in enumerate(lined[1:], 1)]
     sums = pl.pallas_call(
         functools.partial(project_peers, cut),
-        out_shape=[bf16(share, columns - cut)] * peers,
+        out_shape=[bf16(share, cores * width + head), bf16(share, columns - cut - head)] * peers,
         in_specs=in_vmem(peers + 2),
-        out_specs=in_vmem(peers),
+        out_specs=in_vmem(2 * peers),
         compiler_params=params(32),
         cost_estimate=cost(1),
         name="project_peers",
@@ -350,34 +393,35 @@
         cost_estimate=cost(1),
         name="project_own",
     )(mine, left, right, core_weight)
-    summed = [to_chip(array, step) for step, array in enumerate(sums, 1)]
-    own_left, *chip_weights = lax.optimization_barrier((own_left, *chip_weights))
+    sums, chip_weights = lax.optimization_barrier((sums, chip_weights))
+    firsts = [to_chip(array, step) for step, array in enumerate(sums[::2], 1)]
+    seconds = [to_chip(array, step) for step, array in enumerate(sums[1::2], 1)]
     chip_core_weights = [swap_cores(weight) for weight in chip_weights]
     gate = gate[None, :]
     out = pl.pallas_call(
         functools.partial(finish_left, peers, cut),
         out_shape=bf16(share, columns),
-        in_specs=in_vmem(3 + 3 * peers),
+        in_specs=in_vmem(4 + 3 * peers),
         out_specs=pl.BlockSpec(memory_space=pl.ANY),
-        scratch_shapes=[pltpu.VMEM((share, cut), jnp.bfloat16), pltpu.SemaphoreType.DMA],
+        scratch_shapes=[pltpu.VMEM((share, cut + head), jnp.bfloat16), pltpu.SemaphoreType.DMA],
         compiler_params=params(32),
         cost_estimate=cost(2),
         name="finish_left",
-    )(residual, gate, own_left, *arrived, *chip_weights, *chip_core_weights)
+    )(residual, gate, own_left, own_right, *firsts, *chip_weights, *chip_core_weights)
     return pl.pallas_call(
-        functools.partial(finish_right, cut),
+        finish_right,
         out_shape=bf16(share, columns),
         in_specs=in_vmem(3 + peers) + [pl.BlockSpec(memory_space=pl.ANY)],
         out_specs=pl.BlockSpec(memory_space=pl.ANY),
         scratch_shapes=[
-            pltpu.VMEM((share, columns - cut), jnp.bfloat16),
+            pltpu.VMEM((share, columns - cut - head), jnp.bfloat16),
             pltpu.SemaphoreType.DMA,
         ],
         input_output_aliases={3 + peers: 0},
         compiler_params=params(16),
         cost_estimate=cost(1),
         name="finish_right",
-    )(residual, gate, own_right, *summed, out)
+    )(residual, gate, own_right, *seconds, out)
 
 
 def solution(mesh):

time: 50.3 us -> 46.7 us (0.928)
  starting transfers between devices: 22.2 us -> 19.6 us
  waiting for transfers between devices: 17.1 us -> 16.5 us
    ppermute x3, waiting for transfers between devices: 9.08 us -> 6.81 us  [to_chip(): lax.ppermute(array, 'tp', [(t, (t // cores + step) % chips * cores + t %...]
    ppermute x8, starting transfers between devices: 13 us -> 10.8 us  [swap(): return lax.ppermute(array, 'seq', [(i, i ^ place) for i in range(seq)])]
    ppermute x8, waiting for transfers between devices: 7.17 us -> 8.83 us  [swap(): return lax.ppermute(array, 'seq', [(i, i ^ place) for i in range(seq)])]
    ppermute x2, starting transfers between devices: 1.85 us -> 1.09 us  [swap_cores(): return lax.ppermute(array, 'tp', [(t, t ^ 1) for t in range(tp)])]
    pallas_call x3, Pallas kernels: 4.85 us -> 4.31 us  [the longest x1 2.33 us: shards(): pl.pallas_call(functools.partial(attend_rest, half, cores, batch, at == 0...]
  transfers between devices with their start and end apart: 16 -> 16, of which waited for: 8 -> 9; matrix products, arithmetic and copies ran while one was open for 0% -> 0% of each run, Pallas kernels for 20% -> 21%
where the time goes in v3:
time: 46.7 us; the launch traced here: 46.5 us
  starting transfers between devices  19.6 us (42%)
  waiting for transfers between devices  16.5 us (35%)
  Pallas kernels  10.3 us (22%)
    ppermute x8, starting transfers between devices, swap(): return lax.ppermute(array, 'seq', [(i, i ^ place) for i in range(seq)])  10.8 us
    ppermute x8, waiting for transfers between devices, swap(): return lax.ppermute(array, 'seq', [(i, i ^ place) for i in range(seq)])  8.83 us
    ppermute x3, waiting for transfers between devices, to_chip(): lax.ppermute(array, 'tp', [(t, (t // cores + step) % chips * cores + t %...  6.81 us
    ppermute x3, starting transfers between devices, to_chip(): lax.ppermute(array, 'tp', [(t, (t // cores + step) % chips * cores + t %...  4.62 us
    ppermute x3, starting transfers between devices, across(): lax.ppermute(array, ('seq', 'tp'), [(i * tp + t, (i ^ place) * tp + (t ^...  3.1 us
    pallas_call x1, Pallas kernels, shards(): pl.pallas_call(functools.partial(attend_rest, half, cores, batch, at == 0...  2.33 us
    pallas_call x1, Pallas kernels, shards(): pl.pallas_call(functools.partial(pack, half), out_shape=[bf16(2 * rows, p...  1.59 us
    pallas_call x1, Pallas kernels, shards(): pl.pallas_call(functools.partial(finish_left, peers, cut), out_shape=bf16...  1.49 us
  transfers between devices with their start and end apart: 16, of which 9 were waited for; matrix products, arithmetic and copies ran while one was open for 0% of the time, Pallas kernels for 21%

profile of v3, /device:TPU:0, one launch (start us, length us, event | category | flops | bytes accessed | tf_op | source)
XLA Modules:
  0.0 46.5 jit_solution(3497131502891016927)
XLA Ops:
  0.0 0.0 copy-start.2
  0.0 0.5 collective-permute-start.1
  0.5 1.6 %pack.1 = (bf16[512,128]{1,0:T(8,128)(2,1)S(1)}, bf16[512,128]{1,0:T(8,128)(2,1)S(1)}, bf16[256,128]{1,0:T(8,128)(2,1)S(1)}, bf16[256,128]{1,0:T(8,128)(2,1)S(1)}, bf16[256,2560]{1,0:T(8,128)(2,1)S(1)}) custom-call(bf16[256,256]{1,0:T(8,128)(2,1)} %q.1, bf16[256,256]{1,0:T(8,128)(2,1)} %k.1, bf16[256,256]{1,0:T(8,128)(2,1)} %v.1, bf16[256,5120]{1,0:T(8,128)(2,1)} %weight.2), custom_call_target="tpu_custom_call" | custom-call | bytes 3000000 | tf_op jit(solution)/shard_map/pack/pallas_call | solution.py:302
  2.1 2.6 %collective-permute-start.12 = (bf16[256,2560]{1,0:T(8,128)(2,1)S(1)}, bf16[256,2560]{1,0:T(8,128)(2,1)S(1)}, u32[]{:S(2)}, u32[]{:S(2)}) collective-permute-start(bf16[256,2560]{1,0:T(8,128)(2,1)S(1)} %get-tuple-element.53.left), channel_id=1, source_target_pairs={{0,2},{1,3},{2,0},{3,1},{4,6},{5,7},{6,4},{7,5},{8,10},{9,11},{10,... | collective-permute-start | bytes 3932168 | tf_op jit(solution)/shard_map/ppermute | solution.py:293
  4.7 1.6 %collective-permute-start.3 = (bf16[512,128]{1,0:T(8,128)(2,1)S(1)}, bf16[512,128]{1,0:T(8,128)(2,1)S(1)}, u32[]{:S(2)}, u32[]{:S(2)}) collective-permute-start(bf16[512,128]{1,0:T(8,128)(2,1)S(1)} %get-tuple-element.37.refs_0_), channel_id=1, source_target_pairs={{0,8},{4,12},{8,0},{12,4},{16,24},{20,28},{24,16},{28,20},{1,9},{5... | collective-permute-start | bytes 393224 | tf_op jit(solution)/shard_map/ppermute | solution.py:276
  6.2 2.6 %collective-permute-start = (bf16[512,128]{1,0:T(8,128)(2,1)S(1)}, bf16[512,128]{1,0:T(8,128)(2,1)S(1)}, u32[]{:S(2)}, u32[]{:S(2)}) collective-permute-start(bf16[512,128]{1,0:T(8,128)(2,1)S(1)} %get-tuple-element.34), channel_id=1, source_target_pairs={{0,16},{4,20},{8,24},{12,28},{16,0},{20,4},{24,8},{28,12},{1,17},{... | collective-permute-start | bytes 393224 | tf_op jit(solution)/shard_map/ppermute | solution.py:276
  8.8 1.5 %collective-permute-start.5 = (bf16[512,128]{1,0:T(8,128)(2,1)S(1)}, bf16[512,128]{1,0:T(8,128)(2,1)S(1)}, u32[]{:S(2)}, u32[]{:S(2)}) collective-permute-start(bf16[512,128]{1,0:T(8,128)(2,1)S(1)} %get-tuple-element.37.refs_0_), channel_id=1, source_target_pairs={{0,4},{4,0},{8,12},{12,8},{16,20},{20,16},{24,28},{28,24},{1,5},{5... | collective-permute-start | bytes 393224 | tf_op jit(solution)/shard_map/ppermute | solution.py:276
  10.3 2.4 %collective-permute-done.3.refs_2_ = bf16[512,128]{1,0:T(8,128)(2,1)S(1)} collective-permute-done((bf16[512,128]{1,0:T(8,128)(2,1)S(1)}, bf16[512,128]{1,0:T(8,128)(2,1)S(1)}, u32[]{:S(2)}, u32[]{:S(2)}) %collective-permute-start.3) | collective-permute-done | bytes 131104 | tf_op jit(solution)/shard_map/ppermute | solution.py:276
  12.7 1.5 %collective-permute-start.4 = (bf16[512,128]{1,0:T(8,128)(2,1)S(1)}, bf16[512,128]{1,0:T(8,128)(2,1)S(1)}, u32[]{:S(2)}, u32[]{:S(2)}) collective-permute-start(bf16[512,128]{1,0:T(8,128)(2,1)S(1)} %collective-permute-done.3.refs_2_), channel_id=1, source_target_pairs={{0,4},{4,0},{8,12},{12,8},{16,20},{20,16},{24,28},{28,24},{1,5},{5... | collective-permute-start | bytes 393224 | tf_op jit(solution)/shard_map/ppermute | solution.py:276
  14.2 1.1 %collective-permute-done.refs_4_ = bf16[512,128]{1,0:T(8,128)(2,1)S(1)} collective-permute-done((bf16[512,128]{1,0:T(8,128)(2,1)S(1)}, bf16[512,128]{1,0:T(8,128)(2,1)S(1)}, u32[]{:S(2)}, u32[]{:S(2)}) %collective-permute-start) | collective-permute-done | bytes 131104 | tf_op jit(solution)/shard_map/ppermute | solution.py:276
  15.3 0.0 collective-permute-done.1.refs_2_.core_weight
  15.3 1.4 %collective-permute-start.6 = (bf16[512,128]{1,0:T(8,128)(2,1)S(1)}, bf16[512,128]{1,0:T(8,128)(2,1)S(1)}, u32[]{:S(2)}, u32[]{:S(2)}) collective-permute-start(bf16[512,128]{1,0:T(8,128)(2,1)S(1)} %collective-permute-done.refs_4_), channel_id=1, source_target_pairs={{0,12},{4,8},{8,4},{12,0},{16,28},{20,24},{24,20},{28,16},{1,13},{... | collective-permute-start | bytes 393224 | tf_op jit(solution)/shard_map/ppermute | solution.py:276
  16.7 1.6 %collective-permute-start.7 = (bf16[512,128]{1,0:T(8,128)(2,1)S(1)}, bf16[512,128]{1,0:T(8,128)(2,1)S(1)}, u32[]{:S(2)}, u32[]{:S(2)}) collective-permute-start(bf16[512,128]{1,0:T(8,128)(2,1)S(1)} %collective-permute-done.refs_4_), channel_id=1, source_target_pairs={{0,8},{4,12},{8,0},{12,4},{16,24},{20,28},{24,16},{28,20},{1,9},{5... | collective-permute-start | bytes 393224 | tf_op jit(solution)/shard_map/ppermute | solution.py:276
  18.3 0.0 collective-permute-done.5.refs_3_
  18.3 0.5 %collective-permute-start.8 = (bf16[512,128]{1,0:T(8,128)(2,1)S(1)}, bf16[512,128]{1,0:T(8,128)(2,1)S(1)}, u32[]{:S(2)}, u32[]{:S(2)}) collective-permute-start(bf16[512,128]{1,0:T(8,128)(2,1)S(1)} %collective-permute-done.refs_4_), channel_id=1, source_target_pairs={{0,4},{4,0},{8,12},{12,8},{16,20},{20,16},{24,28},{28,24},{1,5},{5... | collective-permute-start | bytes 393224 | tf_op jit(solution)/shard_map/ppermute | solution.py:276
  18.8 0.9 %collective-permute-done.4.refs_1_ = bf16[512,128]{1,0:T(8,128)(2,1)S(1)} collective-permute-done((bf16[512,128]{1,0:T(8,128)(2,1)S(1)}, bf16[512,128]{1,0:T(8,128)(2,1)S(1)}, u32[]{:S(2)}, u32[]{:S(2)}) %collective-permute-start.4) | collective-permute-done | bytes 131104 | tf_op jit(solution)/shard_map/ppermute | solution.py:276
  19.7 0.2 collective-permute-start.2
  19.9 0.0 copy-done.2
  19.9 1.3 %attend_near.1 = (f32[256,128]{1,0:T(8,128)S(1)}, f32[256,128]{1,0:T(8,128)S(1)}, f32[256,128]{1,0:T(8,128)S(1)}) custom-call(s32[16,16]{1,0:T(8,128)S(1)} %copy-done.2, bf16[256,128]{1,0:T(8,128)(2,1)S(1)} %get-tuple-element.33.queries.q_own, bf16[512,128]{1,0:T(8,128)(2,1)S(1)} %get-tuple-element.37.refs_0_, ...), custom_call_target="tpu_custom_call" | custom-call | bytes 3000000 | tf_op jit(solution)/shard_map/attend_near/pallas_call | solution.py:340
  21.2 4.4 %collective-permute-done.2.q_far = bf16[256,128]{1,0:T(8,128)(2,1)S(1)} collective-permute-done((bf16[256,128]{1,0:T(8,128)(2,1)S(1)}, bf16[256,128]{1,0:T(8,128)(2,1)S(1)}, u32[]{:S(2)}, u32[]{:S(2)}) %collective-permute-start.2) | collective-permute-done | bytes 65568 | tf_op jit(solution)/shard_map/ppermute | solution.py:276
  25.6 0.0 collective-permute-done.6.refs_5_
  25.6 0.0 collective-permute-done.7.refs_6_
  25.6 0.0 collective-permute-done.8.refs_7_
  25.6 2.3 %attend_rest.1 = (bf16[128,128]{1,0:T(8,128)(2,1)S(1)}, bf16[128,128]{1,0:T(8,128)(2,1)S(1)}, bf16[128,128]{1,0:T(8,128)(2,1)S(1)}, bf16[128,128]{1,0:T(8,128)(2,1)S(1)}) custom-call(s32[16,16]{1,0:T(8,128)S(1)} %copy-done.2, bf16[256,128]{1,0:T(8,128)(2,1)S(1)} %get-tuple-element.33.queries.q_own, bf16[256,128]{1,0:T(8,128)(2,1)S(1)} %collective-permute-done.2.q_far, ...), custom_call_target="tpu_custom_call" | custom-call | bytes 9000000 | tf_op jit(solution)/shard_map/attend_rest/pallas_call | solution.py:354
  27.9 1.0 %collective-permute-start.9 = (bf16[128,128]{1,0:T(8,128)(2,1)S(1)}, bf16[128,128]{1,0:T(8,128)(2,1)S(1)}, u32[]{:S(2)}, u32[]{:S(2)}) collective-permute-start(bf16[128,128]{1,0:T(8,128)(2,1)S(1)} %get-tuple-element.43), channel_id=1, source_target_pairs={{0,16},{1,17},{2,18},{3,19},{4,20},{5,21},{6,22},{7,23},{8,24},{9,... | collective-permute-start | bytes 98312 | tf_op jit(solution)/shard_map/ppermute | solution.py:279
  29.0 0.0 collective-permute-start.10
  29.0 2.1 %collective-permute-start.11 = (bf16[128,128]{1,0:T(8,128)(2,1)S(1)}, bf16[128,128]{1,0:T(8,128)(2,1)S(1)}, u32[]{:S(2)}, u32[]{:S(2)}) collective-permute-start(bf16[128,128]{1,0:T(8,128)(2,1)S(1)} %get-tuple-element.45), channel_id=1, source_target_pairs={{0,17},{1,16},{2,19},{3,18},{4,21},{5,20},{6,23},{7,22},{8,25},{9,... | collective-permute-start | bytes 98312 | tf_op jit(solution)/shard_map/ppermute | solution.py:279
  31.0 1.3 %stage.1.refs_1_.right = bf16[256,2560]{1,0:T(8,128)(2,1)S(1)} custom-call(bf16[256,5120]{1,0:T(8,128)(2,1)} %weight.2), custom_call_target="tpu_custom_call" | custom-call | bytes 3000000 | tf_op jit(solution)/shard_map/stage/pallas_call | solution.py:324
  32.4 0.5 %collective-permute-done.9.far = bf16[128,128]{1,0:T(8,128)(2,1)S(1)} collective-permute-done((bf16[128,128]{1,0:T(8,128)(2,1)S(1)}, bf16[128,128]{1,0:T(8,128)(2,1)S(1)}, u32[]{:S(2)}, u32[]{:S(2)}) %collective-permute-start.9) | collective-permute-done | bytes 32800 | tf_op jit(solution)/shard_map/ppermute | solution.py:279
  32.9 0.0 collective-permute-done.10.other
  32.9 0.3 collective-permute-done.11.far_other
  33.3 0.5 %project_peers.1 = (bf16[64,2176]{1,0:T(8,128)(2,1)S(1)}, bf16[64,896]{1,0:T(8,128)(2,1)S(1)}) custom-call(bf16[64,512]{1,0:T(8,128)(2,1)S(1)} %get-tuple-element.47.refs_0_, bf16[256,2560]{1,0:T(8,128)(2,1)S(1)} %stage.1.refs_1_.right, bf16[256,5120]{1,0:T(8,128)(2,1)S(1)} %collective-permute-done.1.refs_2_.core_weight), custom_call_target="tpu_custom_call" | custom-call | bytes 3000000 | tf_op jit(solution)/shard_map/project_peers/pallas_call | solution.py:377
  33.8 0.0 copy-start
  33.8 0.0 copy-start.1
  33.8 0.3 collective-permute-done.12.refs_1_
  34.1 0.6 %collective-permute-start.15 = (bf16[256,2560]{1,0:T(8,128)(2,1)S(1)}, bf16[256,2560]{1,0:T(8,128)(2,1)S(1)}, u32[]{:S(2)}, u32[]{:S(2)}) collective-permute-start(bf16[256,2560]{1,0:T(8,128)(2,1)S(1)} %collective-permute-done.12.refs_1_), channel_id=1, source_target_pairs={{0,1},{1,0},{2,3},{3,2},{4,5},{5,4},{6,7},{7,6},{8,9},{9,8},{10,11... | collective-permute-start | bytes 3932168 | tf_op jit(solution)/shard_map/ppermute | solution.py:290
  34.7 1.1 %collective-permute-start.14 = (bf16[64,2176]{1,0:T(8,128)(2,1)S(1)}, bf16[64,2176]{1,0:T(8,128)(2,1)S(1)}, u32[]{:S(2)}, u32[]{:S(2)}) collective-permute-start(bf16[64,2176]{1,0:T(8,128)(2,1)S(1)} %get-tuple-element.59), channel_id=1, source_target_pairs={{0,2},{1,3},{2,0},{3,1},{4,6},{5,7},{6,4},{7,5},{8,10},{9,11},{10,... | collective-permute-start | bytes 835592 | tf_op jit(solution)/shard_map/ppermute | solution.py:293
  35.8 0.9 %collective-permute-start.13 = (bf16[64,896]{1,0:T(8,128)(2,1)S(1)}, bf16[64,896]{1,0:T(8,128)(2,1)S(1)}, u32[]{:S(2)}, u32[]{:S(2)}) collective-permute-start(bf16[64,896]{1,0:T(8,128)(2,1)S(1)} %get-tuple-element.57), channel_id=1, source_target_pairs={{0,2},{1,3},{2,0},{3,1},{4,6},{5,7},{6,4},{7,5},{8,10},{9,11},{10,... | collective-permute-start | bytes 344072 | tf_op jit(solution)/shard_map/ppermute | solution.py:293
  36.8 1.0 %project_own.1 = (f32[64,2560]{1,0:T(8,128)S(1)}, f32[64,2560]{1,0:T(8,128)S(1)}) custom-call(bf16[64,512]{1,0:T(8,128)(2,1)S(1)} %get-tuple-element.52.attended, bf16[256,2560]{1,0:T(8,128)(2,1)S(1)} %get-tuple-element.53.left, bf16[256,2560]{1,0:T(8,128)(2,1)S(1)} %stage.1.refs_1_.right, bf16[256,5120]{1,0:T(8,128)(2,1)S(1)} %collective-permute-done.1.refs_2_.core_weight), custom_call_target="tpu_custom_call" | custom-call | bytes 3000000 | tf_op jit(solution)/shard_map/project_own/pallas_call | solution.py:387
  37.8 6.5 %collective-permute-done.14.refs_0_ = bf16[64,2176]{1,0:T(8,128)(2,1)S(1)} collective-permute-done((bf16[64,2176]{1,0:T(8,128)(2,1)S(1)}, bf16[64,2176]{1,0:T(8,128)(2,1)S(1)}, u32[]{:S(2)}, u32[]{:S(2)}) %collective-permute-start.14) | collective-permute-done | bytes 278560 | tf_op jit(solution)/shard_map/ppermute | solution.py:293
  44.2 0.0 collective-permute-done.15.refs_2_
  44.2 0.0 copy-done
  44.2 0.0 copy-done.1
  44.3 1.5 %finish_left.1.refs_1_ = bf16[64,5120]{1,0:T(8,128)(2,1)} custom-call(bf16[64,5120]{1,0:T(8,128)(2,1)S(1)} %copy-done, f32[1,5120]{1,0:T(1,128)S(1)} %bitcast.1, f32[64,2560]{1,0:T(8,128)S(1)} %get-tuple-element.58.own_left, f32[64,2560]{1,0:T(8,128)S(1)} %get-tuple-element.54.own_right.own, bf16[64,2176]{1,0:T(8,128)(2,1)S(1)} %collective-permute-done.14.refs_0_, ...), custom_call_target="tpu_custom_call" | custom-call | bytes 6000000 | tf_op jit(solution)/shard_map/finish_left/pallas_call | solution.py:401
  45.8 0.1 collective-permute-done.13.refs_0_
  45.8 0.7 %finish_right.1 = bf16[64,5120]{1,0:T(8,128)(2,1)} custom-call(bf16[64,5120]{1,0:T(8,128)(2,1)S(1)} %copy-done, f32[1,5120]{1,0:T(1,128)S(1)} %bitcast.2, f32[64,2560]{1,0:T(8,128)S(1)} %get-tuple-element.54.own_right.own, bf16[64,896]{1,0:T(8,128)(2,1)S(1)} %collective-permute-done.13.refs_0_, ...), custom_call_target="tpu_custom_call", output_to_operand_aliasing={{}: (4, {})} | custom-call | bytes 3000000 | tf_op jit(solution)/shard_map/finish_right/pallas_call | solution.py:411
  (1 shorter events, 0.0 us)
Async XLA Ops:
  0.0 19.9 %copy-start.2 = (s32[16,16]{1,0:T(8,128)S(1)}, s32[16,16]{1,0:T(8,128)}, u32[]{:S(2)}) copy-start(s32[16,16]{1,0:T(8,128)} %mask.3) | copy-start | bytes 3076
  0.0 15.3 %collective-permute-start.1 = (bf16[256,5120]{1,0:T(8,128)(2,1)}, bf16[256,5120]{1,0:T(8,128)(2,1)S(1)}, u32[]{:S(2)}, u32[]{:S(2)}) collective-permute-start(bf16[256,5120]{1,0:T(8,128)(2,1)} %weight.2), channel_id=1, source_target_pairs={{0,1},{1,0},{2,3},{3,2},{4,5},{5,4},{6,7},{7,6},{8,9},{9,8},{10,11... | collective-permute-start | bytes 7864328 | tf_op jit(solution)/shard_map/ppermute | solution.py:290
  2.1 32.0 %collective-permute-start.12 = (bf16[256,2560]{1,0:T(8,128)(2,1)S(1)}, bf16[256,2560]{1,0:T(8,128)(2,1)S(1)}, u32[]{:S(2)}, u32[]{:S(2)}) collective-permute-start(bf16[256,2560]{1,0:T(8,128)(2,1)S(1)} %get-tuple-element.53.left), channel_id=1, source_target_pairs={{0,2},{1,3},{2,0},{3,1},{4,6},{5,7},{6,4},{7,5},{8,10},{9,11},{10,... | collective-permute-start | bytes 3932168 | tf_op jit(solution)/shard_map/ppermute | solution.py:293
  4.7 8.1 %collective-permute-start.3 = (bf16[512,128]{1,0:T(8,128)(2,1)S(1)}, bf16[512,128]{1,0:T(8,128)(2,1)S(1)}, u32[]{:S(2)}, u32[]{:S(2)}) collective-permute-start(bf16[512,128]{1,0:T(8,128)(2,1)S(1)} %get-tuple-element.37.refs_0_), channel_id=1, source_target_pairs={{0,8},{4,12},{8,0},{12,4},{16,24},{20,28},{24,16},{28,20},{1,9},{5... | collective-permute-start | bytes 393224 | tf_op jit(solution)/shard_map/ppermute | solution.py:276
  6.2 9.1 %collective-permute-start = (bf16[512,128]{1,0:T(8,128)(2,1)S(1)}, bf16[512,128]{1,0:T(8,128)(2,1)S(1)}, u32[]{:S(2)}, u32[]{:S(2)}) collective-permute-start(bf16[512,128]{1,0:T(8,128)(2,1)S(1)} %get-tuple-element.34), channel_id=1, source_target_pairs={{0,16},{4,20},{8,24},{12,28},{16,0},{20,4},{24,8},{28,12},{1,17},{... | collective-permute-start | bytes 393224 | tf_op jit(solution)/shard_map/ppermute | solution.py:276
  8.8 9.5 %collective-permute-start.5 = (bf16[512,128]{1,0:T(8,128)(2,1)S(1)}, bf16[512,128]{1,0:T(8,128)(2,1)S(1)}, u32[]{:S(2)}, u32[]{:S(2)}) collective-permute-start(bf16[512,128]{1,0:T(8,128)(2,1)S(1)} %get-tuple-element.37.refs_0_), channel_id=1, source_target_pairs={{0,4},{4,0},{8,12},{12,8},{16,20},{20,16},{24,28},{28,24},{1,5},{5... | collective-permute-start | bytes 393224 | tf_op jit(solution)/shard_map/ppermute | solution.py:276
  12.7 7.0 %collective-permute-start.4 = (bf16[512,128]{1,0:T(8,128)(2,1)S(1)}, bf16[512,128]{1,0:T(8,128)(2,1)S(1)}, u32[]{:S(2)}, u32[]{:S(2)}) collective-permute-start(bf16[512,128]{1,0:T(8,128)(2,1)S(1)} %collective-permute-done.3.refs_2_), channel_id=1, source_target_pairs={{0,4},{4,0},{8,12},{12,8},{16,20},{20,16},{24,28},{28,24},{1,5},{5... | collective-permute-start | bytes 393224 | tf_op jit(solution)/shard_map/ppermute | solution.py:276
  15.3 10.2 %collective-permute-start.6 = (bf16[512,128]{1,0:T(8,128)(2,1)S(1)}, bf16[512,128]{1,0:T(8,128)(2,1)S(1)}, u32[]{:S(2)}, u32[]{:S(2)}) collective-permute-start(bf16[512,128]{1,0:T(8,128)(2,1)S(1)} %collective-permute-done.refs_4_), channel_id=1, source_target_pairs={{0,12},{4,8},{8,4},{12,0},{16,28},{20,24},{24,20},{28,16},{1,13},{... | collective-permute-start | bytes 393224 | tf_op jit(solution)/shard_map/ppermute | solution.py:276
  16.7 8.9 %collective-permute-start.7 = (bf16[512,128]{1,0:T(8,128)(2,1)S(1)}, bf16[512,128]{1,0:T(8,128)(2,1)S(1)}, u32[]{:S(2)}, u32[]{:S(2)}) collective-permute-start(bf16[512,128]{1,0:T(8,128)(2,1)S(1)} %collective-permute-done.refs_4_), channel_id=1, source_target_pairs={{0,8},{4,12},{8,0},{12,4},{16,24},{20,28},{24,16},{28,20},{1,9},{5... | collective-permute-start | bytes 393224 | tf_op jit(solution)/shard_map/ppermute | solution.py:276
  18.3 7.3 %collective-permute-start.8 = (bf16[512,128]{1,0:T(8,128)(2,1)S(1)}, bf16[512,128]{1,0:T(8,128)(2,1)S(1)}, u32[]{:S(2)}, u32[]{:S(2)}) collective-permute-start(bf16[512,128]{1,0:T(8,128)(2,1)S(1)} %collective-permute-done.refs_4_), channel_id=1, source_target_pairs={{0,4},{4,0},{8,12},{12,8},{16,20},{20,16},{24,28},{28,24},{1,5},{5... | collective-permute-start | bytes 393224 | tf_op jit(solution)/shard_map/ppermute | solution.py:276
  19.7 5.9 %collective-permute-start.2 = (bf16[256,128]{1,0:T(8,128)(2,1)S(1)}, bf16[256,128]{1,0:T(8,128)(2,1)S(1)}, u32[]{:S(2)}, u32[]{:S(2)}) collective-permute-start(bf16[256,128]{1,0:T(8,128)(2,1)S(1)} %get-tuple-element.36), channel_id=1, source_target_pairs={{0,16},{4,20},{8,24},{12,28},{16,0},{20,4},{24,8},{28,12},{1,17},{... | collective-permute-start | bytes 196616 | tf_op jit(solution)/shard_map/ppermute | solution.py:276
  27.9 5.0 %collective-permute-start.9 = (bf16[128,128]{1,0:T(8,128)(2,1)S(1)}, bf16[128,128]{1,0:T(8,128)(2,1)S(1)}, u32[]{:S(2)}, u32[]{:S(2)}) collective-permute-start(bf16[128,128]{1,0:T(8,128)(2,1)S(1)} %get-tuple-element.43), channel_id=1, source_target_pairs={{0,16},{1,17},{2,18},{3,19},{4,20},{5,21},{6,22},{7,23},{8,24},{9,... | collective-permute-start | bytes 98312 | tf_op jit(solution)/shard_map/ppermute | solution.py:279
  29.0 3.9 %collective-permute-start.10 = (bf16[128,128]{1,0:T(8,128)(2,1)S(1)}, bf16[128,128]{1,0:T(8,128)(2,1)S(1)}, u32[]{:S(2)}, u32[]{:S(2)}) collective-permute-start(bf16[128,128]{1,0:T(8,128)(2,1)S(1)} %get-tuple-element.44), channel_id=1, source_target_pairs={{0,1},{1,0},{2,3},{3,2},{4,5},{5,4},{6,7},{7,6},{8,9},{9,8},{10,11... | collective-permute-start | bytes 98312 | tf_op jit(solution)/shard_map/ppermute | solution.py:279
  29.0 4.3 %collective-permute-start.11 = (bf16[128,128]{1,0:T(8,128)(2,1)S(1)}, bf16[128,128]{1,0:T(8,128)(2,1)S(1)}, u32[]{:S(2)}, u32[]{:S(2)}) collective-permute-start(bf16[128,128]{1,0:T(8,128)(2,1)S(1)} %get-tuple-element.45), channel_id=1, source_target_pairs={{0,17},{1,16},{2,19},{3,18},{4,21},{5,20},{6,23},{7,22},{8,25},{9,... | collective-permute-start | bytes 98312 | tf_op jit(solution)/shard_map/ppermute | solution.py:279
  33.8 10.5 %copy-start = (bf16[64,5120]{1,0:T(8,128)(2,1)S(1)}, bf16[64,5120]{1,0:T(8,128)(2,1)}, u32[]{:S(2)}) copy-start(bf16[64,5120]{1,0:T(8,128)(2,1)} %residual.3) | copy-start | bytes 1966084
  33.8 10.4 %copy-start.1 = (f32[5120]{0:T(1024)S(1)}, f32[5120]{0:T(1024)}, u32[]{:S(2)}) copy-start(f32[5120]{0:T(1024)} %param.12) | copy-start | bytes 61444
  34.1 10.2 %collective-permute-start.15 = (bf16[256,2560]{1,0:T(8,128)(2,1)S(1)}, bf16[256,2560]{1,0:T(8,128)(2,1)S(1)}, u32[]{:S(2)}, u32[]{:S(2)}) collective-permute-start(bf16[256,2560]{1,0:T(8,128)(2,1)S(1)} %collective-permute-done.12.refs_1_), channel_id=1, source_target_pairs={{0,1},{1,0},{2,3},{3,2},{4,5},{5,4},{6,7},{7,6},{8,9},{9,8},{10,11... | collective-permute-start | bytes 3932168 | tf_op jit(solution)/shard_map/ppermute | solution.py:290
  34.7 9.5 %collective-permute-start.14 = (bf16[64,2176]{1,0:T(8,128)(2,1)S(1)}, bf16[64,2176]{1,0:T(8,128)(2,1)S(1)}, u32[]{:S(2)}, u32[]{:S(2)}) collective-permute-start(bf16[64,2176]{1,0:T(8,128)(2,1)S(1)} %get-tuple-element.59), channel_id=1, source_target_pairs={{0,2},{1,3},{2,0},{3,1},{4,6},{5,7},{6,4},{7,5},{8,10},{9,11},{10,... | collective-permute-start | bytes 835592 | tf_op jit(solution)/shard_map/ppermute | solution.py:293
  35.8 10.0 %collective-permute-start.13 = (bf16[64,896]{1,0:T(8,128)(2,1)S(1)}, bf16[64,896]{1,0:T(8,128)(2,1)S(1)}, u32[]{:S(2)}, u32[]{:S(2)}) collective-permute-start(bf16[64,896]{1,0:T(8,128)(2,1)S(1)} %get-tuple-element.57), channel_id=1, source_target_pairs={{0,2},{1,3},{2,0},{3,1},{4,6},{5,7},{6,4},{7,5},{8,10},{9,11},{10,... | collective-permute-start | bytes 344072 | tf_op jit(solution)/shard_map/ppermute | solution.py:293

commit v4 on v3

--- a/solution.py
+++ b/solution.py
@@ -16,7 +16,7 @@
 BATCH = 4
 LANES = 128
 CUT_NUM, CUT_DEN = 1, 2
-HEAD_NUM, HEAD_DEN = 2, 3
+HEAD_NUM, HEAD_DEN = 1, 3
 
 VMEM = pltpu.MemorySpace.VMEM
 SMEM = pltpu.MemorySpace.SMEM
@@ -65,30 +65,21 @@
         copy.wait()
 
 
-def attend(queries, place, mask, pieces, state):
+def attend(queries, first_row, bias, pieces, state):
     rows = queries.shape[0]
     blocks = rows // BLOCK
-    bias = [
-        [
-            [
-                jnp.where(mask[place * blocks + a, owner * blocks + b] > 0, 0.0, NEGATIVE)
-                for b in range(blocks)
-            ]
-            for a in range(blocks)
-        ]
-        for _, owner in pieces
-    ]
     outs = {}
     for head in range(queries.shape[1] // HD):
         at = slice(head * HD, (head + 1) * HD)
         raw = [dot(queries[:, at], piece[:rows, at], ((1,), (1,))) for piece, _ in pieces]
         for a in range(blocks):
             band = slice(a * BLOCK, (a + 1) * BLOCK)
-            tiles = [
-                raw[n][band, b * BLOCK : (b + 1) * BLOCK] * SCORE_SCALE + bias[n][a][b]
-                for n in range(len(pieces))
-                for b in range(blocks)
-            ]
+            tiles = []
+            for n, (_, place) in enumerate(pieces):
+                for b in range(blocks):
+                    row = (first_row + a) * bias.shape[0] // (2 * blocks) + place * blocks + b
+                    tile = raw[n][band, b * BLOCK : (b + 1) * BLOCK]
+                    tiles.append(tile * SCORE_SCALE + bias[row : row + 1, :])
             top = jnp.max(functools.reduce(jnp.maximum, tiles), axis=1, keepdims=True)
             if state is not None:
                 old_top, old_total, old_summed = (ref[band, at] for ref in state)
@@ -118,51 +109,48 @@
         new_summed[where] = summed
 
 
-def attend_near(places, first, mask, queries, *refs):
+def attend_first(half, places, mask, queries, *refs):
+    bias, state = refs[-4], refs[-3:]
     me = lax.axis_index("seq")
-    pieces = [(ref, me ^ place) for ref, place in zip(refs, places)]
-    state = None if first else refs[len(places) : -3]
-    keep_state(attend(queries, me, mask, pieces, state), refs[-3:])
-
-
-def attend_rest(half, cores, places, first, last, mask, q_own, q_far, *refs):
-    count = len(places)
-    near, far = refs[:count], refs[count : 2 * count]
-    own_state, rest = refs[2 * count : 2 * count + 3], refs[2 * count + 3 :]
-    far_state = None
-    if not first:
-        far_state, rest = rest[:3], rest[3:]
-    me = lax.axis_index("seq")
-    near = [(ref, me ^ place) for ref, place in zip(near, places)]
-    far = [(ref, me ^ half ^ place) for ref, place in zip(far, places)]
-    for_far = attend(q_far, me ^ half, mask, near + far, far_state)
-    for_own = attend(q_own, me, mask, far, own_state)
+    blocks = queries.shape[0] // BLOCK
+    keys = bias.shape[0] // (2 * blocks)
+    for a in range(2 * blocks):
+        row = (me if a < blocks else me ^ half) * blocks + a % blocks
+        for b in range(keys):
+            column = (me ^ (b // blocks)) * blocks + b % blocks
+            allowed = jnp.where(mask[row, column] > 0, 0.0, NEGATIVE)
+            bias[a * keys + b : a * keys + b + 1, :] = jnp.full((1, BLOCK), allowed, jnp.float32)
+    keep_state(attend(queries, 0, bias, list(zip(refs, places)), None), state)
+
+
+def attend_more(first_row, cores, places, last, stateful, bias, queries, *refs):
+    pieces, rest = list(zip(refs, places)), refs[len(places) :]
+    state = None
+    if stateful:
+        state, rest = rest[:3], rest[3:]
+    outs = attend(queries, first_row, bias, pieces, state)
     if not last:
-        keep_state(for_own, rest[:3])
-        keep_state(for_far, rest[3:])
+        keep_state(outs, rest)
         return
-    own_mine, own_other, far_mine, far_other = rest
+    mine, other = rest
     core = lax.rem(lax.axis_index("tp"), cores)
     chips = lax.axis_size("tp") // cores
-    rows, width = q_own.shape
+    rows, width = queries.shape
     share = rows // (chips * cores)
-    for outs, mine, other in ((for_far, far_mine, far_other), (for_own, own_mine, own_other)):
-        for head in range(width // HD):
-            at = slice(head * HD, (head + 1) * HD)
-            whole = []
-            for a in range(rows // BLOCK):
-                _, total, summed = outs[head, a]
-                whole.append(
-                    (summed / jnp.sum(total, axis=1, keepdims=True)).astype(jnp.bfloat16)
-                )
-            whole = jnp.concatenate(whole, axis=0)
-            for chip in range(chips):
-                start = chip * cores * share
-                one = whole[start : start + share]
-                two = whole[start + share : start + 2 * share]
-                to = slice(chip * share, (chip + 1) * share)
-                mine[to, at] = jnp.where(core == 0, one, two)
-                other[to, at] = jnp.where(core == 0, two, one)
+    for head in range(width // HD):
+        at = slice(head * HD, (head + 1) * HD)
+        whole = []
+        for a in range(rows // BLOCK):
+            _, total, summed = outs[head, a]
+            whole.append((summed / jnp.sum(total, axis=1, keepdims=True)).astype(jnp.bfloat16))
+        whole = jnp.concatenate(whole, axis=0)
+        for chip in range(chips):
+            start = chip * cores * share
+            one = whole[start : start + share]
+            two = whole[start + share : start + 2 * share]
+            to = slice(chip * share, (chip + 1) * share)
+            mine[to, at] = jnp.where(core == 0, one, two)
+            other[to, at] = jnp.where(core == 0, two, one)
 
 
 def stage(weight, right, sem):
@@ -225,19 +213,27 @@
     copy.wait()
 
 
-def finish_left(peers, cut, residual, gate, own_left, own_right, *refs):
+def finish_head(residual, gate, own_right, *refs):
+    firsts, (out, block, sem) = refs[:-3], refs[-3:]
+    head = block.shape[1]
+    cut = out.shape[1] - own_right.shape[1]
+    branch = own_right[:, :head]
+    for first in firsts:
+        branch = branch + first[:, first.shape[1] - head :].astype(jnp.float32)
+    columns = slice(cut, cut + head)
+    block[...] = gated(residual[:, columns], gate[:, columns], branch)
+    write_out(block, out, columns, sem)
+
+
+def finish_left(peers, cut, residual, gate, own, *refs):
     firsts, weights, core_weights = refs[:peers], refs[peers : 2 * peers], refs[2 * peers : 3 * peers]
-    out, block, sem = refs[3 * peers :]
-    end = block.shape[1]
-    head = end - cut
-    left, right = own_left[...], own_right[:, :head]
+    _, out, block, sem = refs[3 * peers :]
+    branch = own[...]
     for first, weight, core_weight in zip(firsts, weights, core_weights):
-        rows = first.shape[1] - head
-        left = left + project(first.at[:, :rows], weight, core_weight, slice(None))
-        right = right + first[:, rows:].astype(jnp.float32)
-    block[:, :cut] = gated(residual[:, :cut], gate[:, :cut], left)
-    block[:, cut:] = gated(residual[:, cut:end], gate[:, cut:end], right)
-    write_out(block, out, slice(0, end), sem)
+        rows = 2 * weight.shape[0]
+        branch = branch + project(first.at[:, :rows], weight, core_weight, slice(None))
+    block[...] = gated(residual[:, :cut], gate[:, :cut], branch)
+    write_out(block, out, slice(0, cut), sem)
 
 
 def finish_right(residual, gate, own, *refs):
@@ -252,7 +248,9 @@
 
 
 def cost(microseconds):
-    return pl.CostEstimate(flops=0, bytes_accessed=microseconds * 3_000_000, transcendentals=0)
+    return pl.CostEstimate(
+        flops=int(microseconds * 1_000_000_000), bytes_accessed=0, transcendentals=0
+    )
 
 
 def params(mib):
@@ -306,11 +304,11 @@
         out_specs=in_vmem(5),
         scratch_shapes=[pltpu.SemaphoreType.DMA((7,))],
         compiler_params=params(16),
-        cost_estimate=cost(1),
+        cost_estimate=cost(1.6),
         name="pack",
     )(*in_hbm(queries, keys, values, out_weight))
     kv_far = swap(kv_send, half)
-    order = list(range(half - 1, 0, -1))
+    order = sorted(range(1, half), key=lambda m: (m.bit_count(), -m))
     direct = [m for m in order if m % 2 == 0 or m == 1]
     near = {m: swap(kv_keep, m) for m in direct}
     chip_weights = [to_chip(left, step) for step in range(1, chips)]
@@ -328,40 +326,45 @@
         out_specs=pl.BlockSpec(memory_space=VMEM),
         scratch_shapes=[pltpu.SemaphoreType.DMA],
         compiler_params=params(16),
-        cost_estimate=cost(1),
+        cost_estimate=cost(1.3),
         name="stage",
     )(*in_hbm(weight))
     near[0], far[0] = kv_keep, kv_far
     places = [0] + order
     batches = [places[at : at + BATCH] for at in range(0, len(places), BATCH)]
-    smem = pl.BlockSpec(memory_space=SMEM)
-    own_state = []
-    for at, batch in enumerate(batches):
-        own_state = pl.pallas_call(
-            functools.partial(attend_near, batch, at == 0),
-            out_shape=[f32(rows, part)] * 3,
-            in_specs=[smem] + in_vmem(1 + len(batch) + len(own_state)),
-            out_specs=in_vmem(3),
-            compiler_params=params(32),
-            cost_estimate=cost(1),
-            name="attend_near",
-        )(block_mask, q_keep, *[near[m] for m in batch], *own_state)
-    far_state = []
-    for at, batch in enumerate(batches):
-        last = at == len(batches) - 1
-        state = [*own_state, *far_state]
-        out_shape = [bf16(rows // cores, part)] * 4 if last else [f32(rows, part)] * 6
-        outs = pl.pallas_call(
-            functools.partial(attend_rest, half, cores, batch, at == 0, last),
-            out_shape=out_shape,
-            in_specs=[smem] + in_vmem(2 + 2 * len(batch) + len(state)),
-            out_specs=in_vmem(len(out_shape)),
-            compiler_params=params(32),
-            cost_estimate=cost(3),
-            name="attend_rest",
-        )(block_mask, q_keep, q_far, *[near[m] for m in batch], *[far[m] for m in batch], *state)
-        own_state, far_state = outs[:3], outs[3:]
-    own_mine, own_other, far_mine, far_other = outs
+    blocks = rows // BLOCK
+    state_shape = [f32(rows, part)] * 3
+
+    def attend_all(first_row, queries, batches, state, microseconds):
+        for at, pieces in enumerate(batches):
+            last = at == len(batches) - 1
+            out_shape = [bf16(rows // cores, part)] * 2 if last else state_shape
+            held = [place for place, _ in pieces]
+            state = pl.pallas_call(
+                functools.partial(attend_more, first_row, cores, held, last, bool(state)),
+                out_shape=out_shape,
+                in_specs=in_vmem(2 + len(pieces) + len(state)),
+                out_specs=in_vmem(len(out_shape)),
+                compiler_params=params(32),
+                cost_estimate=cost(microseconds),
+                name="attend_far" if first_row else "attend_own",
+            )(bias, queries, *[array for _, array in pieces], *state)
+        return state
+
+    bias, *own_state = pl.pallas_call(
+        functools.partial(attend_first, half, batches[0]),
+        out_shape=[f32(2 * blocks * seq * blocks, BLOCK)] + state_shape,
+        in_specs=[pl.BlockSpec(memory_space=SMEM)] + in_vmem(1 + len(batches[0])),
+        out_specs=in_vmem(4),
+        compiler_params=params(32),
+        cost_estimate=cost(1.3),
+        name="attend_near",
+    )(block_mask, q_keep, *[near[m] for m in batches[0]])
+    near_batches = [[(m, near[m]) for m in batch] for batch in batches]
+    far_batches = [[(m ^ half, far[m]) for m in batch] for batch in batches]
+    both = [one + two for one, two in zip(near_batches, far_batches)]
+    far_mine, far_other = attend_all(blocks, q_far, both, [], 2)
+    own_mine, own_other = attend_all(0, q_keep, near_batches[1:] + far_batches, own_state, 1)
     from_far = across(far_mine, half, 0)
     from_far_core = across(far_other, half, 1)
     from_core = across(own_other, 0, 1)
@@ -371,7 +374,7 @@
         in_specs=in_vmem(4),
         out_specs=in_vmem(chips),
         compiler_params=params(16),
-        cost_estimate=cost(1),
+        cost_estimate=cost(0.1),
         name="line_up",
     )(own_mine, from_far, from_core, from_far_core)
     sums = pl.pallas_call(
@@ -380,34 +383,45 @@
         in_specs=in_vmem(peers + 2),
         out_specs=in_vmem(2 * peers),
         compiler_params=params(32),
-        cost_estimate=cost(1),
+        cost_estimate=cost(0.5),
         name="project_peers",
     )(*lined[1:], right, core_weight)
-    mine, *sums = lax.optimization_barrier((lined[0], *sums))
+    mine, chip_weights, *_ = lax.optimization_barrier((lined[0], chip_weights, *sums))
     own_left, own_right = pl.pallas_call(
         functools.partial(project_own, cut),
         out_shape=[f32(share, cut), f32(share, columns - cut)],
         in_specs=in_vmem(4),
         out_specs=in_vmem(2),
         compiler_params=params(32),
-        cost_estimate=cost(1),
+        cost_estimate=cost(0.1),
         name="project_own",
     )(mine, left, right, core_weight)
-    sums, chip_weights = lax.optimization_barrier((sums, chip_weights))
     firsts = [to_chip(array, step) for step, array in enumerate(sums[::2], 1)]
     seconds = [to_chip(array, step) for step, array in enumerate(sums[1::2], 1)]
     chip_core_weights = [swap_cores(weight) for weight in chip_weights]
     gate = gate[None, :]
+    anywhere = pl.BlockSpec(memory_space=pl.ANY)
+    out = pl.pallas_call(
+        finish_head,
+        out_shape=bf16(share, columns),
+        in_specs=in_vmem(3 + peers),
+        out_specs=anywhere,
+        scratch_shapes=[pltpu.VMEM((share, head), jnp.bfloat16), pltpu.SemaphoreType.DMA],
+        compiler_params=params(16),
+        cost_estimate=cost(20),
+        name="finish_head",
+    )(residual, gate, own_right, *firsts)
     out = pl.pallas_call(
         functools.partial(finish_left, peers, cut),
         out_shape=bf16(share, columns),
-        in_specs=in_vmem(4 + 3 * peers),
-        out_specs=pl.BlockSpec(memory_space=pl.ANY),
-        scratch_shapes=[pltpu.VMEM((share, cut + head), jnp.bfloat16), pltpu.SemaphoreType.DMA],
+        in_specs=in_vmem(3 + 3 * peers) + [anywhere],
+        out_specs=anywhere,
+        scratch_shapes=[pltpu.VMEM((share, cut), jnp.bfloat16), pltpu.SemaphoreType.DMA],
+        input_output_aliases={3 + 3 * peers: 0},
         compiler_params=params(32),
-        cost_estimate=cost(2),
+        cost_estimate=cost(1.5),
         name="finish_left",
-    )(residual, gate, own_left, own_right, *firsts, *chip_weights, *chip_core_weights)
+    )(residual, gate, own_left, *firsts, *chip_weights, *chip_core_weights, out)
     return pl.pallas_call(
         finish_right,
         out_shape=bf16(share, columns),
@@ -419,7 +433,7 @@
         ],
         input_output_aliases={3 + peers: 0},
         compiler_params=params(16),
-        cost_estimate=cost(1),
+        cost_estimate=cost(0.7),
         name="finish_right",
     )(residual, gate, own_right, *seconds, out)
 

time: 46.7 us -> 45.2 us (0.968)
  waiting for transfers between devices: 16.5 us -> 15.2 us
  starting transfers between devices: 19.6 us -> 19.1 us
    ppermute x3, waiting for transfers between devices: 6.81 us -> 6.03 us  [to_chip(): lax.ppermute(array, 'tp', [(t, (t // cores + step) % chips * cores + t %...]
    ppermute x2, starting transfers between devices: 1.09 us -> 0.46 us  [swap_cores(): return lax.ppermute(array, 'tp', [(t, t ^ 1) for t in range(tp)])]
    pallas_call x2 -> x4, Pallas kernels: 3.61 us -> 3.94 us  [the longest x2 1.91 us: attend_all(): pl.pallas_call(functools.partial(attend_more, first_row, cores, held, las...]
  transfers between devices with their start and end apart: 16 -> 16, of which waited for: 9 -> 8; matrix products, arithmetic and copies ran while one was open for 0% -> 0% of each run, Pallas kernels for 21% -> 22%
where the time goes in v4:
time: 45.2 us; the launch traced here: 45 us
  starting transfers between devices  19.1 us (42%)
  waiting for transfers between devices  15.2 us (34%)
  Pallas kernels  10.6 us (23%)
    ppermute x8, starting transfers between devices, swap(): return lax.ppermute(array, 'seq', [(i, i ^ place) for i in range(seq)])  10.8 us
    ppermute x8, waiting for transfers between devices, swap(): return lax.ppermute(array, 'seq', [(i, i ^ place) for i in range(seq)])  8.75 us
    ppermute x3, waiting for transfers between devices, to_chip(): lax.ppermute(array, 'tp', [(t, (t // cores + step) % chips * cores + t %...  6.03 us
    ppermute x3, starting transfers between devices, to_chip(): lax.ppermute(array, 'tp', [(t, (t // cores + step) % chips * cores + t %...  4.68 us
    ppermute x3, starting transfers between devices, across(): lax.ppermute(array, ('seq', 'tp'), [(i * tp + t, (i ^ place) * tp + (t ^...  3.17 us
    pallas_call x2, Pallas kernels, attend_all(): pl.pallas_call(functools.partial(attend_more, first_row, cores, held, las...  1.91 us
    pallas_call x1, Pallas kernels, shards(): pl.pallas_call(functools.partial(pack, half), out_shape=[bf16(2 * rows, p...  1.59 us
    pallas_call x1, Pallas kernels, shards(): pl.pallas_call(functools.partial(attend_first, half, batches[0]), out_sha...  1.33 us
  transfers between devices with their start and end apart: 16, of which 8 were waited for; matrix products, arithmetic and copies ran while one was open for 0% of the time, Pallas kernels for 22%

profile of v4, /device:TPU:0, one launch (start us, length us, event | category | flops | bytes accessed | tf_op | source)
XLA Modules:
  0.0 45.0 jit_solution(9137576460296129805)
XLA Ops:
  0.0 0.0 copy-start.2
  0.0 0.5 %collective-permute-start.4 = (bf16[256,5120]{1,0:T(8,128)(2,1)}, bf16[256,5120]{1,0:T(8,128)(2,1)S(1)}, u32[]{:S(2)}, u32[]{:S(2)}) collective-permute-start(bf16[256,5120]{1,0:T(8,128)(2,1)} %weight.2), channel_id=1, source_target_pairs={{0,1},{1,0},{2,3},{3,2},{4,5},{5,4},{6,7},{7,6},{8,9},{9,8},{10,11... | collective-permute-start | bytes 7864328 | tf_op jit(solution)/shard_map/ppermute | solution.py:288
  0.5 1.6 %pack.1 = (bf16[512,128]{1,0:T(8,128)(2,1)S(1)}, bf16[512,128]{1,0:T(8,128)(2,1)S(1)}, bf16[256,128]{1,0:T(8,128)(2,1)S(1)}, bf16[256,128]{1,0:T(8,128)(2,1)S(1)}, bf16[256,2560]{1,0:T(8,128)(2,1)S(1)}) custom-call(bf16[256,256]{1,0:T(8,128)(2,1)} %q.1, bf16[256,256]{1,0:T(8,128)(2,1)} %k.1, bf16[256,256]{1,0:T(8,128)(2,1)} %v.1, bf16[256,5120]{1,0:T(8,128)(2,1)} %weight.2), custom_call_target="tpu_custom_call" | custom-call | flops 1600000000 | tf_op jit(solution)/shard_map/pack/pallas_call | solution.py:300
  2.1 2.6 %collective-permute-start.12 = (bf16[256,2560]{1,0:T(8,128)(2,1)S(1)}, bf16[256,2560]{1,0:T(8,128)(2,1)S(1)}, u32[]{:S(2)}, u32[]{:S(2)}) collective-permute-start(bf16[256,2560]{1,0:T(8,128)(2,1)S(1)} %get-tuple-element.45.left), channel_id=1, source_target_pairs={{0,2},{1,3},{2,0},{3,1},{4,6},{5,7},{6,4},{7,5},{8,10},{9,11},{10,... | collective-permute-start | bytes 3932168 | tf_op jit(solution)/shard_map/ppermute | solution.py:291
  4.7 1.6 %collective-permute-start = (bf16[512,128]{1,0:T(8,128)(2,1)S(1)}, bf16[512,128]{1,0:T(8,128)(2,1)S(1)}, u32[]{:S(2)}, u32[]{:S(2)}) collective-permute-start(bf16[512,128]{1,0:T(8,128)(2,1)S(1)} %get-tuple-element.31.refs_0_), channel_id=1, source_target_pairs={{0,8},{4,12},{8,0},{12,4},{16,24},{20,28},{24,16},{28,20},{1,9},{5... | collective-permute-start | bytes 393224 | tf_op jit(solution)/shard_map/ppermute | solution.py:274
  6.2 2.6 %collective-permute-start.3 = (bf16[512,128]{1,0:T(8,128)(2,1)S(1)}, bf16[512,128]{1,0:T(8,128)(2,1)S(1)}, u32[]{:S(2)}, u32[]{:S(2)}) collective-permute-start(bf16[512,128]{1,0:T(8,128)(2,1)S(1)} %get-tuple-element.33), channel_id=1, source_target_pairs={{0,16},{4,20},{8,24},{12,28},{16,0},{20,4},{24,8},{28,12},{1,17},{... | collective-permute-start | bytes 393224 | tf_op jit(solution)/shard_map/ppermute | solution.py:274
  8.8 1.5 %collective-permute-start.1 = (bf16[512,128]{1,0:T(8,128)(2,1)S(1)}, bf16[512,128]{1,0:T(8,128)(2,1)S(1)}, u32[]{:S(2)}, u32[]{:S(2)}) collective-permute-start(bf16[512,128]{1,0:T(8,128)(2,1)S(1)} %get-tuple-element.31.refs_0_), channel_id=1, source_target_pairs={{0,4},{4,0},{8,12},{12,8},{16,20},{20,16},{24,28},{28,24},{1,5},{5... | collective-permute-start | bytes 393224 | tf_op jit(solution)/shard_map/ppermute | solution.py:274
  10.3 2.4 %collective-permute-done.refs_1_ = bf16[512,128]{1,0:T(8,128)(2,1)S(1)} collective-permute-done((bf16[512,128]{1,0:T(8,128)(2,1)S(1)}, bf16[512,128]{1,0:T(8,128)(2,1)S(1)}, u32[]{:S(2)}, u32[]{:S(2)}) %collective-permute-start) | collective-permute-done | bytes 131104 | tf_op jit(solution)/shard_map/ppermute | solution.py:274
  12.7 1.5 %collective-permute-start.2 = (bf16[512,128]{1,0:T(8,128)(2,1)S(1)}, bf16[512,128]{1,0:T(8,128)(2,1)S(1)}, u32[]{:S(2)}, u32[]{:S(2)}) collective-permute-start(bf16[512,128]{1,0:T(8,128)(2,1)S(1)} %collective-permute-done.refs_1_), channel_id=1, source_target_pairs={{0,4},{4,0},{8,12},{12,8},{16,20},{20,16},{24,28},{28,24},{1,5},{5... | collective-permute-start | bytes 393224 | tf_op jit(solution)/shard_map/ppermute | solution.py:274
  14.2 1.1 %collective-permute-done.3.refs_0_.refs_4_ = bf16[512,128]{1,0:T(8,128)(2,1)S(1)} collective-permute-done((bf16[512,128]{1,0:T(8,128)(2,1)S(1)}, bf16[512,128]{1,0:T(8,128)(2,1)S(1)}, u32[]{:S(2)}, u32[]{:S(2)}) %collective-permute-start.3) | collective-permute-done | bytes 131104 | tf_op jit(solution)/shard_map/ppermute | solution.py:274
  15.3 0.0 collective-permute-done.4.refs_2_.core_weight
  15.3 1.4 %collective-permute-start.7 = (bf16[512,128]{1,0:T(8,128)(2,1)S(1)}, bf16[512,128]{1,0:T(8,128)(2,1)S(1)}, u32[]{:S(2)}, u32[]{:S(2)}) collective-permute-start(bf16[512,128]{1,0:T(8,128)(2,1)S(1)} %collective-permute-done.3.refs_0_.refs_4_), channel_id=1, source_target_pairs={{0,12},{4,8},{8,4},{12,0},{16,28},{20,24},{24,20},{28,16},{1,13},{... | collective-permute-start | bytes 393224 | tf_op jit(solution)/shard_map/ppermute | solution.py:274
  16.7 0.5 %collective-permute-start.6 = (bf16[512,128]{1,0:T(8,128)(2,1)S(1)}, bf16[512,128]{1,0:T(8,128)(2,1)S(1)}, u32[]{:S(2)}, u32[]{:S(2)}) collective-permute-start(bf16[512,128]{1,0:T(8,128)(2,1)S(1)} %collective-permute-done.3.refs_0_.refs_4_), channel_id=1, source_target_pairs={{0,4},{4,0},{8,12},{12,8},{16,20},{20,16},{24,28},{28,24},{1,5},{5... | collective-permute-start | bytes 393224 | tf_op jit(solution)/shard_map/ppermute | solution.py:274
  17.2 0.0 collective-permute-done.1.refs_2_
  17.2 1.6 %collective-permute-start.5 = (bf16[512,128]{1,0:T(8,128)(2,1)S(1)}, bf16[512,128]{1,0:T(8,128)(2,1)S(1)}, u32[]{:S(2)}, u32[]{:S(2)}) collective-permute-start(bf16[512,128]{1,0:T(8,128)(2,1)S(1)} %collective-permute-done.3.refs_0_.refs_4_), channel_id=1, source_target_pairs={{0,8},{4,12},{8,0},{12,4},{16,24},{20,28},{24,16},{28,20},{1,9},{5... | collective-permute-start | bytes 393224 | tf_op jit(solution)/shard_map/ppermute | solution.py:274
  18.8 0.9 %collective-permute-done.2.refs_3_ = bf16[512,128]{1,0:T(8,128)(2,1)S(1)} collective-permute-done((bf16[512,128]{1,0:T(8,128)(2,1)S(1)}, bf16[512,128]{1,0:T(8,128)(2,1)S(1)}, u32[]{:S(2)}, u32[]{:S(2)}) %collective-permute-start.2) | collective-permute-done | bytes 131104 | tf_op jit(solution)/shard_map/ppermute | solution.py:274
  19.7 0.2 collective-permute-start.8
  19.9 0.0 copy-done.2
  19.9 1.3 %attend_near.1 = (f32[64,128]{1,0:T(8,128)S(1)}, f32[256,128]{1,0:T(8,128)S(1)}, f32[256,128]{1,0:T(8,128)S(1)}, f32[256,128]{1,0:T(8,128)S(1)}) custom-call(s32[16,16]{1,0:T(8,128)S(1)} %copy-done.2, bf16[256,128]{1,0:T(8,128)(2,1)S(1)} %get-tuple-element.30.queries, bf16[512,128]{1,0:T(8,128)(2,1)S(1)} %get-tuple-element.31.refs_0_, ...), custom_call_target="tpu_custom_call" | custom-call | flops 1300000000 | tf_op jit(solution)/shard_map/attend_near/pallas_call | solution.py:354
  21.2 4.3 %collective-permute-done.8.queries = bf16[256,128]{1,0:T(8,128)(2,1)S(1)} collective-permute-done((bf16[256,128]{1,0:T(8,128)(2,1)S(1)}, bf16[256,128]{1,0:T(8,128)(2,1)S(1)}, u32[]{:S(2)}, u32[]{:S(2)}) %collective-permute-start.8) | collective-permute-done | bytes 65568 | tf_op jit(solution)/shard_map/ppermute | solution.py:274
  25.6 0.0 collective-permute-done.7.refs_3_.refs_7_
  25.6 0.0 collective-permute-done.6.refs_2_.refs_6_
  25.6 0.0 collective-permute-done.5.refs_1_.refs_5_
  25.6 1.1 %attend_far.1 = (bf16[128,128]{1,0:T(8,128)(2,1)S(1)}, bf16[128,128]{1,0:T(8,128)(2,1)S(1)}) custom-call(f32[64,128]{1,0:T(8,128)S(1)} %get-tuple-element.32.bias, bf16[256,128]{1,0:T(8,128)(2,1)S(1)} %collective-permute-done.8.queries, bf16[512,128]{1,0:T(8,128)(2,1)S(1)} %get-tuple-element.31.refs_0_, bf16[512,128]{1,0:T(8,128)(2,1)S(1)} %collective-permute-done.refs_1_, ...), custom_call_target="tpu_custom_call" | custom-call | flops 2000000000 | tf_op jit(solution)/shard_map/attend_far/pallas_call | solution.py:343
  26.7 1.2 %collective-permute-start.9 = (bf16[128,128]{1,0:T(8,128)(2,1)S(1)}, bf16[128,128]{1,0:T(8,128)(2,1)S(1)}, u32[]{:S(2)}, u32[]{:S(2)}) collective-permute-start(bf16[128,128]{1,0:T(8,128)(2,1)S(1)} %get-tuple-element.41), channel_id=1, source_target_pairs={{0,16},{1,17},{2,18},{3,19},{4,20},{5,21},{6,22},{7,23},{8,24},{9,... | collective-permute-start | bytes 98312 | tf_op jit(solution)/shard_map/ppermute | solution.py:277
  27.9 0.0 collective-permute-start.11
  27.9 0.8 %attend_own.1 = (bf16[128,128]{1,0:T(8,128)(2,1)S(1)}, bf16[128,128]{1,0:T(8,128)(2,1)S(1)}) custom-call(f32[64,128]{1,0:T(8,128)S(1)} %get-tuple-element.32.bias, bf16[256,128]{1,0:T(8,128)(2,1)S(1)} %get-tuple-element.30.queries, bf16[512,128]{1,0:T(8,128)(2,1)S(1)} %collective-permute-done.3.refs_0_.refs_4_, ...), custom_call_target="tpu_custom_call" | custom-call | flops 1000000000 | tf_op jit(solution)/shard_map/attend_own/pallas_call | solution.py:343
  28.7 2.0 %collective-permute-start.10 = (bf16[128,128]{1,0:T(8,128)(2,1)S(1)}, bf16[128,128]{1,0:T(8,128)(2,1)S(1)}, u32[]{:S(2)}, u32[]{:S(2)}) collective-permute-start(bf16[128,128]{1,0:T(8,128)(2,1)S(1)} %get-tuple-element.42), channel_id=1, source_target_pairs={{0,1},{1,0},{2,3},{3,2},{4,5},{5,4},{6,7},{7,6},{8,9},{9,8},{10,11... | collective-permute-start | bytes 98312 | tf_op jit(solution)/shard_map/ppermute | solution.py:277
  30.7 1.3 %stage.1.refs_1_.right = bf16[256,2560]{1,0:T(8,128)(2,1)S(1)} custom-call(bf16[256,5120]{1,0:T(8,128)(2,1)} %weight.2), custom_call_target="tpu_custom_call" | custom-call | flops 1300000000 | tf_op jit(solution)/shard_map/stage/pallas_call | solution.py:322
  32.0 0.2 collective-permute-done.9.far
  32.3 0.2 collective-permute-done.11.far_other
  32.4 0.0 collective-permute-done.10.other
  32.5 0.6 %project_peers.1 = (bf16[64,1280]{1,0:T(8,128)(2,1)S(1)}, bf16[64,1792]{1,0:T(8,128)(2,1)S(1)}) custom-call(bf16[64,512]{1,0:T(8,128)(2,1)S(1)} %get-tuple-element.46.refs_0_, bf16[256,2560]{1,0:T(8,128)(2,1)S(1)} %stage.1.refs_1_.right, bf16[256,5120]{1,0:T(8,128)(2,1)S(1)} %collective-permute-done.4.refs_2_.core_weight), custom_call_target="tpu_custom_call" | custom-call | flops 500000000 | tf_op jit(solution)/shard_map/project_peers/pallas_call | solution.py:380
  33.0 0.2 collective-permute-start.14
  33.3 1.9 %collective-permute-start.13 = (bf16[64,1792]{1,0:T(8,128)(2,1)S(1)}, bf16[64,1792]{1,0:T(8,128)(2,1)S(1)}, u32[]{:S(2)}, u32[]{:S(2)}) collective-permute-start(bf16[64,1792]{1,0:T(8,128)(2,1)S(1)} %get-tuple-element.50), channel_id=1, source_target_pairs={{0,2},{1,3},{2,0},{3,1},{4,6},{5,7},{6,4},{7,5},{8,10},{9,11},{10,... | collective-permute-start | bytes 688136 | tf_op jit(solution)/shard_map/ppermute | solution.py:291
  35.1 0.0 collective-permute-done.12.refs_1_
  35.1 0.0 copy-start
  35.1 0.0 copy-start.1
  35.1 0.0 collective-permute-start.15
  35.2 1.0 %project_own.1 = (f32[64,2560]{1,0:T(8,128)S(1)}, f32[64,2560]{1,0:T(8,128)S(1)}) custom-call(bf16[64,512]{1,0:T(8,128)(2,1)S(1)} %get-tuple-element.51.attended, bf16[256,2560]{1,0:T(8,128)(2,1)S(1)} %get-tuple-element.45.left, bf16[256,2560]{1,0:T(8,128)(2,1)S(1)} %stage.1.refs_1_.right, bf16[256,5120]{1,0:T(8,128)(2,1)S(1)} %collective-permute-done.4.refs_2_.core_weight), custom_call_target="tpu_custom_call" | custom-call | flops 100000000 | tf_op jit(solution)/shard_map/project_own/pallas_call | solution.py:390
  36.2 4.0 %collective-permute-done.14.refs_0_ = bf16[64,1280]{1,0:T(8,128)(2,1)S(1)} collective-permute-done((bf16[64,1280]{1,0:T(8,128)(2,1)S(1)}, bf16[64,1280]{1,0:T(8,128)(2,1)S(1)}, u32[]{:S(2)}, u32[]{:S(2)}) %collective-permute-start.14) | collective-permute-done | bytes 163872 | tf_op jit(solution)/shard_map/ppermute | solution.py:291
  40.2 0.0 copy-done
  40.2 0.0 copy-done.1
  40.2 0.7 %finish_head.1.refs_3_ = bf16[64,5120]{1,0:T(8,128)(2,1)} custom-call(bf16[64,5120]{1,0:T(8,128)(2,1)S(1)} %copy-done, f32[1,5120]{1,0:T(1,128)S(1)} %bitcast.1, f32[64,2560]{1,0:T(8,128)S(1)} %get-tuple-element.52.own_right.own, bf16[64,1280]{1,0:T(8,128)(2,1)S(1)} %collective-permute-done.14.refs_0_), custom_call_target="tpu_custom_call" | custom-call | flops 20000000000 | tf_op jit(solution)/shard_map/finish_head/pallas_call | solution.py:404
  40.9 0.0 collective-permute-done.15.refs_2_
  40.9 1.3 %finish_left.1.refs_1_ = bf16[64,5120]{1,0:T(8,128)(2,1)} custom-call(bf16[64,5120]{1,0:T(8,128)(2,1)S(1)} %copy-done, f32[1,5120]{1,0:T(1,128)S(1)} %bitcast.2, f32[64,2560]{1,0:T(8,128)S(1)} %get-tuple-element.53.own, bf16[64,1280]{1,0:T(8,128)(2,1)S(1)} %collective-permute-done.14.refs_0_, ...), custom_call_target="tpu_custom_call", output_to_operand_aliasing={{}: (6, {})} | custom-call | flops 1500000000 | tf_op jit(solution)/shard_map/finish_left/pallas_call | solution.py:414
  42.2 2.0 %collective-permute-done.13.refs_0_ = bf16[64,1792]{1,0:T(8,128)(2,1)S(1)} collective-permute-done((bf16[64,1792]{1,0:T(8,128)(2,1)S(1)}, bf16[64,1792]{1,0:T(8,128)(2,1)S(1)}, u32[]{:S(2)}, u32[]{:S(2)}) %collective-permute-start.13) | collective-permute-done | bytes 229408 | tf_op jit(solution)/shard_map/ppermute | solution.py:291
  44.2 0.8 %finish_right.1 = bf16[64,5120]{1,0:T(8,128)(2,1)} custom-call(bf16[64,5120]{1,0:T(8,128)(2,1)S(1)} %copy-done, f32[1,5120]{1,0:T(1,128)S(1)} %bitcast.3, f32[64,2560]{1,0:T(8,128)S(1)} %get-tuple-element.52.own_right.own, bf16[64,1792]{1,0:T(8,128)(2,1)S(1)} %collective-permute-done.13.refs_0_, ...), custom_call_target="tpu_custom_call", output_to_operand_aliasing={{}: (4, {})} | custom-call | flops 700000000 | tf_op jit(solution)/shard_map/finish_right/pallas_call | solution.py:425
  (1 shorter events, 0.0 us)
Async XLA Ops:
  0.0 19.9 %copy-start.2 = (s32[16,16]{1,0:T(8,128)S(1)}, s32[16,16]{1,0:T(8,128)}, u32[]{:S(2)}) copy-start(s32[16,16]{1,0:T(8,128)} %mask.1) | copy-start | bytes 3076
  0.0 15.3 %collective-permute-start.4 = (bf16[256,5120]{1,0:T(8,128)(2,1)}, bf16[256,5120]{1,0:T(8,128)(2,1)S(1)}, u32[]{:S(2)}, u32[]{:S(2)}) collective-permute-start(bf16[256,5120]{1,0:T(8,128)(2,1)} %weight.2), channel_id=1, source_target_pairs={{0,1},{1,0},{2,3},{3,2},{4,5},{5,4},{6,7},{7,6},{8,9},{9,8},{10,11... | collective-permute-start | bytes 7864328 | tf_op jit(solution)/shard_map/ppermute | solution.py:288
  2.1 33.1 %collective-permute-start.12 = (bf16[256,2560]{1,0:T(8,128)(2,1)S(1)}, bf16[256,2560]{1,0:T(8,128)(2,1)S(1)}, u32[]{:S(2)}, u32[]{:S(2)}) collective-permute-start(bf16[256,2560]{1,0:T(8,128)(2,1)S(1)} %get-tuple-element.45.left), channel_id=1, source_target_pairs={{0,2},{1,3},{2,0},{3,1},{4,6},{5,7},{6,4},{7,5},{8,10},{9,11},{10,... | collective-permute-start | bytes 3932168 | tf_op jit(solution)/shard_map/ppermute | solution.py:291
  4.7 8.1 %collective-permute-start = (bf16[512,128]{1,0:T(8,128)(2,1)S(1)}, bf16[512,128]{1,0:T(8,128)(2,1)S(1)}, u32[]{:S(2)}, u32[]{:S(2)}) collective-permute-start(bf16[512,128]{1,0:T(8,128)(2,1)S(1)} %get-tuple-element.31.refs_0_), channel_id=1, source_target_pairs={{0,8},{4,12},{8,0},{12,4},{16,24},{20,28},{24,16},{28,20},{1,9},{5... | collective-permute-start | bytes 393224 | tf_op jit(solution)/shard_map/ppermute | solution.py:274
  6.2 9.1 %collective-permute-start.3 = (bf16[512,128]{1,0:T(8,128)(2,1)S(1)}, bf16[512,128]{1,0:T(8,128)(2,1)S(1)}, u32[]{:S(2)}, u32[]{:S(2)}) collective-permute-start(bf16[512,128]{1,0:T(8,128)(2,1)S(1)} %get-tuple-element.33), channel_id=1, source_target_pairs={{0,16},{4,20},{8,24},{12,28},{16,0},{20,4},{24,8},{28,12},{1,17},{... | collective-permute-start | bytes 393224 | tf_op jit(solution)/shard_map/ppermute | solution.py:274
  8.8 8.4 %collective-permute-start.1 = (bf16[512,128]{1,0:T(8,128)(2,1)S(1)}, bf16[512,128]{1,0:T(8,128)(2,1)S(1)}, u32[]{:S(2)}, u32[]{:S(2)}) collective-permute-start(bf16[512,128]{1,0:T(8,128)(2,1)S(1)} %get-tuple-element.31.refs_0_), channel_id=1, source_target_pairs={{0,4},{4,0},{8,12},{12,8},{16,20},{20,16},{24,28},{28,24},{1,5},{5... | collective-permute-start | bytes 393224 | tf_op jit(solution)/shard_map/ppermute | solution.py:274
  12.7 7.0 %collective-permute-start.2 = (bf16[512,128]{1,0:T(8,128)(2,1)S(1)}, bf16[512,128]{1,0:T(8,128)(2,1)S(1)}, u32[]{:S(2)}, u32[]{:S(2)}) collective-permute-start(bf16[512,128]{1,0:T(8,128)(2,1)S(1)} %collective-permute-done.refs_1_), channel_id=1, source_target_pairs={{0,4},{4,0},{8,12},{12,8},{16,20},{20,16},{24,28},{28,24},{1,5},{5... | collective-permute-start | bytes 393224 | tf_op jit(solution)/shard_map/ppermute | solution.py:274
  15.3 10.2 %collective-permute-start.7 = (bf16[512,128]{1,0:T(8,128)(2,1)S(1)}, bf16[512,128]{1,0:T(8,128)(2,1)S(1)}, u32[]{:S(2)}, u32[]{:S(2)}) collective-permute-start(bf16[512,128]{1,0:T(8,128)(2,1)S(1)} %collective-permute-done.3.refs_0_.refs_4_), channel_id=1, source_target_pairs={{0,12},{4,8},{8,4},{12,0},{16,28},{20,24},{24,20},{28,16},{1,13},{... | collective-permute-start | bytes 393224 | tf_op jit(solution)/shard_map/ppermute | solution.py:274
  16.7 8.9 %collective-permute-start.6 = (bf16[512,128]{1,0:T(8,128)(2,1)S(1)}, bf16[512,128]{1,0:T(8,128)(2,1)S(1)}, u32[]{:S(2)}, u32[]{:S(2)}) collective-permute-start(bf16[512,128]{1,0:T(8,128)(2,1)S(1)} %collective-permute-done.3.refs_0_.refs_4_), channel_id=1, source_target_pairs={{0,4},{4,0},{8,12},{12,8},{16,20},{20,16},{24,28},{28,24},{1,5},{5... | collective-permute-start | bytes 393224 | tf_op jit(solution)/shard_map/ppermute | solution.py:274
  17.2 8.3 %collective-permute-start.5 = (bf16[512,128]{1,0:T(8,128)(2,1)S(1)}, bf16[512,128]{1,0:T(8,128)(2,1)S(1)}, u32[]{:S(2)}, u32[]{:S(2)}) collective-permute-start(bf16[512,128]{1,0:T(8,128)(2,1)S(1)} %collective-permute-done.3.refs_0_.refs_4_), channel_id=1, source_target_pairs={{0,8},{4,12},{8,0},{12,4},{16,24},{20,28},{24,16},{28,20},{1,9},{5... | collective-permute-start | bytes 393224 | tf_op jit(solution)/shard_map/ppermute | solution.py:274
  19.7 5.9 %collective-permute-start.8 = (bf16[256,128]{1,0:T(8,128)(2,1)S(1)}, bf16[256,128]{1,0:T(8,128)(2,1)S(1)}, u32[]{:S(2)}, u32[]{:S(2)}) collective-permute-start(bf16[256,128]{1,0:T(8,128)(2,1)S(1)} %get-tuple-element.40), channel_id=1, source_target_pairs={{0,16},{4,20},{8,24},{12,28},{16,0},{20,4},{24,8},{28,12},{1,17},{... | collective-permute-start | bytes 196616 | tf_op jit(solution)/shard_map/ppermute | solution.py:274
  26.7 5.6 %collective-permute-start.9 = (bf16[128,128]{1,0:T(8,128)(2,1)S(1)}, bf16[128,128]{1,0:T(8,128)(2,1)S(1)}, u32[]{:S(2)}, u32[]{:S(2)}) collective-permute-start(bf16[128,128]{1,0:T(8,128)(2,1)S(1)} %get-tuple-element.41), channel_id=1, source_target_pairs={{0,16},{1,17},{2,18},{3,19},{4,20},{5,21},{6,22},{7,23},{8,24},{9,... | collective-permute-start | bytes 98312 | tf_op jit(solution)/shard_map/ppermute | solution.py:277
  27.9 4.6 %collective-permute-start.11 = (bf16[128,128]{1,0:T(8,128)(2,1)S(1)}, bf16[128,128]{1,0:T(8,128)(2,1)S(1)}, u32[]{:S(2)}, u32[]{:S(2)}) collective-permute-start(bf16[128,128]{1,0:T(8,128)(2,1)S(1)} %get-tuple-element.43), channel_id=1, source_target_pairs={{0,17},{1,16},{2,19},{3,18},{4,21},{5,20},{6,23},{7,22},{8,25},{9,... | collective-permute-start | bytes 98312 | tf_op jit(solution)/shard_map/ppermute | solution.py:277
  28.7 3.8 %collective-permute-start.10 = (bf16[128,128]{1,0:T(8,128)(2,1)S(1)}, bf16[128,128]{1,0:T(8,128)(2,1)S(1)}, u32[]{:S(2)}, u32[]{:S(2)}) collective-permute-start(bf16[128,128]{1,0:T(8,128)(2,1)S(1)} %get-tuple-element.42), channel_id=1, source_target_pairs={{0,1},{1,0},{2,3},{3,2},{4,5},{5,4},{6,7},{7,6},{8,9},{9,8},{10,11... | collective-permute-start | bytes 98312 | tf_op jit(solution)/shard_map/ppermute | solution.py:277
  33.0 7.1 %collective-permute-start.14 = (bf16[64,1280]{1,0:T(8,128)(2,1)S(1)}, bf16[64,1280]{1,0:T(8,128)(2,1)S(1)}, u32[]{:S(2)}, u32[]{:S(2)}) collective-permute-start(bf16[64,1280]{1,0:T(8,128)(2,1)S(1)} %get-tuple-element.49), channel_id=1, source_target_pairs={{0,2},{1,3},{2,0},{3,1},{4,6},{5,7},{6,4},{7,5},{8,10},{9,11},{10,... | collective-permute-start | bytes 491528 | tf_op jit(solution)/shard_map/ppermute | solution.py:291
  33.3 11.0 %collective-permute-start.13 = (bf16[64,1792]{1,0:T(8,128)(2,1)S(1)}, bf16[64,1792]{1,0:T(8,128)(2,1)S(1)}, u32[]{:S(2)}, u32[]{:S(2)}) collective-permute-start(bf16[64,1792]{1,0:T(8,128)(2,1)S(1)} %get-tuple-element.50), channel_id=1, source_target_pairs={{0,2},{1,3},{2,0},{3,1},{4,6},{5,7},{6,4},{7,5},{8,10},{9,11},{10,... | collective-permute-start | bytes 688136 | tf_op jit(solution)/shard_map/ppermute | solution.py:291
  35.1 5.0 %copy-start = (bf16[64,5120]{1,0:T(8,128)(2,1)S(1)}, bf16[64,5120]{1,0:T(8,128)(2,1)}, u32[]{:S(2)}) copy-start(bf16[64,5120]{1,0:T(8,128)(2,1)} %residual.5) | copy-start | bytes 1966084
  35.1 5.0 %copy-start.1 = (f32[5120]{0:T(1024)S(1)}, f32[5120]{0:T(1024)}, u32[]{:S(2)}) copy-start(f32[5120]{0:T(1024)} %param.12) | copy-start | bytes 61444
  35.1 5.7 %collective-permute-start.15 = (bf16[256,2560]{1,0:T(8,128)(2,1)S(1)}, bf16[256,2560]{1,0:T(8,128)(2,1)S(1)}, u32[]{:S(2)}, u32[]{:S(2)}) collective-permute-start(bf16[256,2560]{1,0:T(8,128)(2,1)S(1)} %collective-permute-done.12.refs_1_), channel_id=1, source_target_pairs={{0,1},{1,0},{2,3},{3,2},{4,5},{5,4},{6,7},{7,6},{8,9},{9,8},{10,11... | collective-permute-start | bytes 3932168 | tf_op jit(solution)/shard_map/ppermute | solution.py:288

commit v5 on v4

--- a/solution.py
+++ b/solution.py
@@ -15,7 +15,7 @@
 SCORE_SCALE = LOG2E / HD**0.5
 BATCH = 4
 LANES = 128
-CUT_NUM, CUT_DEN = 1, 2
+CUT_NUM, CUT_DEN = 12, 25
 HEAD_NUM, HEAD_DEN = 1, 3
 
 VMEM = pltpu.MemorySpace.VMEM
@@ -159,7 +159,7 @@
     copy.wait()
 
 
-def line_up(half, cores, own, far, other, far_other, *outs):
+def line_up(half, cores, own, far_other, other, far, *outs):
     low = lax.axis_index("seq") < half
     chips = len(outs)
     chip = lax.axis_index("tp") // cores
@@ -308,7 +308,7 @@
         name="pack",
     )(*in_hbm(queries, keys, values, out_weight))
     kv_far = swap(kv_send, half)
-    order = sorted(range(1, half), key=lambda m: (m.bit_count(), -m))
+    order = sorted(range(1, half), key=lambda m: (m % 2 == 0, -m))
     direct = [m for m in order if m % 2 == 0 or m == 1]
     near = {m: swap(kv_keep, m) for m in direct}
     chip_weights = [to_chip(left, step) for step in range(1, chips)]
@@ -363,7 +363,7 @@
     near_batches = [[(m, near[m]) for m in batch] for batch in batches]
     far_batches = [[(m ^ half, far[m]) for m in batch] for batch in batches]
     both = [one + two for one, two in zip(near_batches, far_batches)]
-    far_mine, far_other = attend_all(blocks, q_far, both, [], 2)
+    far_mine, far_other = attend_all(blocks, q_far, both, [], 5)
     own_mine, own_other = attend_all(0, q_keep, near_batches[1:] + far_batches, own_state, 1)
     from_far = across(far_mine, half, 0)
     from_far_core = across(far_other, half, 1)
@@ -376,7 +376,7 @@
         compiler_params=params(16),
         cost_estimate=cost(0.1),
         name="line_up",
-    )(own_mine, from_far, from_core, from_far_core)
+    )(own_mine, from_far_core, from_core, from_far)
     sums = pl.pallas_call(
         functools.partial(project_peers, cut),
         out_shape=[bf16(share, cores * width + head), bf16(share, columns - cut - head)] * peers,

time: 45.2 us -> 44.3 us (0.980)
  waiting for transfers between devices: 15.2 us -> 14.7 us
    ppermute x8, waiting for transfers between devices: 8.75 us -> 7.39 us  [swap(): return lax.ppermute(array, 'seq', [(i, i ^ place) for i in range(seq)])]
    ppermute x3, starting transfers between devices: 4.68 us -> 3.61 us  [to_chip(): lax.ppermute(array, 'tp', [(t, (t // cores + step) % chips * cores + t %...]
    ppermute x8, starting transfers between devices: 10.8 us -> 11.9 us  [swap(): return lax.ppermute(array, 'seq', [(i, i ^ place) for i in range(seq)])]
    ppermute x3, waiting for transfers between devices: 6.03 us -> 6.54 us  [to_chip(): lax.ppermute(array, 'tp', [(t, (t // cores + step) % chips * cores + t %...]
  transfers between devices with their start and end apart: 16 -> 16, of which waited for: 8 -> 7; matrix products, arithmetic and copies ran while one was open for 0% -> 0% of each run, Pallas kernels for 22% -> 22%
where the time goes in v5:
time: 44.3 us; the launch traced here: 44.1 us
  starting transfers between devices  18.9 us (43%)
  waiting for transfers between devices  14.7 us (33%)
  Pallas kernels  10.4 us (23%)
    ppermute x8, starting transfers between devices, swap(): return lax.ppermute(array, 'seq', [(i, i ^ place) for i in range(seq)])  11.9 us
    ppermute x8, waiting for transfers between devices, swap(): return lax.ppermute(array, 'seq', [(i, i ^ place) for i in range(seq)])  7.39 us
    ppermute x3, waiting for transfers between devices, to_chip(): lax.ppermute(array, 'tp', [(t, (t // cores + step) % chips * cores + t %...  6.54 us
    ppermute x3, starting transfers between devices, to_chip(): lax.ppermute(array, 'tp', [(t, (t // cores + step) % chips * cores + t %...  3.61 us
    ppermute x3, starting transfers between devices, across(): lax.ppermute(array, ('seq', 'tp'), [(i * tp + t, (i ^ place) * tp + (t ^...  2.88 us
    pallas_call x2, Pallas kernels, attend_all(): pl.pallas_call(functools.partial(attend_more, first_row, cores, held, las...  1.91 us
    pallas_call x1, Pallas kernels, shards(): pl.pallas_call(functools.partial(pack, half), out_shape=[bf16(2 * rows, p...  1.57 us
    pallas_call x1, Pallas kernels, shards(): pl.pallas_call(stage, out_shape=bf16(width, columns - cut), in_specs=[pl....  1.35 us
  transfers between devices with their start and end apart: 16, of which 7 were waited for; matrix products, arithmetic and copies ran while one was open for 0% of the time, Pallas kernels for 22%

profile of v5, /device:TPU:0, one launch (start us, length us, event | category | flops | bytes accessed | tf_op | source)
XLA Modules:
  0.0 44.1 jit_solution(11074718129650812001)
XLA Ops:
  0.0 0.0 copy-start.2
  0.0 0.5 %collective-permute-start.4 = (bf16[256,5120]{1,0:T(8,128)(2,1)}, bf16[256,5120]{1,0:T(8,128)(2,1)S(1)}, u32[]{:S(2)}, u32[]{:S(2)}) collective-permute-start(bf16[256,5120]{1,0:T(8,128)(2,1)} %weight.2), channel_id=1, source_target_pairs={{0,1},{1,0},{2,3},{3,2},{4,5},{5,4},{6,7},{7,6},{8,9},{9,8},{10,11... | collective-permute-start | bytes 7864328 | tf_op jit(solution)/shard_map/ppermute | solution.py:288
  0.5 1.6 %pack.1 = (bf16[512,128]{1,0:T(8,128)(2,1)S(1)}, bf16[512,128]{1,0:T(8,128)(2,1)S(1)}, bf16[256,128]{1,0:T(8,128)(2,1)S(1)}, bf16[256,128]{1,0:T(8,128)(2,1)S(1)}, bf16[256,2432]{1,0:T(8,128)(2,1)S(1)}) custom-call(bf16[256,256]{1,0:T(8,128)(2,1)} %q.1, bf16[256,256]{1,0:T(8,128)(2,1)} %k.1, bf16[256,256]{1,0:T(8,128)(2,1)} %v.1, bf16[256,5120]{1,0:T(8,128)(2,1)} %weight.2), custom_call_target="tpu_custom_call" | custom-call | flops 1600000000 | tf_op jit(solution)/shard_map/pack/pallas_call | solution.py:300
  2.0 2.6 %collective-permute-start = (bf16[512,128]{1,0:T(8,128)(2,1)S(1)}, bf16[512,128]{1,0:T(8,128)(2,1)S(1)}, u32[]{:S(2)}, u32[]{:S(2)}) collective-permute-start(bf16[512,128]{1,0:T(8,128)(2,1)S(1)} %get-tuple-element.31.refs_0_), channel_id=1, source_target_pairs={{0,8},{4,12},{8,0},{12,4},{16,24},{20,28},{24,16},{28,20},{1,9},{5... | collective-permute-start | bytes 393224 | tf_op jit(solution)/shard_map/ppermute | solution.py:274
  4.7 1.5 %collective-permute-start.12 = (bf16[256,2432]{1,0:T(8,128)(2,1)S(1)}, bf16[256,2432]{1,0:T(8,128)(2,1)S(1)}, u32[]{:S(2)}, u32[]{:S(2)}) collective-permute-start(bf16[256,2432]{1,0:T(8,128)(2,1)S(1)} %get-tuple-element.45.left), channel_id=1, source_target_pairs={{0,2},{1,3},{2,0},{3,1},{4,6},{5,7},{6,4},{7,5},{8,10},{9,11},{10,... | collective-permute-start | bytes 3735560 | tf_op jit(solution)/shard_map/ppermute | solution.py:291
  6.2 2.6 %collective-permute-start.3 = (bf16[512,128]{1,0:T(8,128)(2,1)S(1)}, bf16[512,128]{1,0:T(8,128)(2,1)S(1)}, u32[]{:S(2)}, u32[]{:S(2)}) collective-permute-start(bf16[512,128]{1,0:T(8,128)(2,1)S(1)} %get-tuple-element.33), channel_id=1, source_target_pairs={{0,16},{4,20},{8,24},{12,28},{16,0},{20,4},{24,8},{28,12},{1,17},{... | collective-permute-start | bytes 393224 | tf_op jit(solution)/shard_map/ppermute | solution.py:274
  8.8 1.5 %collective-permute-start.2 = (bf16[512,128]{1,0:T(8,128)(2,1)S(1)}, bf16[512,128]{1,0:T(8,128)(2,1)S(1)}, u32[]{:S(2)}, u32[]{:S(2)}) collective-permute-start(bf16[512,128]{1,0:T(8,128)(2,1)S(1)} %get-tuple-element.31.refs_0_), channel_id=1, source_target_pairs={{0,4},{4,0},{8,12},{12,8},{16,20},{20,16},{24,28},{28,24},{1,5},{5... | collective-permute-start | bytes 393224 | tf_op jit(solution)/shard_map/ppermute | solution.py:274
  10.3 0.0 collective-permute-done.refs_3_
  10.3 0.5 %collective-permute-start.1 = (bf16[512,128]{1,0:T(8,128)(2,1)S(1)}, bf16[512,128]{1,0:T(8,128)(2,1)S(1)}, u32[]{:S(2)}, u32[]{:S(2)}) collective-permute-start(bf16[512,128]{1,0:T(8,128)(2,1)S(1)} %collective-permute-done.refs_3_), channel_id=1, source_target_pairs={{0,4},{4,0},{8,12},{12,8},{16,20},{20,16},{24,28},{28,24},{1,5},{5... | collective-permute-start | bytes 393224 | tf_op jit(solution)/shard_map/ppermute | solution.py:274
  10.8 4.4 %collective-permute-done.3.refs_0_.refs_4_ = bf16[512,128]{1,0:T(8,128)(2,1)S(1)} collective-permute-done((bf16[512,128]{1,0:T(8,128)(2,1)S(1)}, bf16[512,128]{1,0:T(8,128)(2,1)S(1)}, u32[]{:S(2)}, u32[]{:S(2)}) %collective-permute-start.3) | collective-permute-done | bytes 131104 | tf_op jit(solution)/shard_map/ppermute | solution.py:274
  15.2 0.0 collective-permute-done.4.refs_2_.core_weight
  15.3 0.0 collective-permute-start.7
  15.3 1.5 %collective-permute-start.6 = (bf16[512,128]{1,0:T(8,128)(2,1)S(1)}, bf16[512,128]{1,0:T(8,128)(2,1)S(1)}, u32[]{:S(2)}, u32[]{:S(2)}) collective-permute-start(bf16[512,128]{1,0:T(8,128)(2,1)S(1)} %collective-permute-done.3.refs_0_.refs_4_), channel_id=1, source_target_pairs={{0,4},{4,0},{8,12},{12,8},{16,20},{20,16},{24,28},{28,24},{1,5},{5... | collective-permute-start | bytes 393224 | tf_op jit(solution)/shard_map/ppermute | solution.py:274
  16.7 0.0 collective-permute-done.2.refs_2_
  16.8 2.0 %collective-permute-start.5 = (bf16[512,128]{1,0:T(8,128)(2,1)S(1)}, bf16[512,128]{1,0:T(8,128)(2,1)S(1)}, u32[]{:S(2)}, u32[]{:S(2)}) collective-permute-start(bf16[512,128]{1,0:T(8,128)(2,1)S(1)} %collective-permute-done.3.refs_0_.refs_4_), channel_id=1, source_target_pairs={{0,12},{4,8},{8,4},{12,0},{16,28},{20,24},{24,20},{28,16},{1,13},{... | collective-permute-start | bytes 393224 | tf_op jit(solution)/shard_map/ppermute | solution.py:274
  18.7 0.0 collective-permute-done.1.refs_1_
  18.8 1.2 %collective-permute-start.8 = (bf16[256,128]{1,0:T(8,128)(2,1)S(1)}, bf16[256,128]{1,0:T(8,128)(2,1)S(1)}, u32[]{:S(2)}, u32[]{:S(2)}) collective-permute-start(bf16[256,128]{1,0:T(8,128)(2,1)S(1)} %get-tuple-element.40), channel_id=1, source_target_pairs={{0,16},{4,20},{8,24},{12,28},{16,0},{20,4},{24,8},{28,12},{1,17},{... | collective-permute-start | bytes 196616 | tf_op jit(solution)/shard_map/ppermute | solution.py:274
  19.9 0.0 copy-done.2
  19.9 1.3 %attend_near.1 = (f32[64,128]{1,0:T(8,128)S(1)}, f32[256,128]{1,0:T(8,128)S(1)}, f32[256,128]{1,0:T(8,128)S(1)}, f32[256,128]{1,0:T(8,128)S(1)}) custom-call(s32[16,16]{1,0:T(8,128)S(1)} %copy-done.2, bf16[256,128]{1,0:T(8,128)(2,1)S(1)} %get-tuple-element.30.queries, bf16[512,128]{1,0:T(8,128)(2,1)S(1)} %get-tuple-element.31.refs_0_, ...), custom_call_target="tpu_custom_call" | custom-call | flops 1300000000 | tf_op jit(solution)/shard_map/attend_near/pallas_call | solution.py:354
  21.2 2.7 %collective-permute-done.8.queries = bf16[256,128]{1,0:T(8,128)(2,1)S(1)} collective-permute-done((bf16[256,128]{1,0:T(8,128)(2,1)S(1)}, bf16[256,128]{1,0:T(8,128)(2,1)S(1)}, u32[]{:S(2)}, u32[]{:S(2)}) %collective-permute-start.8) | collective-permute-done | bytes 65568 | tf_op jit(solution)/shard_map/ppermute | solution.py:274
  24.0 0.0 collective-permute-done.7.refs_3_.refs_7_
  24.0 0.0 collective-permute-done.6.refs_2_.refs_6_
  24.0 0.2 collective-permute-done.5.refs_1_.refs_5_
  24.2 1.1 %attend_far.1 = (bf16[128,128]{1,0:T(8,128)(2,1)S(1)}, bf16[128,128]{1,0:T(8,128)(2,1)S(1)}) custom-call(f32[64,128]{1,0:T(8,128)S(1)} %get-tuple-element.32.bias, bf16[256,128]{1,0:T(8,128)(2,1)S(1)} %collective-permute-done.8.queries, bf16[512,128]{1,0:T(8,128)(2,1)S(1)} %get-tuple-element.31.refs_0_, bf16[512,128]{1,0:T(8,128)(2,1)S(1)} %collective-permute-done.1.refs_1_, ...), custom_call_target="tpu_custom_call" | custom-call | flops 5000000000 | tf_op jit(solution)/shard_map/attend_far/pallas_call | solution.py:343
  25.3 0.1 collective-permute-start.9
  25.4 2.0 %collective-permute-start.11 = (bf16[128,128]{1,0:T(8,128)(2,1)S(1)}, bf16[128,128]{1,0:T(8,128)(2,1)S(1)}, u32[]{:S(2)}, u32[]{:S(2)}) collective-permute-start(bf16[128,128]{1,0:T(8,128)(2,1)S(1)} %get-tuple-element.43), channel_id=1, source_target_pairs={{0,16},{1,17},{2,18},{3,19},{4,20},{5,21},{6,22},{7,23},{8,24},{9,... | collective-permute-start | bytes 98312 | tf_op jit(solution)/shard_map/ppermute | solution.py:277
  27.4 0.8 %attend_own.1 = (bf16[128,128]{1,0:T(8,128)(2,1)S(1)}, bf16[128,128]{1,0:T(8,128)(2,1)S(1)}) custom-call(f32[64,128]{1,0:T(8,128)S(1)} %get-tuple-element.32.bias, bf16[256,128]{1,0:T(8,128)(2,1)S(1)} %get-tuple-element.30.queries, bf16[512,128]{1,0:T(8,128)(2,1)S(1)} %collective-permute-done.3.refs_0_.refs_4_, ...), custom_call_target="tpu_custom_call" | custom-call | flops 1000000000 | tf_op jit(solution)/shard_map/attend_own/pallas_call | solution.py:343
  28.2 0.8 %collective-permute-start.10 = (bf16[128,128]{1,0:T(8,128)(2,1)S(1)}, bf16[128,128]{1,0:T(8,128)(2,1)S(1)}, u32[]{:S(2)}, u32[]{:S(2)}) collective-permute-start(bf16[128,128]{1,0:T(8,128)(2,1)S(1)} %get-tuple-element.42), channel_id=1, source_target_pairs={{0,1},{1,0},{2,3},{3,2},{4,5},{5,4},{6,7},{7,6},{8,9},{9,8},{10,11... | collective-permute-start | bytes 98312 | tf_op jit(solution)/shard_map/ppermute | solution.py:277
  29.0 1.3 %stage.1.refs_1_.right = bf16[256,2688]{1,0:T(8,128)(2,1)S(1)} custom-call(bf16[256,5120]{1,0:T(8,128)(2,1)} %weight.2), custom_call_target="tpu_custom_call" | custom-call | flops 1300000000 | tf_op jit(solution)/shard_map/stage/pallas_call | solution.py:322
  30.4 0.0 collective-permute-done.9.far_other
  30.4 0.8 %collective-permute-done.11.far = bf16[128,128]{1,0:T(8,128)(2,1)S(1)} collective-permute-done((bf16[128,128]{1,0:T(8,128)(2,1)S(1)}, bf16[128,128]{1,0:T(8,128)(2,1)S(1)}, u32[]{:S(2)}, u32[]{:S(2)}) %collective-permute-start.11) | collective-permute-done | bytes 32800 | tf_op jit(solution)/shard_map/ppermute | solution.py:277
  31.2 0.0 collective-permute-done.10.other
  31.2 0.6 %project_peers.1 = (bf16[64,1408]{1,0:T(8,128)(2,1)S(1)}, bf16[64,1792]{1,0:T(8,128)(2,1)S(1)}) custom-call(bf16[64,512]{1,0:T(8,128)(2,1)S(1)} %get-tuple-element.46.refs_0_, bf16[256,2688]{1,0:T(8,128)(2,1)S(1)} %stage.1.refs_1_.right, bf16[256,5120]{1,0:T(8,128)(2,1)S(1)} %collective-permute-done.4.refs_2_.core_weight), custom_call_target="tpu_custom_call" | custom-call | flops 500000000 | tf_op jit(solution)/shard_map/project_peers/pallas_call | solution.py:380
  31.8 1.2 %collective-permute-start.14 = (bf16[64,1408]{1,0:T(8,128)(2,1)S(1)}, bf16[64,1408]{1,0:T(8,128)(2,1)S(1)}, u32[]{:S(2)}, u32[]{:S(2)}) collective-permute-start(bf16[64,1408]{1,0:T(8,128)(2,1)S(1)} %get-tuple-element.49), channel_id=1, source_target_pairs={{0,2},{1,3},{2,0},{3,1},{4,6},{5,7},{6,4},{7,5},{8,10},{9,11},{10,... | collective-permute-start | bytes 540680 | tf_op jit(solution)/shard_map/ppermute | solution.py:291
  33.0 0.9 %collective-permute-start.13 = (bf16[64,1792]{1,0:T(8,128)(2,1)S(1)}, bf16[64,1792]{1,0:T(8,128)(2,1)S(1)}, u32[]{:S(2)}, u32[]{:S(2)}) collective-permute-start(bf16[64,1792]{1,0:T(8,128)(2,1)S(1)} %get-tuple-element.50), channel_id=1, source_target_pairs={{0,2},{1,3},{2,0},{3,1},{4,6},{5,7},{6,4},{7,5},{8,10},{9,11},{10,... | collective-permute-start | bytes 688136 | tf_op jit(solution)/shard_map/ppermute | solution.py:291
  33.9 0.3 collective-permute-done.12.refs_1_
  34.2 0.0 copy-start
  34.2 0.0 copy-start.1
  34.2 0.0 collective-permute-start.15
  34.2 0.9 %project_own.1 = (f32[64,2432]{1,0:T(8,128)S(1)}, f32[64,2688]{1,0:T(8,128)S(1)}) custom-call(bf16[64,512]{1,0:T(8,128)(2,1)S(1)} %get-tuple-element.51.attended, bf16[256,2432]{1,0:T(8,128)(2,1)S(1)} %get-tuple-element.45.left, bf16[256,2688]{1,0:T(8,128)(2,1)S(1)} %stage.1.refs_1_.right, bf16[256,5120]{1,0:T(8,128)(2,1)S(1)} %collective-permute-done.4.refs_2_.core_weight), custom_call_target="tpu_custom_call" | custom-call | flops 100000000 | tf_op jit(solution)/shard_map/project_own/pallas_call | solution.py:390
  35.1 4.2 %collective-permute-done.14.refs_0_ = bf16[64,1408]{1,0:T(8,128)(2,1)S(1)} collective-permute-done((bf16[64,1408]{1,0:T(8,128)(2,1)S(1)}, bf16[64,1408]{1,0:T(8,128)(2,1)S(1)}, u32[]{:S(2)}, u32[]{:S(2)}) %collective-permute-start.14) | collective-permute-done | bytes 180256 | tf_op jit(solution)/shard_map/ppermute | solution.py:291
  39.3 0.0 copy-done
  39.3 0.0 copy-done.1
  39.3 0.7 %finish_head.1.refs_3_ = bf16[64,5120]{1,0:T(8,128)(2,1)} custom-call(bf16[64,5120]{1,0:T(8,128)(2,1)S(1)} %copy-done, f32[1,5120]{1,0:T(1,128)S(1)} %bitcast.1, f32[64,2688]{1,0:T(8,128)S(1)} %get-tuple-element.52.own_right.own, bf16[64,1408]{1,0:T(8,128)(2,1)S(1)} %collective-permute-done.14.refs_0_), custom_call_target="tpu_custom_call" | custom-call | flops 20000000000 | tf_op jit(solution)/shard_map/finish_head/pallas_call | solution.py:404
  40.0 0.0 collective-permute-done.15.refs_2_
  40.0 1.3 %finish_left.1.refs_1_ = bf16[64,5120]{1,0:T(8,128)(2,1)} custom-call(bf16[64,5120]{1,0:T(8,128)(2,1)S(1)} %copy-done, f32[1,5120]{1,0:T(1,128)S(1)} %bitcast.2, f32[64,2432]{1,0:T(8,128)S(1)} %get-tuple-element.53.own, bf16[64,1408]{1,0:T(8,128)(2,1)S(1)} %collective-permute-done.14.refs_0_, ...), custom_call_target="tpu_custom_call", output_to_operand_aliasing={{}: (6, {})} | custom-call | flops 1500000000 | tf_op jit(solution)/shard_map/finish_left/pallas_call | solution.py:414
  41.2 2.1 %collective-permute-done.13.refs_0_ = bf16[64,1792]{1,0:T(8,128)(2,1)S(1)} collective-permute-done((bf16[64,1792]{1,0:T(8,128)(2,1)S(1)}, bf16[64,1792]{1,0:T(8,128)(2,1)S(1)}, u32[]{:S(2)}, u32[]{:S(2)}) %collective-permute-start.13) | collective-permute-done | bytes 229408 | tf_op jit(solution)/shard_map/ppermute | solution.py:291
  43.3 0.8 %finish_right.1 = bf16[64,5120]{1,0:T(8,128)(2,1)} custom-call(bf16[64,5120]{1,0:T(8,128)(2,1)S(1)} %copy-done, f32[1,5120]{1,0:T(1,128)S(1)} %bitcast.3, f32[64,2688]{1,0:T(8,128)S(1)} %get-tuple-element.52.own_right.own, bf16[64,1792]{1,0:T(8,128)(2,1)S(1)} %collective-permute-done.13.refs_0_, ...), custom_call_target="tpu_custom_call", output_to_operand_aliasing={{}: (4, {})} | custom-call | flops 700000000 | tf_op jit(solution)/shard_map/finish_right/pallas_call | solution.py:425
  (1 shorter events, 0.0 us)
Async XLA Ops:
  0.0 19.9 %copy-start.2 = (s32[16,16]{1,0:T(8,128)S(1)}, s32[16,16]{1,0:T(8,128)}, u32[]{:S(2)}) copy-start(s32[16,16]{1,0:T(8,128)} %mask.1) | copy-start | bytes 3076
  0.0 15.2 %collective-permute-start.4 = (bf16[256,5120]{1,0:T(8,128)(2,1)}, bf16[256,5120]{1,0:T(8,128)(2,1)S(1)}, u32[]{:S(2)}, u32[]{:S(2)}) collective-permute-start(bf16[256,5120]{1,0:T(8,128)(2,1)} %weight.2), channel_id=1, source_target_pairs={{0,1},{1,0},{2,3},{3,2},{4,5},{5,4},{6,7},{7,6},{8,9},{9,8},{10,11... | collective-permute-start | bytes 7864328 | tf_op jit(solution)/shard_map/ppermute | solution.py:288
  2.0 8.3 %collective-permute-start = (bf16[512,128]{1,0:T(8,128)(2,1)S(1)}, bf16[512,128]{1,0:T(8,128)(2,1)S(1)}, u32[]{:S(2)}, u32[]{:S(2)}) collective-permute-start(bf16[512,128]{1,0:T(8,128)(2,1)S(1)} %get-tuple-element.31.refs_0_), channel_id=1, source_target_pairs={{0,8},{4,12},{8,0},{12,4},{16,24},{20,28},{24,16},{28,20},{1,9},{5... | collective-permute-start | bytes 393224 | tf_op jit(solution)/shard_map/ppermute | solution.py:274
  4.7 29.5 %collective-permute-start.12 = (bf16[256,2432]{1,0:T(8,128)(2,1)S(1)}, bf16[256,2432]{1,0:T(8,128)(2,1)S(1)}, u32[]{:S(2)}, u32[]{:S(2)}) collective-permute-start(bf16[256,2432]{1,0:T(8,128)(2,1)S(1)} %get-tuple-element.45.left), channel_id=1, source_target_pairs={{0,2},{1,3},{2,0},{3,1},{4,6},{5,7},{6,4},{7,5},{8,10},{9,11},{10,... | collective-permute-start | bytes 3735560 | tf_op jit(solution)/shard_map/ppermute | solution.py:291
  6.2 9.0 %collective-permute-start.3 = (bf16[512,128]{1,0:T(8,128)(2,1)S(1)}, bf16[512,128]{1,0:T(8,128)(2,1)S(1)}, u32[]{:S(2)}, u32[]{:S(2)}) collective-permute-start(bf16[512,128]{1,0:T(8,128)(2,1)S(1)} %get-tuple-element.33), channel_id=1, source_target_pairs={{0,16},{4,20},{8,24},{12,28},{16,0},{20,4},{24,8},{28,12},{1,17},{... | collective-permute-start | bytes 393224 | tf_op jit(solution)/shard_map/ppermute | solution.py:274
  8.8 8.0 %collective-permute-start.2 = (bf16[512,128]{1,0:T(8,128)(2,1)S(1)}, bf16[512,128]{1,0:T(8,128)(2,1)S(1)}, u32[]{:S(2)}, u32[]{:S(2)}) collective-permute-start(bf16[512,128]{1,0:T(8,128)(2,1)S(1)} %get-tuple-element.31.refs_0_), channel_id=1, source_target_pairs={{0,4},{4,0},{8,12},{12,8},{16,20},{20,16},{24,28},{28,24},{1,5},{5... | collective-permute-start | bytes 393224 | tf_op jit(solution)/shard_map/ppermute | solution.py:274
  10.3 8.5 %collective-permute-start.1 = (bf16[512,128]{1,0:T(8,128)(2,1)S(1)}, bf16[512,128]{1,0:T(8,128)(2,1)S(1)}, u32[]{:S(2)}, u32[]{:S(2)}) collective-permute-start(bf16[512,128]{1,0:T(8,128)(2,1)S(1)} %collective-permute-done.refs_3_), channel_id=1, source_target_pairs={{0,4},{4,0},{8,12},{12,8},{16,20},{20,16},{24,28},{28,24},{1,5},{5... | collective-permute-start | bytes 393224 | tf_op jit(solution)/shard_map/ppermute | solution.py:274
  15.3 8.7 %collective-permute-start.7 = (bf16[512,128]{1,0:T(8,128)(2,1)S(1)}, bf16[512,128]{1,0:T(8,128)(2,1)S(1)}, u32[]{:S(2)}, u32[]{:S(2)}) collective-permute-start(bf16[512,128]{1,0:T(8,128)(2,1)S(1)} %collective-permute-done.3.refs_0_.refs_4_), channel_id=1, source_target_pairs={{0,8},{4,12},{8,0},{12,4},{16,24},{20,28},{24,16},{28,20},{1,9},{5... | collective-permute-start | bytes 393224 | tf_op jit(solution)/shard_map/ppermute | solution.py:274
  15.3 8.7 %collective-permute-start.6 = (bf16[512,128]{1,0:T(8,128)(2,1)S(1)}, bf16[512,128]{1,0:T(8,128)(2,1)S(1)}, u32[]{:S(2)}, u32[]{:S(2)}) collective-permute-start(bf16[512,128]{1,0:T(8,128)(2,1)S(1)} %collective-permute-done.3.refs_0_.refs_4_), channel_id=1, source_target_pairs={{0,4},{4,0},{8,12},{12,8},{16,20},{20,16},{24,28},{28,24},{1,5},{5... | collective-permute-start | bytes 393224 | tf_op jit(solution)/shard_map/ppermute | solution.py:274
  16.8 7.4 %collective-permute-start.5 = (bf16[512,128]{1,0:T(8,128)(2,1)S(1)}, bf16[512,128]{1,0:T(8,128)(2,1)S(1)}, u32[]{:S(2)}, u32[]{:S(2)}) collective-permute-start(bf16[512,128]{1,0:T(8,128)(2,1)S(1)} %collective-permute-done.3.refs_0_.refs_4_), channel_id=1, source_target_pairs={{0,12},{4,8},{8,4},{12,0},{16,28},{20,24},{24,20},{28,16},{1,13},{... | collective-permute-start | bytes 393224 | tf_op jit(solution)/shard_map/ppermute | solution.py:274
  18.8 5.2 %collective-permute-start.8 = (bf16[256,128]{1,0:T(8,128)(2,1)S(1)}, bf16[256,128]{1,0:T(8,128)(2,1)S(1)}, u32[]{:S(2)}, u32[]{:S(2)}) collective-permute-start(bf16[256,128]{1,0:T(8,128)(2,1)S(1)} %get-tuple-element.40), channel_id=1, source_target_pairs={{0,16},{4,20},{8,24},{12,28},{16,0},{20,4},{24,8},{28,12},{1,17},{... | collective-permute-start | bytes 196616 | tf_op jit(solution)/shard_map/ppermute | solution.py:274
  25.3 5.1 %collective-permute-start.9 = (bf16[128,128]{1,0:T(8,128)(2,1)S(1)}, bf16[128,128]{1,0:T(8,128)(2,1)S(1)}, u32[]{:S(2)}, u32[]{:S(2)}) collective-permute-start(bf16[128,128]{1,0:T(8,128)(2,1)S(1)} %get-tuple-element.41), channel_id=1, source_target_pairs={{0,17},{1,16},{2,19},{3,18},{4,21},{5,20},{6,23},{7,22},{8,25},{9,... | collective-permute-start | bytes 98312 | tf_op jit(solution)/shard_map/ppermute | solution.py:277
  25.4 5.8 %collective-permute-start.11 = (bf16[128,128]{1,0:T(8,128)(2,1)S(1)}, bf16[128,128]{1,0:T(8,128)(2,1)S(1)}, u32[]{:S(2)}, u32[]{:S(2)}) collective-permute-start(bf16[128,128]{1,0:T(8,128)(2,1)S(1)} %get-tuple-element.43), channel_id=1, source_target_pairs={{0,16},{1,17},{2,18},{3,19},{4,20},{5,21},{6,22},{7,23},{8,24},{9,... | collective-permute-start | bytes 98312 | tf_op jit(solution)/shard_map/ppermute | solution.py:277
  28.2 3.0 %collective-permute-start.10 = (bf16[128,128]{1,0:T(8,128)(2,1)S(1)}, bf16[128,128]{1,0:T(8,128)(2,1)S(1)}, u32[]{:S(2)}, u32[]{:S(2)}) collective-permute-start(bf16[128,128]{1,0:T(8,128)(2,1)S(1)} %get-tuple-element.42), channel_id=1, source_target_pairs={{0,1},{1,0},{2,3},{3,2},{4,5},{5,4},{6,7},{7,6},{8,9},{9,8},{10,11... | collective-permute-start | bytes 98312 | tf_op jit(solution)/shard_map/ppermute | solution.py:277
  31.8 7.5 %collective-permute-start.14 = (bf16[64,1408]{1,0:T(8,128)(2,1)S(1)}, bf16[64,1408]{1,0:T(8,128)(2,1)S(1)}, u32[]{:S(2)}, u32[]{:S(2)}) collective-permute-start(bf16[64,1408]{1,0:T(8,128)(2,1)S(1)} %get-tuple-element.49), channel_id=1, source_target_pairs={{0,2},{1,3},{2,0},{3,1},{4,6},{5,7},{6,4},{7,5},{8,10},{9,11},{10,... | collective-permute-start | bytes 540680 | tf_op jit(solution)/shard_map/ppermute | solution.py:291
  33.0 10.4 %collective-permute-start.13 = (bf16[64,1792]{1,0:T(8,128)(2,1)S(1)}, bf16[64,1792]{1,0:T(8,128)(2,1)S(1)}, u32[]{:S(2)}, u32[]{:S(2)}) collective-permute-start(bf16[64,1792]{1,0:T(8,128)(2,1)S(1)} %get-tuple-element.50), channel_id=1, source_target_pairs={{0,2},{1,3},{2,0},{3,1},{4,6},{5,7},{6,4},{7,5},{8,10},{9,11},{10,... | collective-permute-start | bytes 688136 | tf_op jit(solution)/shard_map/ppermute | solution.py:291
  34.2 5.1 %copy-start = (bf16[64,5120]{1,0:T(8,128)(2,1)S(1)}, bf16[64,5120]{1,0:T(8,128)(2,1)}, u32[]{:S(2)}) copy-start(bf16[64,5120]{1,0:T(8,128)(2,1)} %residual.5) | copy-start | bytes 1966084
  34.2 5.1 %copy-start.1 = (f32[5120]{0:T(1024)S(1)}, f32[5120]{0:T(1024)}, u32[]{:S(2)}) copy-start(f32[5120]{0:T(1024)} %param.12) | copy-start | bytes 61444
  34.2 5.8 %collective-permute-start.15 = (bf16[256,2432]{1,0:T(8,128)(2,1)S(1)}, bf16[256,2432]{1,0:T(8,128)(2,1)S(1)}, u32[]{:S(2)}, u32[]{:S(2)}) collective-permute-start(bf16[256,2432]{1,0:T(8,128)(2,1)S(1)} %collective-permute-done.12.refs_1_), channel_id=1, source_target_pairs={{0,1},{1,0},{2,3},{3,2},{4,5},{5,4},{6,7},{7,6},{8,9},{9,8},{10,11... | collective-permute-start | bytes 3735560 | tf_op jit(solution)/shard_map/ppermute | solution.py:288

commit v6 on v5

--- a/solution.py
+++ b/solution.py
@@ -181,21 +181,25 @@
     return dot(attended[:, :rows], weight[...]) + dot(attended[:, rows:], core_weight[:, cut])
 
 
-def project_peers(cut, *refs):
-    peers = (len(refs) - 2) // 3
+def project_heads(cut, *refs):
+    peers = (len(refs) - 2) // 2
     right, core_weight = refs[peers : peers + 2]
-    outs = refs[peers + 2 :]
-    for n, attended in enumerate(refs[:peers]):
-        first, second = outs[2 * n : 2 * n + 2]
+    for attended, out in zip(refs[:peers], refs[peers + 2 :]):
         rows = attended.shape[1]
-        head = first.shape[1] - rows
-        first[:, :rows] = attended[...]
-        first[:, rows:] = project(
+        head = out.shape[1] - rows
+        out[:, :rows] = attended[...]
+        out[:, rows:] = project(
             attended, right.at[:, :head], core_weight, slice(cut, cut + head)
         ).astype(jnp.bfloat16)
-        second[...] = project(
-            attended, right.at[:, head:], core_weight, slice(cut + head, None)
-        ).astype(jnp.bfloat16)
+
+
+def project_tails(*refs):
+    peers = (len(refs) - 2) // 2
+    right, core_weight = refs[peers : peers + 2]
+    for attended, out in zip(refs[:peers], refs[peers + 2 :]):
+        start = right.shape[1] - out.shape[1]
+        columns = slice(core_weight.shape[1] - out.shape[1], None)
+        out[...] = project(attended, right.at[:, start:], core_weight, columns).astype(jnp.bfloat16)
 
 
 def project_own(cut, attended, left, right, core_weight, out_left, out_right):
@@ -377,15 +381,25 @@
         cost_estimate=cost(0.1),
         name="line_up",
     )(own_mine, from_far_core, from_core, from_far)
-    sums = pl.pallas_call(
-        functools.partial(project_peers, cut),
-        out_shape=[bf16(share, cores * width + head), bf16(share, columns - cut - head)] * peers,
+    heads = pl.pallas_call(
+        functools.partial(project_heads, cut),
+        out_shape=[bf16(share, cores * width + head)] * peers,
         in_specs=in_vmem(peers + 2),
-        out_specs=in_vmem(2 * peers),
+        out_specs=in_vmem(peers),
         compiler_params=params(32),
-        cost_estimate=cost(0.5),
-        name="project_peers",
+        cost_estimate=cost(0.3),
+        name="project_heads",
     )(*lined[1:], right, core_weight)
+    tails = pl.pallas_call(
+        project_tails,
+        out_shape=[bf16(share, columns - cut - head)] * peers,
+        in_specs=in_vmem(peers + 2),
+        out_specs=in_vmem(peers),
+        compiler_params=params(32),
+        cost_estimate=cost(0.4),
+        name="project_tails",
+    )(*lined[1:], right, core_weight)
+    sums = [*heads, *tails]
     mine, chip_weights, *_ = lax.optimization_barrier((lined[0], chip_weights, *sums))
     own_left, own_right = pl.pallas_call(
         functools.partial(project_own, cut),
@@ -396,8 +410,8 @@
         cost_estimate=cost(0.1),
         name="project_own",
     )(mine, left, right, core_weight)
-    firsts = [to_chip(array, step) for step, array in enumerate(sums[::2], 1)]
-    seconds = [to_chip(array, step) for step, array in enumerate(sums[1::2], 1)]
+    firsts = [to_chip(array, step) for step, array in enumerate(heads, 1)]
+    seconds = [to_chip(array, step) for step, array in enumerate(tails, 1)]
     chip_core_weights = [swap_cores(weight) for weight in chip_weights]
     gate = gate[None, :]
     anywhere = pl.BlockSpec(memory_space=pl.ANY)

time: 44.3 us -> 44 us (level)
  waiting for transfers between devices: 14.7 us -> 14.2 us
    ppermute x3, waiting for transfers between devices: 6.54 us -> 6.04 us  [to_chip(): lax.ppermute(array, 'tp', [(t, (t // cores + step) % chips * cores + t %...]
where the time goes in v6:
time: 44 us; the launch traced here: 43.8 us
  starting transfers between devices  18.9 us (43%)
  waiting for transfers between devices  14.2 us (32%)
  Pallas kernels  10.5 us (24%)
    ppermute x8, starting transfers between devices, swap(): return lax.ppermute(array, 'seq', [(i, i ^ place) for i in range(seq)])  11.9 us
    ppermute x8, waiting for transfers between devices, swap(): return lax.ppermute(array, 'seq', [(i, i ^ place) for i in range(seq)])  7.39 us
    ppermute x3, waiting for transfers between devices, to_chip(): lax.ppermute(array, 'tp', [(t, (t // cores + step) % chips * cores + t %...  6.04 us
    ppermute x3, starting transfers between devices, to_chip(): lax.ppermute(array, 'tp', [(t, (t // cores + step) % chips * cores + t %...  3.68 us
    ppermute x3, starting transfers between devices, across(): lax.ppermute(array, ('seq', 'tp'), [(i * tp + t, (i ^ place) * tp + (t ^...  2.88 us
    pallas_call x2, Pallas kernels, attend_all(): pl.pallas_call(functools.partial(attend_more, first_row, cores, held, las...  1.91 us
    pallas_call x1, Pallas kernels, shards(): pl.pallas_call(functools.partial(pack, half), out_shape=[bf16(2 * rows, p...  1.57 us
    pallas_call x1, Pallas kernels, shards(): pl.pallas_call(stage, out_shape=bf16(width, columns - cut), in_specs=[pl....  1.35 us
  transfers between devices with their start and end apart: 16, of which 7 were waited for; matrix products, arithmetic and copies ran while one was open for 0% of the time, Pallas kernels for 22%

profile of v6, /device:TPU:0, one launch (start us, length us, event | category | flops | bytes accessed | tf_op | source)
XLA Modules:
  0.0 43.8 jit_solution(13550317687652558141)
XLA Ops:
  0.0 0.0 copy-start.2
  0.0 0.5 %collective-permute-start.4 = (bf16[256,5120]{1,0:T(8,128)(2,1)}, bf16[256,5120]{1,0:T(8,128)(2,1)S(1)}, u32[]{:S(2)}, u32[]{:S(2)}) collective-permute-start(bf16[256,5120]{1,0:T(8,128)(2,1)} %weight.2), channel_id=1, source_target_pairs={{0,1},{1,0},{2,3},{3,2},{4,5},{5,4},{6,7},{7,6},{8,9},{9,8},{10,11... | collective-permute-start | bytes 7864328 | tf_op jit(solution)/shard_map/ppermute | solution.py:292
  0.5 1.6 %pack.1 = (bf16[512,128]{1,0:T(8,128)(2,1)S(1)}, bf16[512,128]{1,0:T(8,128)(2,1)S(1)}, bf16[256,128]{1,0:T(8,128)(2,1)S(1)}, bf16[256,128]{1,0:T(8,128)(2,1)S(1)}, bf16[256,2432]{1,0:T(8,128)(2,1)S(1)}) custom-call(bf16[256,256]{1,0:T(8,128)(2,1)} %q.1, bf16[256,256]{1,0:T(8,128)(2,1)} %k.1, bf16[256,256]{1,0:T(8,128)(2,1)} %v.1, bf16[256,5120]{1,0:T(8,128)(2,1)} %weight.2), custom_call_target="tpu_custom_call" | custom-call | flops 1600000000 | tf_op jit(solution)/shard_map/pack/pallas_call | solution.py:304
  2.0 2.6 %collective-permute-start = (bf16[512,128]{1,0:T(8,128)(2,1)S(1)}, bf16[512,128]{1,0:T(8,128)(2,1)S(1)}, u32[]{:S(2)}, u32[]{:S(2)}) collective-permute-start(bf16[512,128]{1,0:T(8,128)(2,1)S(1)} %get-tuple-element.29.refs_0_), channel_id=1, source_target_pairs={{0,8},{4,12},{8,0},{12,4},{16,24},{20,28},{24,16},{28,20},{1,9},{5... | collective-permute-start | bytes 393224 | tf_op jit(solution)/shard_map/ppermute | solution.py:278
  4.7 1.5 %collective-permute-start.12 = (bf16[256,2432]{1,0:T(8,128)(2,1)S(1)}, bf16[256,2432]{1,0:T(8,128)(2,1)S(1)}, u32[]{:S(2)}, u32[]{:S(2)}) collective-permute-start(bf16[256,2432]{1,0:T(8,128)(2,1)S(1)} %get-tuple-element.43.left), channel_id=1, source_target_pairs={{0,2},{1,3},{2,0},{3,1},{4,6},{5,7},{6,4},{7,5},{8,10},{9,11},{10,... | collective-permute-start | bytes 3735560 | tf_op jit(solution)/shard_map/ppermute | solution.py:295
  6.2 2.6 %collective-permute-start.3 = (bf16[512,128]{1,0:T(8,128)(2,1)S(1)}, bf16[512,128]{1,0:T(8,128)(2,1)S(1)}, u32[]{:S(2)}, u32[]{:S(2)}) collective-permute-start(bf16[512,128]{1,0:T(8,128)(2,1)S(1)} %get-tuple-element.31), channel_id=1, source_target_pairs={{0,16},{4,20},{8,24},{12,28},{16,0},{20,4},{24,8},{28,12},{1,17},{... | collective-permute-start | bytes 393224 | tf_op jit(solution)/shard_map/ppermute | solution.py:278
  8.8 1.5 %collective-permute-start.2 = (bf16[512,128]{1,0:T(8,128)(2,1)S(1)}, bf16[512,128]{1,0:T(8,128)(2,1)S(1)}, u32[]{:S(2)}, u32[]{:S(2)}) collective-permute-start(bf16[512,128]{1,0:T(8,128)(2,1)S(1)} %get-tuple-element.29.refs_0_), channel_id=1, source_target_pairs={{0,4},{4,0},{8,12},{12,8},{16,20},{20,16},{24,28},{28,24},{1,5},{5... | collective-permute-start | bytes 393224 | tf_op jit(solution)/shard_map/ppermute | solution.py:278
  10.3 0.0 collective-permute-done.refs_3_
  10.3 0.5 %collective-permute-start.1 = (bf16[512,128]{1,0:T(8,128)(2,1)S(1)}, bf16[512,128]{1,0:T(8,128)(2,1)S(1)}, u32[]{:S(2)}, u32[]{:S(2)}) collective-permute-start(bf16[512,128]{1,0:T(8,128)(2,1)S(1)} %collective-permute-done.refs_3_), channel_id=1, source_target_pairs={{0,4},{4,0},{8,12},{12,8},{16,20},{20,16},{24,28},{28,24},{1,5},{5... | collective-permute-start | bytes 393224 | tf_op jit(solution)/shard_map/ppermute | solution.py:278
  10.8 4.4 %collective-permute-done.3.refs_0_.refs_4_ = bf16[512,128]{1,0:T(8,128)(2,1)S(1)} collective-permute-done((bf16[512,128]{1,0:T(8,128)(2,1)S(1)}, bf16[512,128]{1,0:T(8,128)(2,1)S(1)}, u32[]{:S(2)}, u32[]{:S(2)}) %collective-permute-start.3) | collective-permute-done | bytes 131104 | tf_op jit(solution)/shard_map/ppermute | solution.py:278
  15.2 0.0 collective-permute-done.4.refs_2_.core_weight
  15.3 0.0 collective-permute-start.7
  15.3 1.5 %collective-permute-start.6 = (bf16[512,128]{1,0:T(8,128)(2,1)S(1)}, bf16[512,128]{1,0:T(8,128)(2,1)S(1)}, u32[]{:S(2)}, u32[]{:S(2)}) collective-permute-start(bf16[512,128]{1,0:T(8,128)(2,1)S(1)} %collective-permute-done.3.refs_0_.refs_4_), channel_id=1, source_target_pairs={{0,4},{4,0},{8,12},{12,8},{16,20},{20,16},{24,28},{28,24},{1,5},{5... | collective-permute-start | bytes 393224 | tf_op jit(solution)/shard_map/ppermute | solution.py:278
  16.7 0.0 collective-permute-done.2.refs_2_
  16.8 2.0 %collective-permute-start.5 = (bf16[512,128]{1,0:T(8,128)(2,1)S(1)}, bf16[512,128]{1,0:T(8,128)(2,1)S(1)}, u32[]{:S(2)}, u32[]{:S(2)}) collective-permute-start(bf16[512,128]{1,0:T(8,128)(2,1)S(1)} %collective-permute-done.3.refs_0_.refs_4_), channel_id=1, source_target_pairs={{0,12},{4,8},{8,4},{12,0},{16,28},{20,24},{24,20},{28,16},{1,13},{... | collective-permute-start | bytes 393224 | tf_op jit(solution)/shard_map/ppermute | solution.py:278
  18.7 0.0 collective-permute-done.1.refs_1_
  18.8 1.2 %collective-permute-start.8 = (bf16[256,128]{1,0:T(8,128)(2,1)S(1)}, bf16[256,128]{1,0:T(8,128)(2,1)S(1)}, u32[]{:S(2)}, u32[]{:S(2)}) collective-permute-start(bf16[256,128]{1,0:T(8,128)(2,1)S(1)} %get-tuple-element.38), channel_id=1, source_target_pairs={{0,16},{4,20},{8,24},{12,28},{16,0},{20,4},{24,8},{28,12},{1,17},{... | collective-permute-start | bytes 196616 | tf_op jit(solution)/shard_map/ppermute | solution.py:278
  19.9 0.0 copy-done.2
  19.9 1.3 %attend_near.1 = (f32[64,128]{1,0:T(8,128)S(1)}, f32[256,128]{1,0:T(8,128)S(1)}, f32[256,128]{1,0:T(8,128)S(1)}, f32[256,128]{1,0:T(8,128)S(1)}) custom-call(s32[16,16]{1,0:T(8,128)S(1)} %copy-done.2, bf16[256,128]{1,0:T(8,128)(2,1)S(1)} %get-tuple-element.28.queries, bf16[512,128]{1,0:T(8,128)(2,1)S(1)} %get-tuple-element.29.refs_0_, ...), custom_call_target="tpu_custom_call" | custom-call | flops 1300000000 | tf_op jit(solution)/shard_map/attend_near/pallas_call | solution.py:358
  21.2 2.7 %collective-permute-done.8.queries = bf16[256,128]{1,0:T(8,128)(2,1)S(1)} collective-permute-done((bf16[256,128]{1,0:T(8,128)(2,1)S(1)}, bf16[256,128]{1,0:T(8,128)(2,1)S(1)}, u32[]{:S(2)}, u32[]{:S(2)}) %collective-permute-start.8) | collective-permute-done | bytes 65568 | tf_op jit(solution)/shard_map/ppermute | solution.py:278
  24.0 0.0 collective-permute-done.7.refs_3_.refs_7_
  24.0 0.0 collective-permute-done.6.refs_2_.refs_6_
  24.0 0.2 collective-permute-done.5.refs_1_.refs_5_
  24.2 1.1 %attend_far.1 = (bf16[128,128]{1,0:T(8,128)(2,1)S(1)}, bf16[128,128]{1,0:T(8,128)(2,1)S(1)}) custom-call(f32[64,128]{1,0:T(8,128)S(1)} %get-tuple-element.30.bias, bf16[256,128]{1,0:T(8,128)(2,1)S(1)} %collective-permute-done.8.queries, bf16[512,128]{1,0:T(8,128)(2,1)S(1)} %get-tuple-element.29.refs_0_, bf16[512,128]{1,0:T(8,128)(2,1)S(1)} %collective-permute-done.1.refs_1_, ...), custom_call_target="tpu_custom_call" | custom-call | flops 5000000000 | tf_op jit(solution)/shard_map/attend_far/pallas_call | solution.py:347
  25.3 0.1 collective-permute-start.9
  25.4 2.0 %collective-permute-start.11 = (bf16[128,128]{1,0:T(8,128)(2,1)S(1)}, bf16[128,128]{1,0:T(8,128)(2,1)S(1)}, u32[]{:S(2)}, u32[]{:S(2)}) collective-permute-start(bf16[128,128]{1,0:T(8,128)(2,1)S(1)} %get-tuple-element.41), channel_id=1, source_target_pairs={{0,16},{1,17},{2,18},{3,19},{4,20},{5,21},{6,22},{7,23},{8,24},{9,... | collective-permute-start | bytes 98312 | tf_op jit(solution)/shard_map/ppermute | solution.py:281
  27.4 0.8 %attend_own.1 = (bf16[128,128]{1,0:T(8,128)(2,1)S(1)}, bf16[128,128]{1,0:T(8,128)(2,1)S(1)}) custom-call(f32[64,128]{1,0:T(8,128)S(1)} %get-tuple-element.30.bias, bf16[256,128]{1,0:T(8,128)(2,1)S(1)} %get-tuple-element.28.queries, bf16[512,128]{1,0:T(8,128)(2,1)S(1)} %collective-permute-done.3.refs_0_.refs_4_, ...), custom_call_target="tpu_custom_call" | custom-call | flops 1000000000 | tf_op jit(solution)/shard_map/attend_own/pallas_call | solution.py:347
  28.2 0.8 %collective-permute-start.10 = (bf16[128,128]{1,0:T(8,128)(2,1)S(1)}, bf16[128,128]{1,0:T(8,128)(2,1)S(1)}, u32[]{:S(2)}, u32[]{:S(2)}) collective-permute-start(bf16[128,128]{1,0:T(8,128)(2,1)S(1)} %get-tuple-element.40), channel_id=1, source_target_pairs={{0,1},{1,0},{2,3},{3,2},{4,5},{5,4},{6,7},{7,6},{8,9},{9,8},{10,11... | collective-permute-start | bytes 98312 | tf_op jit(solution)/shard_map/ppermute | solution.py:281
  29.0 1.3 %stage.1.refs_1_.right = bf16[256,2688]{1,0:T(8,128)(2,1)S(1)} custom-call(bf16[256,5120]{1,0:T(8,128)(2,1)} %weight.2), custom_call_target="tpu_custom_call" | custom-call | flops 1300000000 | tf_op jit(solution)/shard_map/stage/pallas_call | solution.py:326
  30.4 0.0 collective-permute-done.9.far_other
  30.4 0.8 %collective-permute-done.11.far = bf16[128,128]{1,0:T(8,128)(2,1)S(1)} collective-permute-done((bf16[128,128]{1,0:T(8,128)(2,1)S(1)}, bf16[128,128]{1,0:T(8,128)(2,1)S(1)}, u32[]{:S(2)}, u32[]{:S(2)}) %collective-permute-start.11) | collective-permute-done | bytes 32800 | tf_op jit(solution)/shard_map/ppermute | solution.py:281
  31.2 0.0 collective-permute-done.10.other
  31.2 0.3 project_heads.1
  31.5 1.2 %collective-permute-start.14 = (bf16[64,1408]{1,0:T(8,128)(2,1)S(1)}, bf16[64,1408]{1,0:T(8,128)(2,1)S(1)}, u32[]{:S(2)}, u32[]{:S(2)}) collective-permute-start(bf16[64,1408]{1,0:T(8,128)(2,1)S(1)} %project_heads.1), channel_id=1, source_target_pairs={{0,2},{1,3},{2,0},{3,1},{4,6},{5,7},{6,4},{7,5},{8,10},{9,11},{10,... | collective-permute-start | bytes 540680 | tf_op jit(solution)/shard_map/ppermute | solution.py:295
  32.6 0.4 project_tails.1
  33.1 1.0 %collective-permute-start.13 = (bf16[64,1792]{1,0:T(8,128)(2,1)S(1)}, bf16[64,1792]{1,0:T(8,128)(2,1)S(1)}, u32[]{:S(2)}, u32[]{:S(2)}) collective-permute-start(bf16[64,1792]{1,0:T(8,128)(2,1)S(1)} %project_tails.1), channel_id=1, source_target_pairs={{0,2},{1,3},{2,0},{3,1},{4,6},{5,7},{6,4},{7,5},{8,10},{9,11},{10,... | collective-permute-start | bytes 688136 | tf_op jit(solution)/shard_map/ppermute | solution.py:295
  34.1 0.1 collective-permute-done.12.refs_1_
  34.2 0.0 copy-start
  34.2 0.0 collective-permute-start.15
  34.2 0.9 %project_own.1 = (f32[64,2432]{1,0:T(8,128)S(1)}, f32[64,2688]{1,0:T(8,128)S(1)}) custom-call(bf16[64,512]{1,0:T(8,128)(2,1)S(1)} %get-tuple-element.47.attended, bf16[256,2432]{1,0:T(8,128)(2,1)S(1)} %get-tuple-element.43.left, bf16[256,2688]{1,0:T(8,128)(2,1)S(1)} %stage.1.refs_1_.right, bf16[256,5120]{1,0:T(8,128)(2,1)S(1)} %collective-permute-done.4.refs_2_.core_weight), custom_call_target="tpu_custom_call" | custom-call | flops 100000000 | tf_op jit(solution)/shard_map/project_own/pallas_call | solution.py:404
  35.1 3.8 %collective-permute-done.14.refs_0_ = bf16[64,1408]{1,0:T(8,128)(2,1)S(1)} collective-permute-done((bf16[64,1408]{1,0:T(8,128)(2,1)S(1)}, bf16[64,1408]{1,0:T(8,128)(2,1)S(1)}, u32[]{:S(2)}, u32[]{:S(2)}) %collective-permute-start.14) | collective-permute-done | bytes 180256 | tf_op jit(solution)/shard_map/ppermute | solution.py:295
  38.9 0.0 copy-done
  38.9 0.0 copy-done.1
  38.9 0.7 %finish_head.1.refs_3_ = bf16[64,5120]{1,0:T(8,128)(2,1)} custom-call(bf16[64,5120]{1,0:T(8,128)(2,1)S(1)} %copy-done, f32[1,5120]{1,0:T(1,128)S(1)} %bitcast.1, f32[64,2688]{1,0:T(8,128)S(1)} %get-tuple-element.48.own_right.own, bf16[64,1408]{1,0:T(8,128)(2,1)S(1)} %collective-permute-done.14.refs_0_), custom_call_target="tpu_custom_call" | custom-call | flops 20000000000 | tf_op jit(solution)/shard_map/finish_head/pallas_call | solution.py:418
  39.7 0.0 collective-permute-done.15.refs_2_
  39.7 1.3 %finish_left.1.refs_1_ = bf16[64,5120]{1,0:T(8,128)(2,1)} custom-call(bf16[64,5120]{1,0:T(8,128)(2,1)S(1)} %copy-done, f32[1,5120]{1,0:T(1,128)S(1)} %bitcast.2, f32[64,2432]{1,0:T(8,128)S(1)} %get-tuple-element.49.own, bf16[64,1408]{1,0:T(8,128)(2,1)S(1)} %collective-permute-done.14.refs_0_, ...), custom_call_target="tpu_custom_call", output_to_operand_aliasing={{}: (6, {})} | custom-call | flops 1500000000 | tf_op jit(solution)/shard_map/finish_left/pallas_call | solution.py:428
  40.9 2.1 %collective-permute-done.13.refs_0_ = bf16[64,1792]{1,0:T(8,128)(2,1)S(1)} collective-permute-done((bf16[64,1792]{1,0:T(8,128)(2,1)S(1)}, bf16[64,1792]{1,0:T(8,128)(2,1)S(1)}, u32[]{:S(2)}, u32[]{:S(2)}) %collective-permute-start.13) | collective-permute-done | bytes 229408 | tf_op jit(solution)/shard_map/ppermute | solution.py:295
  43.0 0.8 %finish_right.1 = bf16[64,5120]{1,0:T(8,128)(2,1)} custom-call(bf16[64,5120]{1,0:T(8,128)(2,1)S(1)} %copy-done, f32[1,5120]{1,0:T(1,128)S(1)} %bitcast.3, f32[64,2688]{1,0:T(8,128)S(1)} %get-tuple-element.48.own_right.own, bf16[64,1792]{1,0:T(8,128)(2,1)S(1)} %collective-permute-done.13.refs_0_, ...), custom_call_target="tpu_custom_call", output_to_operand_aliasing={{}: (4, {})} | custom-call | flops 700000000 | tf_op jit(solution)/shard_map/finish_right/pallas_call | solution.py:439
  (2 shorter events, 0.0 us)
Async XLA Ops:
  0.0 19.9 %copy-start.2 = (s32[16,16]{1,0:T(8,128)S(1)}, s32[16,16]{1,0:T(8,128)}, u32[]{:S(2)}) copy-start(s32[16,16]{1,0:T(8,128)} %mask.1) | copy-start | bytes 3076
  0.0 15.2 %collective-permute-start.4 = (bf16[256,5120]{1,0:T(8,128)(2,1)}, bf16[256,5120]{1,0:T(8,128)(2,1)S(1)}, u32[]{:S(2)}, u32[]{:S(2)}) collective-permute-start(bf16[256,5120]{1,0:T(8,128)(2,1)} %weight.2), channel_id=1, source_target_pairs={{0,1},{1,0},{2,3},{3,2},{4,5},{5,4},{6,7},{7,6},{8,9},{9,8},{10,11... | collective-permute-start | bytes 7864328 | tf_op jit(solution)/shard_map/ppermute | solution.py:292
  2.0 8.3 %collective-permute-start = (bf16[512,128]{1,0:T(8,128)(2,1)S(1)}, bf16[512,128]{1,0:T(8,128)(2,1)S(1)}, u32[]{:S(2)}, u32[]{:S(2)}) collective-permute-start(bf16[512,128]{1,0:T(8,128)(2,1)S(1)} %get-tuple-element.29.refs_0_), channel_id=1, source_target_pairs={{0,8},{4,12},{8,0},{12,4},{16,24},{20,28},{24,16},{28,20},{1,9},{5... | collective-permute-start | bytes 393224 | tf_op jit(solution)/shard_map/ppermute | solution.py:278
  4.7 29.5 %collective-permute-start.12 = (bf16[256,2432]{1,0:T(8,128)(2,1)S(1)}, bf16[256,2432]{1,0:T(8,128)(2,1)S(1)}, u32[]{:S(2)}, u32[]{:S(2)}) collective-permute-start(bf16[256,2432]{1,0:T(8,128)(2,1)S(1)} %get-tuple-element.43.left), channel_id=1, source_target_pairs={{0,2},{1,3},{2,0},{3,1},{4,6},{5,7},{6,4},{7,5},{8,10},{9,11},{10,... | collective-permute-start | bytes 3735560 | tf_op jit(solution)/shard_map/ppermute | solution.py:295
  6.2 9.0 %collective-permute-start.3 = (bf16[512,128]{1,0:T(8,128)(2,1)S(1)}, bf16[512,128]{1,0:T(8,128)(2,1)S(1)}, u32[]{:S(2)}, u32[]{:S(2)}) collective-permute-start(bf16[512,128]{1,0:T(8,128)(2,1)S(1)} %get-tuple-element.31), channel_id=1, source_target_pairs={{0,16},{4,20},{8,24},{12,28},{16,0},{20,4},{24,8},{28,12},{1,17},{... | collective-permute-start | bytes 393224 | tf_op jit(solution)/shard_map/ppermute | solution.py:278
  8.8 8.0 %collective-permute-start.2 = (bf16[512,128]{1,0:T(8,128)(2,1)S(1)}, bf16[512,128]{1,0:T(8,128)(2,1)S(1)}, u32[]{:S(2)}, u32[]{:S(2)}) collective-permute-start(bf16[512,128]{1,0:T(8,128)(2,1)S(1)} %get-tuple-element.29.refs_0_), channel_id=1, source_target_pairs={{0,4},{4,0},{8,12},{12,8},{16,20},{20,16},{24,28},{28,24},{1,5},{5... | collective-permute-start | bytes 393224 | tf_op jit(solution)/shard_map/ppermute | solution.py:278
  10.3 8.5 %collective-permute-start.1 = (bf16[512,128]{1,0:T(8,128)(2,1)S(1)}, bf16[512,128]{1,0:T(8,128)(2,1)S(1)}, u32[]{:S(2)}, u32[]{:S(2)}) collective-permute-start(bf16[512,128]{1,0:T(8,128)(2,1)S(1)} %collective-permute-done.refs_3_), channel_id=1, source_target_pairs={{0,4},{4,0},{8,12},{12,8},{16,20},{20,16},{24,28},{28,24},{1,5},{5... | collective-permute-start | bytes 393224 | tf_op jit(solution)/shard_map/ppermute | solution.py:278
  15.3 8.7 %collective-permute-start.7 = (bf16[512,128]{1,0:T(8,128)(2,1)S(1)}, bf16[512,128]{1,0:T(8,128)(2,1)S(1)}, u32[]{:S(2)}, u32[]{:S(2)}) collective-permute-start(bf16[512,128]{1,0:T(8,128)(2,1)S(1)} %collective-permute-done.3.refs_0_.refs_4_), channel_id=1, source_target_pairs={{0,8},{4,12},{8,0},{12,4},{16,24},{20,28},{24,16},{28,20},{1,9},{5... | collective-permute-start | bytes 393224 | tf_op jit(solution)/shard_map/ppermute | solution.py:278
  15.3 8.7 %collective-permute-start.6 = (bf16[512,128]{1,0:T(8,128)(2,1)S(1)}, bf16[512,128]{1,0:T(8,128)(2,1)S(1)}, u32[]{:S(2)}, u32[]{:S(2)}) collective-permute-start(bf16[512,128]{1,0:T(8,128)(2,1)S(1)} %collective-permute-done.3.refs_0_.refs_4_), channel_id=1, source_target_pairs={{0,4},{4,0},{8,12},{12,8},{16,20},{20,16},{24,28},{28,24},{1,5},{5... | collective-permute-start | bytes 393224 | tf_op jit(solution)/shard_map/ppermute | solution.py:278
  16.8 7.4 %collective-permute-start.5 = (bf16[512,128]{1,0:T(8,128)(2,1)S(1)}, bf16[512,128]{1,0:T(8,128)(2,1)S(1)}, u32[]{:S(2)}, u32[]{:S(2)}) collective-permute-start(bf16[512,128]{1,0:T(8,128)(2,1)S(1)} %collective-permute-done.3.refs_0_.refs_4_), channel_id=1, source_target_pairs={{0,12},{4,8},{8,4},{12,0},{16,28},{20,24},{24,20},{28,16},{1,13},{... | collective-permute-start | bytes 393224 | tf_op jit(solution)/shard_map/ppermute | solution.py:278
  18.8 5.2 %collective-permute-start.8 = (bf16[256,128]{1,0:T(8,128)(2,1)S(1)}, bf16[256,128]{1,0:T(8,128)(2,1)S(1)}, u32[]{:S(2)}, u32[]{:S(2)}) collective-permute-start(bf16[256,128]{1,0:T(8,128)(2,1)S(1)} %get-tuple-element.38), channel_id=1, source_target_pairs={{0,16},{4,20},{8,24},{12,28},{16,0},{20,4},{24,8},{28,12},{1,17},{... | collective-permute-start | bytes 196616 | tf_op jit(solution)/shard_map/ppermute | solution.py:278
  25.3 5.1 %collective-permute-start.9 = (bf16[128,128]{1,0:T(8,128)(2,1)S(1)}, bf16[128,128]{1,0:T(8,128)(2,1)S(1)}, u32[]{:S(2)}, u32[]{:S(2)}) collective-permute-start(bf16[128,128]{1,0:T(8,128)(2,1)S(1)} %get-tuple-element.39), channel_id=1, source_target_pairs={{0,17},{1,16},{2,19},{3,18},{4,21},{5,20},{6,23},{7,22},{8,25},{9,... | collective-permute-start | bytes 98312 | tf_op jit(solution)/shard_map/ppermute | solution.py:281
  25.4 5.8 %collective-permute-start.11 = (bf16[128,128]{1,0:T(8,128)(2,1)S(1)}, bf16[128,128]{1,0:T(8,128)(2,1)S(1)}, u32[]{:S(2)}, u32[]{:S(2)}) collective-permute-start(bf16[128,128]{1,0:T(8,128)(2,1)S(1)} %get-tuple-element.41), channel_id=1, source_target_pairs={{0,16},{1,17},{2,18},{3,19},{4,20},{5,21},{6,22},{7,23},{8,24},{9,... | collective-permute-start | bytes 98312 | tf_op jit(solution)/shard_map/ppermute | solution.py:281
  28.2 3.0 %collective-permute-start.10 = (bf16[128,128]{1,0:T(8,128)(2,1)S(1)}, bf16[128,128]{1,0:T(8,128)(2,1)S(1)}, u32[]{:S(2)}, u32[]{:S(2)}) collective-permute-start(bf16[128,128]{1,0:T(8,128)(2,1)S(1)} %get-tuple-element.40), channel_id=1, source_target_pairs={{0,1},{1,0},{2,3},{3,2},{4,5},{5,4},{6,7},{7,6},{8,9},{9,8},{10,11... | collective-permute-start | bytes 98312 | tf_op jit(solution)/shard_map/ppermute | solution.py:281
  31.5 7.5 %collective-permute-start.14 = (bf16[64,1408]{1,0:T(8,128)(2,1)S(1)}, bf16[64,1408]{1,0:T(8,128)(2,1)S(1)}, u32[]{:S(2)}, u32[]{:S(2)}) collective-permute-start(bf16[64,1408]{1,0:T(8,128)(2,1)S(1)} %project_heads.1), channel_id=1, source_target_pairs={{0,2},{1,3},{2,0},{3,1},{4,6},{5,7},{6,4},{7,5},{8,10},{9,11},{10,... | collective-permute-start | bytes 540680 | tf_op jit(solution)/shard_map/ppermute | solution.py:295
  33.1 10.0 %collective-permute-start.13 = (bf16[64,1792]{1,0:T(8,128)(2,1)S(1)}, bf16[64,1792]{1,0:T(8,128)(2,1)S(1)}, u32[]{:S(2)}, u32[]{:S(2)}) collective-permute-start(bf16[64,1792]{1,0:T(8,128)(2,1)S(1)} %project_tails.1), channel_id=1, source_target_pairs={{0,2},{1,3},{2,0},{3,1},{4,6},{5,7},{6,4},{7,5},{8,10},{9,11},{10,... | collective-permute-start | bytes 688136 | tf_op jit(solution)/shard_map/ppermute | solution.py:295
  34.2 4.8 %copy-start = (bf16[64,5120]{1,0:T(8,128)(2,1)S(1)}, bf16[64,5120]{1,0:T(8,128)(2,1)}, u32[]{:S(2)}) copy-start(bf16[64,5120]{1,0:T(8,128)(2,1)} %residual.5) | copy-start | bytes 1966084
  34.2 4.8 %copy-start.1 = (f32[5120]{0:T(1024)S(1)}, f32[5120]{0:T(1024)}, u32[]{:S(2)}) copy-start(f32[5120]{0:T(1024)} %param.12) | copy-start | bytes 61444
  34.2 5.5 %collective-permute-start.15 = (bf16[256,2432]{1,0:T(8,128)(2,1)S(1)}, bf16[256,2432]{1,0:T(8,128)(2,1)S(1)}, u32[]{:S(2)}, u32[]{:S(2)}) collective-permute-start(bf16[256,2432]{1,0:T(8,128)(2,1)S(1)} %collective-permute-done.12.refs_1_), channel_id=1, source_target_pairs={{0,1},{1,0},{2,3},{3,2},{4,5},{5,4},{6,7},{7,6},{8,9},{9,8},{10,11... | collective-permute-start | bytes 3735560 | tf_op jit(solution)/shard_map/ppermute | solution.py:292

commit v7 on v6

--- a/solution.py
+++ b/solution.py
@@ -16,7 +16,7 @@
 BATCH = 4
 LANES = 128
 CUT_NUM, CUT_DEN = 12, 25
-HEAD_NUM, HEAD_DEN = 1, 3
+HEAD_NUM, HEAD_DEN = 9, 20
 
 VMEM = pltpu.MemorySpace.VMEM
 SMEM = pltpu.MemorySpace.SMEM

time: 44 us -> 44 us (level)
  no operation moved by 1% of the time
where the time goes in v7:
time: 44 us; the launch traced here: 43.8 us
  starting transfers between devices  18.9 us (43%)
  waiting for transfers between devices  14.3 us (32%)
  Pallas kernels  10.5 us (24%)
    ppermute x8, starting transfers between devices, swap(): return lax.ppermute(array, 'seq', [(i, i ^ place) for i in range(seq)])  11.9 us
    ppermute x8, waiting for transfers between devices, swap(): return lax.ppermute(array, 'seq', [(i, i ^ place) for i in range(seq)])  7.39 us
    ppermute x3, waiting for transfers between devices, to_chip(): lax.ppermute(array, 'tp', [(t, (t // cores + step) % chips * cores + t %...  6.06 us
    ppermute x3, starting transfers between devices, to_chip(): lax.ppermute(array, 'tp', [(t, (t // cores + step) % chips * cores + t %...  3.68 us
    ppermute x3, starting transfers between devices, across(): lax.ppermute(array, ('seq', 'tp'), [(i * tp + t, (i ^ place) * tp + (t ^...  2.88 us
    pallas_call x2, Pallas kernels, attend_all(): pl.pallas_call(functools.partial(attend_more, first_row, cores, held, las...  1.91 us
    pallas_call x1, Pallas kernels, shards(): pl.pallas_call(functools.partial(pack, half), out_shape=[bf16(2 * rows, p...  1.57 us
    pallas_call x1, Pallas kernels, shards(): pl.pallas_call(stage, out_shape=bf16(width, columns - cut), in_specs=[pl....  1.35 us
  transfers between devices with their start and end apart: 16, of which 7 were waited for; matrix products, arithmetic and copies ran while one was open for 0% of the time, Pallas kernels for 22%

profile of v7, /device:TPU:0, one launch (start us, length us, event | category | flops | bytes accessed | tf_op | source)
XLA Modules:
  0.0 43.8 jit_solution(14812125515804945909)
XLA Ops:
  0.0 0.0 copy-start.2
  0.0 0.5 %collective-permute-start.4 = (bf16[256,5120]{1,0:T(8,128)(2,1)}, bf16[256,5120]{1,0:T(8,128)(2,1)S(1)}, u32[]{:S(2)}, u32[]{:S(2)}) collective-permute-start(bf16[256,5120]{1,0:T(8,128)(2,1)} %weight.2), channel_id=1, source_target_pairs={{0,1},{1,0},{2,3},{3,2},{4,5},{5,4},{6,7},{7,6},{8,9},{9,8},{10,11... | collective-permute-start | bytes 7864328 | tf_op jit(solution)/shard_map/ppermute | solution.py:292
  0.5 1.6 %pack.1 = (bf16[512,128]{1,0:T(8,128)(2,1)S(1)}, bf16[512,128]{1,0:T(8,128)(2,1)S(1)}, bf16[256,128]{1,0:T(8,128)(2,1)S(1)}, bf16[256,128]{1,0:T(8,128)(2,1)S(1)}, bf16[256,2432]{1,0:T(8,128)(2,1)S(1)}) custom-call(bf16[256,256]{1,0:T(8,128)(2,1)} %q.1, bf16[256,256]{1,0:T(8,128)(2,1)} %k.1, bf16[256,256]{1,0:T(8,128)(2,1)} %v.1, bf16[256,5120]{1,0:T(8,128)(2,1)} %weight.2), custom_call_target="tpu_custom_call" | custom-call | flops 1600000000 | tf_op jit(solution)/shard_map/pack/pallas_call | solution.py:304
  2.0 2.6 %collective-permute-start = (bf16[512,128]{1,0:T(8,128)(2,1)S(1)}, bf16[512,128]{1,0:T(8,128)(2,1)S(1)}, u32[]{:S(2)}, u32[]{:S(2)}) collective-permute-start(bf16[512,128]{1,0:T(8,128)(2,1)S(1)} %get-tuple-element.29.refs_0_), channel_id=1, source_target_pairs={{0,8},{4,12},{8,0},{12,4},{16,24},{20,28},{24,16},{28,20},{1,9},{5... | collective-permute-start | bytes 393224 | tf_op jit(solution)/shard_map/ppermute | solution.py:278
  4.7 1.5 %collective-permute-start.12 = (bf16[256,2432]{1,0:T(8,128)(2,1)S(1)}, bf16[256,2432]{1,0:T(8,128)(2,1)S(1)}, u32[]{:S(2)}, u32[]{:S(2)}) collective-permute-start(bf16[256,2432]{1,0:T(8,128)(2,1)S(1)} %get-tuple-element.43.left), channel_id=1, source_target_pairs={{0,2},{1,3},{2,0},{3,1},{4,6},{5,7},{6,4},{7,5},{8,10},{9,11},{10,... | collective-permute-start | bytes 3735560 | tf_op jit(solution)/shard_map/ppermute | solution.py:295
  6.2 2.6 %collective-permute-start.3 = (bf16[512,128]{1,0:T(8,128)(2,1)S(1)}, bf16[512,128]{1,0:T(8,128)(2,1)S(1)}, u32[]{:S(2)}, u32[]{:S(2)}) collective-permute-start(bf16[512,128]{1,0:T(8,128)(2,1)S(1)} %get-tuple-element.31), channel_id=1, source_target_pairs={{0,16},{4,20},{8,24},{12,28},{16,0},{20,4},{24,8},{28,12},{1,17},{... | collective-permute-start | bytes 393224 | tf_op jit(solution)/shard_map/ppermute | solution.py:278
  8.8 1.5 %collective-permute-start.2 = (bf16[512,128]{1,0:T(8,128)(2,1)S(1)}, bf16[512,128]{1,0:T(8,128)(2,1)S(1)}, u32[]{:S(2)}, u32[]{:S(2)}) collective-permute-start(bf16[512,128]{1,0:T(8,128)(2,1)S(1)} %get-tuple-element.29.refs_0_), channel_id=1, source_target_pairs={{0,4},{4,0},{8,12},{12,8},{16,20},{20,16},{24,28},{28,24},{1,5},{5... | collective-permute-start | bytes 393224 | tf_op jit(solution)/shard_map/ppermute | solution.py:278
  10.3 0.0 collective-permute-done.refs_3_
  10.3 0.5 %collective-permute-start.1 = (bf16[512,128]{1,0:T(8,128)(2,1)S(1)}, bf16[512,128]{1,0:T(8,128)(2,1)S(1)}, u32[]{:S(2)}, u32[]{:S(2)}) collective-permute-start(bf16[512,128]{1,0:T(8,128)(2,1)S(1)} %collective-permute-done.refs_3_), channel_id=1, source_target_pairs={{0,4},{4,0},{8,12},{12,8},{16,20},{20,16},{24,28},{28,24},{1,5},{5... | collective-permute-start | bytes 393224 | tf_op jit(solution)/shard_map/ppermute | solution.py:278
  10.8 4.4 %collective-permute-done.3.refs_0_.refs_4_ = bf16[512,128]{1,0:T(8,128)(2,1)S(1)} collective-permute-done((bf16[512,128]{1,0:T(8,128)(2,1)S(1)}, bf16[512,128]{1,0:T(8,128)(2,1)S(1)}, u32[]{:S(2)}, u32[]{:S(2)}) %collective-permute-start.3) | collective-permute-done | bytes 131104 | tf_op jit(solution)/shard_map/ppermute | solution.py:278
  15.2 0.0 collective-permute-done.4.refs_2_.core_weight
  15.3 0.0 collective-permute-start.7
  15.3 1.5 %collective-permute-start.6 = (bf16[512,128]{1,0:T(8,128)(2,1)S(1)}, bf16[512,128]{1,0:T(8,128)(2,1)S(1)}, u32[]{:S(2)}, u32[]{:S(2)}) collective-permute-start(bf16[512,128]{1,0:T(8,128)(2,1)S(1)} %collective-permute-done.3.refs_0_.refs_4_), channel_id=1, source_target_pairs={{0,4},{4,0},{8,12},{12,8},{16,20},{20,16},{24,28},{28,24},{1,5},{5... | collective-permute-start | bytes 393224 | tf_op jit(solution)/shard_map/ppermute | solution.py:278
  16.7 0.0 collective-permute-done.2.refs_2_
  16.8 2.0 %collective-permute-start.5 = (bf16[512,128]{1,0:T(8,128)(2,1)S(1)}, bf16[512,128]{1,0:T(8,128)(2,1)S(1)}, u32[]{:S(2)}, u32[]{:S(2)}) collective-permute-start(bf16[512,128]{1,0:T(8,128)(2,1)S(1)} %collective-permute-done.3.refs_0_.refs_4_), channel_id=1, source_target_pairs={{0,12},{4,8},{8,4},{12,0},{16,28},{20,24},{24,20},{28,16},{1,13},{... | collective-permute-start | bytes 393224 | tf_op jit(solution)/shard_map/ppermute | solution.py:278
  18.7 0.0 collective-permute-done.1.refs_1_
  18.8 1.2 %collective-permute-start.8 = (bf16[256,128]{1,0:T(8,128)(2,1)S(1)}, bf16[256,128]{1,0:T(8,128)(2,1)S(1)}, u32[]{:S(2)}, u32[]{:S(2)}) collective-permute-start(bf16[256,128]{1,0:T(8,128)(2,1)S(1)} %get-tuple-element.38), channel_id=1, source_target_pairs={{0,16},{4,20},{8,24},{12,28},{16,0},{20,4},{24,8},{28,12},{1,17},{... | collective-permute-start | bytes 196616 | tf_op jit(solution)/shard_map/ppermute | solution.py:278
  19.9 0.0 copy-done.2
  19.9 1.3 %attend_near.1 = (f32[64,128]{1,0:T(8,128)S(1)}, f32[256,128]{1,0:T(8,128)S(1)}, f32[256,128]{1,0:T(8,128)S(1)}, f32[256,128]{1,0:T(8,128)S(1)}) custom-call(s32[16,16]{1,0:T(8,128)S(1)} %copy-done.2, bf16[256,128]{1,0:T(8,128)(2,1)S(1)} %get-tuple-element.28.queries, bf16[512,128]{1,0:T(8,128)(2,1)S(1)} %get-tuple-element.29.refs_0_, ...), custom_call_target="tpu_custom_call" | custom-call | flops 1300000000 | tf_op jit(solution)/shard_map/attend_near/pallas_call | solution.py:358
  21.2 2.7 %collective-permute-done.8.queries = bf16[256,128]{1,0:T(8,128)(2,1)S(1)} collective-permute-done((bf16[256,128]{1,0:T(8,128)(2,1)S(1)}, bf16[256,128]{1,0:T(8,128)(2,1)S(1)}, u32[]{:S(2)}, u32[]{:S(2)}) %collective-permute-start.8) | collective-permute-done | bytes 65568 | tf_op jit(solution)/shard_map/ppermute | solution.py:278
  24.0 0.0 collective-permute-done.7.refs_3_.refs_7_
  24.0 0.0 collective-permute-done.6.refs_2_.refs_6_
  24.0 0.2 collective-permute-done.5.refs_1_.refs_5_
  24.2 1.1 %attend_far.1 = (bf16[128,128]{1,0:T(8,128)(2,1)S(1)}, bf16[128,128]{1,0:T(8,128)(2,1)S(1)}) custom-call(f32[64,128]{1,0:T(8,128)S(1)} %get-tuple-element.30.bias, bf16[256,128]{1,0:T(8,128)(2,1)S(1)} %collective-permute-done.8.queries, bf16[512,128]{1,0:T(8,128)(2,1)S(1)} %get-tuple-element.29.refs_0_, bf16[512,128]{1,0:T(8,128)(2,1)S(1)} %collective-permute-done.1.refs_1_, ...), custom_call_target="tpu_custom_call" | custom-call | flops 5000000000 | tf_op jit(solution)/shard_map/attend_far/pallas_call | solution.py:347
  25.3 0.1 collective-permute-start.9
  25.4 2.0 %collective-permute-start.11 = (bf16[128,128]{1,0:T(8,128)(2,1)S(1)}, bf16[128,128]{1,0:T(8,128)(2,1)S(1)}, u32[]{:S(2)}, u32[]{:S(2)}) collective-permute-start(bf16[128,128]{1,0:T(8,128)(2,1)S(1)} %get-tuple-element.41), channel_id=1, source_target_pairs={{0,16},{1,17},{2,18},{3,19},{4,20},{5,21},{6,22},{7,23},{8,24},{9,... | collective-permute-start | bytes 98312 | tf_op jit(solution)/shard_map/ppermute | solution.py:281
  27.4 0.8 %attend_own.1 = (bf16[128,128]{1,0:T(8,128)(2,1)S(1)}, bf16[128,128]{1,0:T(8,128)(2,1)S(1)}) custom-call(f32[64,128]{1,0:T(8,128)S(1)} %get-tuple-element.30.bias, bf16[256,128]{1,0:T(8,128)(2,1)S(1)} %get-tuple-element.28.queries, bf16[512,128]{1,0:T(8,128)(2,1)S(1)} %collective-permute-done.3.refs_0_.refs_4_, ...), custom_call_target="tpu_custom_call" | custom-call | flops 1000000000 | tf_op jit(solution)/shard_map/attend_own/pallas_call | solution.py:347
  28.2 0.8 %collective-permute-start.10 = (bf16[128,128]{1,0:T(8,128)(2,1)S(1)}, bf16[128,128]{1,0:T(8,128)(2,1)S(1)}, u32[]{:S(2)}, u32[]{:S(2)}) collective-permute-start(bf16[128,128]{1,0:T(8,128)(2,1)S(1)} %get-tuple-element.40), channel_id=1, source_target_pairs={{0,1},{1,0},{2,3},{3,2},{4,5},{5,4},{6,7},{7,6},{8,9},{9,8},{10,11... | collective-permute-start | bytes 98312 | tf_op jit(solution)/shard_map/ppermute | solution.py:281
  29.0 1.3 %stage.1.refs_1_.right = bf16[256,2688]{1,0:T(8,128)(2,1)S(1)} custom-call(bf16[256,5120]{1,0:T(8,128)(2,1)} %weight.2), custom_call_target="tpu_custom_call" | custom-call | flops 1300000000 | tf_op jit(solution)/shard_map/stage/pallas_call | solution.py:326
  30.4 0.0 collective-permute-done.9.far_other
  30.4 0.8 %collective-permute-done.11.far = bf16[128,128]{1,0:T(8,128)(2,1)S(1)} collective-permute-done((bf16[128,128]{1,0:T(8,128)(2,1)S(1)}, bf16[128,128]{1,0:T(8,128)(2,1)S(1)}, u32[]{:S(2)}, u32[]{:S(2)}) %collective-permute-start.11) | collective-permute-done | bytes 32800 | tf_op jit(solution)/shard_map/ppermute | solution.py:281
  31.2 0.0 collective-permute-done.10.other
  31.2 0.3 project_heads.1
  31.5 1.2 %collective-permute-start.14 = (bf16[64,1664]{1,0:T(8,128)(2,1)S(1)}, bf16[64,1664]{1,0:T(8,128)(2,1)S(1)}, u32[]{:S(2)}, u32[]{:S(2)}) collective-permute-start(bf16[64,1664]{1,0:T(8,128)(2,1)S(1)} %project_heads.1), channel_id=1, source_target_pairs={{0,2},{1,3},{2,0},{3,1},{4,6},{5,7},{6,4},{7,5},{8,10},{9,11},{10,... | collective-permute-start | bytes 638984 | tf_op jit(solution)/shard_map/ppermute | solution.py:295
  32.7 0.4 project_tails.1
  33.1 1.0 %collective-permute-start.13 = (bf16[64,1536]{1,0:T(8,128)(2,1)S(1)}, bf16[64,1536]{1,0:T(8,128)(2,1)S(1)}, u32[]{:S(2)}, u32[]{:S(2)}) collective-permute-start(bf16[64,1536]{1,0:T(8,128)(2,1)S(1)} %project_tails.1), channel_id=1, source_target_pairs={{0,2},{1,3},{2,0},{3,1},{4,6},{5,7},{6,4},{7,5},{8,10},{9,11},{10,... | collective-permute-start | bytes 589832 | tf_op jit(solution)/shard_map/ppermute | solution.py:295
  34.1 0.1 collective-permute-done.12.refs_1_
  34.2 0.0 copy-start
  34.2 0.0 collective-permute-start.15
  34.2 0.9 %project_own.1 = (f32[64,2432]{1,0:T(8,128)S(1)}, f32[64,2688]{1,0:T(8,128)S(1)}) custom-call(bf16[64,512]{1,0:T(8,128)(2,1)S(1)} %get-tuple-element.47.attended, bf16[256,2432]{1,0:T(8,128)(2,1)S(1)} %get-tuple-element.43.left, bf16[256,2688]{1,0:T(8,128)(2,1)S(1)} %stage.1.refs_1_.right, bf16[256,5120]{1,0:T(8,128)(2,1)S(1)} %collective-permute-done.4.refs_2_.core_weight), custom_call_target="tpu_custom_call" | custom-call | flops 100000000 | tf_op jit(solution)/shard_map/project_own/pallas_call | solution.py:404
  35.1 4.6 %collective-permute-done.14.refs_0_ = bf16[64,1664]{1,0:T(8,128)(2,1)S(1)} collective-permute-done((bf16[64,1664]{1,0:T(8,128)(2,1)S(1)}, bf16[64,1664]{1,0:T(8,128)(2,1)S(1)}, u32[]{:S(2)}, u32[]{:S(2)}) %collective-permute-start.14) | collective-permute-done | bytes 213024 | tf_op jit(solution)/shard_map/ppermute | solution.py:295
  39.7 0.0 copy-done
  39.7 0.0 copy-done.1
  39.7 0.7 %finish_head.1.refs_3_ = bf16[64,5120]{1,0:T(8,128)(2,1)} custom-call(bf16[64,5120]{1,0:T(8,128)(2,1)S(1)} %copy-done, f32[1,5120]{1,0:T(1,128)S(1)} %bitcast.1, f32[64,2688]{1,0:T(8,128)S(1)} %get-tuple-element.48.own_right.own, bf16[64,1664]{1,0:T(8,128)(2,1)S(1)} %collective-permute-done.14.refs_0_), custom_call_target="tpu_custom_call" | custom-call | flops 20000000000 | tf_op jit(solution)/shard_map/finish_head/pallas_call | solution.py:418
  40.4 0.0 collective-permute-done.15.refs_2_
  40.4 1.3 %finish_left.1.refs_1_ = bf16[64,5120]{1,0:T(8,128)(2,1)} custom-call(bf16[64,5120]{1,0:T(8,128)(2,1)S(1)} %copy-done, f32[1,5120]{1,0:T(1,128)S(1)} %bitcast.2, f32[64,2432]{1,0:T(8,128)S(1)} %get-tuple-element.49.own, bf16[64,1664]{1,0:T(8,128)(2,1)S(1)} %collective-permute-done.14.refs_0_, ...), custom_call_target="tpu_custom_call", output_to_operand_aliasing={{}: (6, {})} | custom-call | flops 1500000000 | tf_op jit(solution)/shard_map/finish_left/pallas_call | solution.py:428
  41.7 1.4 %collective-permute-done.13.refs_0_ = bf16[64,1536]{1,0:T(8,128)(2,1)S(1)} collective-permute-done((bf16[64,1536]{1,0:T(8,128)(2,1)S(1)}, bf16[64,1536]{1,0:T(8,128)(2,1)S(1)}, u32[]{:S(2)}, u32[]{:S(2)}) %collective-permute-start.13) | collective-permute-done | bytes 196640 | tf_op jit(solution)/shard_map/ppermute | solution.py:295
  43.1 0.8 %finish_right.1 = bf16[64,5120]{1,0:T(8,128)(2,1)} custom-call(bf16[64,5120]{1,0:T(8,128)(2,1)S(1)} %copy-done, f32[1,5120]{1,0:T(1,128)S(1)} %bitcast.3, f32[64,2688]{1,0:T(8,128)S(1)} %get-tuple-element.48.own_right.own, bf16[64,1536]{1,0:T(8,128)(2,1)S(1)} %collective-permute-done.13.refs_0_, ...), custom_call_target="tpu_custom_call", output_to_operand_aliasing={{}: (4, {})} | custom-call | flops 700000000 | tf_op jit(solution)/shard_map/finish_right/pallas_call | solution.py:439
  (2 shorter events, 0.0 us)
Async XLA Ops:
  0.0 19.9 %copy-start.2 = (s32[16,16]{1,0:T(8,128)S(1)}, s32[16,16]{1,0:T(8,128)}, u32[]{:S(2)}) copy-start(s32[16,16]{1,0:T(8,128)} %mask.1) | copy-start | bytes 3076
  0.0 15.2 %collective-permute-start.4 = (bf16[256,5120]{1,0:T(8,128)(2,1)}, bf16[256,5120]{1,0:T(8,128)(2,1)S(1)}, u32[]{:S(2)}, u32[]{:S(2)}) collective-permute-start(bf16[256,5120]{1,0:T(8,128)(2,1)} %weight.2), channel_id=1, source_target_pairs={{0,1},{1,0},{2,3},{3,2},{4,5},{5,4},{6,7},{7,6},{8,9},{9,8},{10,11... | collective-permute-start | bytes 7864328 | tf_op jit(solution)/shard_map/ppermute | solution.py:292
  2.0 8.3 %collective-permute-start = (bf16[512,128]{1,0:T(8,128)(2,1)S(1)}, bf16[512,128]{1,0:T(8,128)(2,1)S(1)}, u32[]{:S(2)}, u32[]{:S(2)}) collective-permute-start(bf16[512,128]{1,0:T(8,128)(2,1)S(1)} %get-tuple-element.29.refs_0_), channel_id=1, source_target_pairs={{0,8},{4,12},{8,0},{12,4},{16,24},{20,28},{24,16},{28,20},{1,9},{5... | collective-permute-start | bytes 393224 | tf_op jit(solution)/shard_map/ppermute | solution.py:278
  4.7 29.5 %collective-permute-start.12 = (bf16[256,2432]{1,0:T(8,128)(2,1)S(1)}, bf16[256,2432]{1,0:T(8,128)(2,1)S(1)}, u32[]{:S(2)}, u32[]{:S(2)}) collective-permute-start(bf16[256,2432]{1,0:T(8,128)(2,1)S(1)} %get-tuple-element.43.left), channel_id=1, source_target_pairs={{0,2},{1,3},{2,0},{3,1},{4,6},{5,7},{6,4},{7,5},{8,10},{9,11},{10,... | collective-permute-start | bytes 3735560 | tf_op jit(solution)/shard_map/ppermute | solution.py:295
  6.2 9.0 %collective-permute-start.3 = (bf16[512,128]{1,0:T(8,128)(2,1)S(1)}, bf16[512,128]{1,0:T(8,128)(2,1)S(1)}, u32[]{:S(2)}, u32[]{:S(2)}) collective-permute-start(bf16[512,128]{1,0:T(8,128)(2,1)S(1)} %get-tuple-element.31), channel_id=1, source_target_pairs={{0,16},{4,20},{8,24},{12,28},{16,0},{20,4},{24,8},{28,12},{1,17},{... | collective-permute-start | bytes 393224 | tf_op jit(solution)/shard_map/ppermute | solution.py:278
  8.8 8.0 %collective-permute-start.2 = (bf16[512,128]{1,0:T(8,128)(2,1)S(1)}, bf16[512,128]{1,0:T(8,128)(2,1)S(1)}, u32[]{:S(2)}, u32[]{:S(2)}) collective-permute-start(bf16[512,128]{1,0:T(8,128)(2,1)S(1)} %get-tuple-element.29.refs_0_), channel_id=1, source_target_pairs={{0,4},{4,0},{8,12},{12,8},{16,20},{20,16},{24,28},{28,24},{1,5},{5... | collective-permute-start | bytes 393224 | tf_op jit(solution)/shard_map/ppermute | solution.py:278
  10.3 8.5 %collective-permute-start.1 = (bf16[512,128]{1,0:T(8,128)(2,1)S(1)}, bf16[512,128]{1,0:T(8,128)(2,1)S(1)}, u32[]{:S(2)}, u32[]{:S(2)}) collective-permute-start(bf16[512,128]{1,0:T(8,128)(2,1)S(1)} %collective-permute-done.refs_3_), channel_id=1, source_target_pairs={{0,4},{4,0},{8,12},{12,8},{16,20},{20,16},{24,28},{28,24},{1,5},{5... | collective-permute-start | bytes 393224 | tf_op jit(solution)/shard_map/ppermute | solution.py:278
  15.3 8.7 %collective-permute-start.7 = (bf16[512,128]{1,0:T(8,128)(2,1)S(1)}, bf16[512,128]{1,0:T(8,128)(2,1)S(1)}, u32[]{:S(2)}, u32[]{:S(2)}) collective-permute-start(bf16[512,128]{1,0:T(8,128)(2,1)S(1)} %collective-permute-done.3.refs_0_.refs_4_), channel_id=1, source_target_pairs={{0,8},{4,12},{8,0},{12,4},{16,24},{20,28},{24,16},{28,20},{1,9},{5... | collective-permute-start | bytes 393224 | tf_op jit(solution)/shard_map/ppermute | solution.py:278
  15.3 8.7 %collective-permute-start.6 = (bf16[512,128]{1,0:T(8,128)(2,1)S(1)}, bf16[512,128]{1,0:T(8,128)(2,1)S(1)}, u32[]{:S(2)}, u32[]{:S(2)}) collective-permute-start(bf16[512,128]{1,0:T(8,128)(2,1)S(1)} %collective-permute-done.3.refs_0_.refs_4_), channel_id=1, source_target_pairs={{0,4},{4,0},{8,12},{12,8},{16,20},{20,16},{24,28},{28,24},{1,5},{5... | collective-permute-start | bytes 393224 | tf_op jit(solution)/shard_map/ppermute | solution.py:278
  16.8 7.4 %collective-permute-start.5 = (bf16[512,128]{1,0:T(8,128)(2,1)S(1)}, bf16[512,128]{1,0:T(8,128)(2,1)S(1)}, u32[]{:S(2)}, u32[]{:S(2)}) collective-permute-start(bf16[512,128]{1,0:T(8,128)(2,1)S(1)} %collective-permute-done.3.refs_0_.refs_4_), channel_id=1, source_target_pairs={{0,12},{4,8},{8,4},{12,0},{16,28},{20,24},{24,20},{28,16},{1,13},{... | collective-permute-start | bytes 393224 | tf_op jit(solution)/shard_map/ppermute | solution.py:278
  18.8 5.2 %collective-permute-start.8 = (bf16[256,128]{1,0:T(8,128)(2,1)S(1)}, bf16[256,128]{1,0:T(8,128)(2,1)S(1)}, u32[]{:S(2)}, u32[]{:S(2)}) collective-permute-start(bf16[256,128]{1,0:T(8,128)(2,1)S(1)} %get-tuple-element.38), channel_id=1, source_target_pairs={{0,16},{4,20},{8,24},{12,28},{16,0},{20,4},{24,8},{28,12},{1,17},{... | collective-permute-start | bytes 196616 | tf_op jit(solution)/shard_map/ppermute | solution.py:278
  25.3 5.1 %collective-permute-start.9 = (bf16[128,128]{1,0:T(8,128)(2,1)S(1)}, bf16[128,128]{1,0:T(8,128)(2,1)S(1)}, u32[]{:S(2)}, u32[]{:S(2)}) collective-permute-start(bf16[128,128]{1,0:T(8,128)(2,1)S(1)} %get-tuple-element.39), channel_id=1, source_target_pairs={{0,17},{1,16},{2,19},{3,18},{4,21},{5,20},{6,23},{7,22},{8,25},{9,... | collective-permute-start | bytes 98312 | tf_op jit(solution)/shard_map/ppermute | solution.py:281
  25.4 5.8 %collective-permute-start.11 = (bf16[128,128]{1,0:T(8,128)(2,1)S(1)}, bf16[128,128]{1,0:T(8,128)(2,1)S(1)}, u32[]{:S(2)}, u32[]{:S(2)}) collective-permute-start(bf16[128,128]{1,0:T(8,128)(2,1)S(1)} %get-tuple-element.41), channel_id=1, source_target_pairs={{0,16},{1,17},{2,18},{3,19},{4,20},{5,21},{6,22},{7,23},{8,24},{9,... | collective-permute-start | bytes 98312 | tf_op jit(solution)/shard_map/ppermute | solution.py:281
  28.2 3.0 %collective-permute-start.10 = (bf16[128,128]{1,0:T(8,128)(2,1)S(1)}, bf16[128,128]{1,0:T(8,128)(2,1)S(1)}, u32[]{:S(2)}, u32[]{:S(2)}) collective-permute-start(bf16[128,128]{1,0:T(8,128)(2,1)S(1)} %get-tuple-element.40), channel_id=1, source_target_pairs={{0,1},{1,0},{2,3},{3,2},{4,5},{5,4},{6,7},{7,6},{8,9},{9,8},{10,11... | collective-permute-start | bytes 98312 | tf_op jit(solution)/shard_map/ppermute | solution.py:281
  31.5 8.2 %collective-permute-start.14 = (bf16[64,1664]{1,0:T(8,128)(2,1)S(1)}, bf16[64,1664]{1,0:T(8,128)(2,1)S(1)}, u32[]{:S(2)}, u32[]{:S(2)}) collective-permute-start(bf16[64,1664]{1,0:T(8,128)(2,1)S(1)} %project_heads.1), channel_id=1, source_target_pairs={{0,2},{1,3},{2,0},{3,1},{4,6},{5,7},{6,4},{7,5},{8,10},{9,11},{10,... | collective-permute-start | bytes 638984 | tf_op jit(solution)/shard_map/ppermute | solution.py:295
  33.1 10.0 %collective-permute-start.13 = (bf16[64,1536]{1,0:T(8,128)(2,1)S(1)}, bf16[64,1536]{1,0:T(8,128)(2,1)S(1)}, u32[]{:S(2)}, u32[]{:S(2)}) collective-permute-start(bf16[64,1536]{1,0:T(8,128)(2,1)S(1)} %project_tails.1), channel_id=1, source_target_pairs={{0,2},{1,3},{2,0},{3,1},{4,6},{5,7},{6,4},{7,5},{8,10},{9,11},{10,... | collective-permute-start | bytes 589832 | tf_op jit(solution)/shard_map/ppermute | solution.py:295
  34.2 5.5 %copy-start = (bf16[64,5120]{1,0:T(8,128)(2,1)S(1)}, bf16[64,5120]{1,0:T(8,128)(2,1)}, u32[]{:S(2)}) copy-start(bf16[64,5120]{1,0:T(8,128)(2,1)} %residual.5) | copy-start | bytes 1966084
  34.2 5.5 %copy-start.1 = (f32[5120]{0:T(1024)S(1)}, f32[5120]{0:T(1024)}, u32[]{:S(2)}) copy-start(f32[5120]{0:T(1024)} %param.12) | copy-start | bytes 61444
  34.2 6.2 %collective-permute-start.15 = (bf16[256,2432]{1,0:T(8,128)(2,1)S(1)}, bf16[256,2432]{1,0:T(8,128)(2,1)S(1)}, u32[]{:S(2)}, u32[]{:S(2)}) collective-permute-start(bf16[256,2432]{1,0:T(8,128)(2,1)S(1)} %collective-permute-done.12.refs_1_), channel_id=1, source_target_pairs={{0,1},{1,0},{2,3},{3,2},{4,5},{5,4},{6,7},{7,6},{8,9},{9,8},{10,11... | collective-permute-start | bytes 3735560 | tf_op jit(solution)/shard_map/ppermute | solution.py:292

commit v8 on v7

--- a/solution.py
+++ b/solution.py
@@ -15,7 +15,7 @@
 SCORE_SCALE = LOG2E / HD**0.5
 BATCH = 4
 LANES = 128
-CUT_NUM, CUT_DEN = 12, 25
+CUT_NUM, CUT_DEN = 23, 50
 HEAD_NUM, HEAD_DEN = 9, 20
 
 VMEM = pltpu.MemorySpace.VMEM

time: 44 us -> 46.3 us (1.052)
  starting transfers between devices: 18.9 us -> 20.1 us
  waiting for transfers between devices: 14.3 us -> 15.3 us
    ppermute x3, waiting for transfers between devices: 6.06 us -> 8.81 us  [to_chip(): lax.ppermute(array, 'tp', [(t, (t // cores + step) % chips * cores + t %...]
    ppermute x8, waiting for transfers between devices: 7.39 us -> 6.18 us  [swap(): return lax.ppermute(array, 'seq', [(i, i ^ place) for i in range(seq)])]
    ppermute x8, starting transfers between devices: 11.9 us -> 13.1 us  [swap(): return lax.ppermute(array, 'seq', [(i, i ^ place) for i in range(seq)])]
    ppermute x3, waiting for transfers between devices: 0.79 us -> 0.28 us  [across(): lax.ppermute(array, ('seq', 'tp'), [(i * tp + t, (i ^ place) * tp + (t ^...]
  transfers between devices with their start and end apart: 16 -> 16, of which waited for: 7 -> 8; matrix products, arithmetic and copies ran while one was open for 0% -> 0% of each run, Pallas kernels for 22% -> 21%
where the time goes in v8:
time: 46.3 us; the launch traced here: 46.2 us
  starting transfers between devices  20.1 us (43%)
  waiting for transfers between devices  15.3 us (33%)
  Pallas kernels  10.7 us (23%)
    ppermute x8, starting transfers between devices, swap(): return lax.ppermute(array, 'seq', [(i, i ^ place) for i in range(seq)])  13.1 us
    ppermute x3, waiting for transfers between devices, to_chip(): lax.ppermute(array, 'tp', [(t, (t // cores + step) % chips * cores + t %...  8.81 us
    ppermute x8, waiting for transfers between devices, swap(): return lax.ppermute(array, 'seq', [(i, i ^ place) for i in range(seq)])  6.18 us
    ppermute x3, starting transfers between devices, to_chip(): lax.ppermute(array, 'tp', [(t, (t // cores + step) % chips * cores + t %...  3.68 us
    ppermute x3, starting transfers between devices, across(): lax.ppermute(array, ('seq', 'tp'), [(i * tp + t, (i ^ place) * tp + (t ^...  2.88 us
    pallas_call x2, Pallas kernels, attend_all(): pl.pallas_call(functools.partial(attend_more, first_row, cores, held, las...  1.91 us
    pallas_call x1, Pallas kernels, shards(): pl.pallas_call(functools.partial(pack, half), out_shape=[bf16(2 * rows, p...  1.55 us
    pallas_call x1, Pallas kernels, shards(): pl.pallas_call(stage, out_shape=bf16(width, columns - cut), in_specs=[pl....  1.37 us
  transfers between devices with their start and end apart: 16, of which 8 were waited for; matrix products, arithmetic and copies ran while one was open for 0% of the time, Pallas kernels for 21%

profile of v8, /device:TPU:0, one launch (start us, length us, event | category | flops | bytes accessed | tf_op | source)
XLA Modules:
  0.0 46.2 jit_solution(14809757331722685421)
XLA Ops:
  0.0 0.0 copy-start.2
  0.0 0.5 collective-permute-start.4
  0.5 1.5 %pack.1 = (bf16[512,128]{1,0:T(8,128)(2,1)S(1)}, bf16[512,128]{1,0:T(8,128)(2,1)S(1)}, bf16[256,128]{1,0:T(8,128)(2,1)S(1)}, bf16[256,128]{1,0:T(8,128)(2,1)S(1)}, bf16[256,2304]{1,0:T(8,128)(2,1)S(1)}) custom-call(bf16[256,256]{1,0:T(8,128)(2,1)} %q.1, bf16[256,256]{1,0:T(8,128)(2,1)} %k.1, bf16[256,256]{1,0:T(8,128)(2,1)} %v.1, bf16[256,5120]{1,0:T(8,128)(2,1)} %weight.2), custom_call_target="tpu_custom_call" | custom-call | flops 1600000000 | tf_op jit(solution)/shard_map/pack/pallas_call | solution.py:304
  2.0 2.7 %collective-permute-start = (bf16[512,128]{1,0:T(8,128)(2,1)S(1)}, bf16[512,128]{1,0:T(8,128)(2,1)S(1)}, u32[]{:S(2)}, u32[]{:S(2)}) collective-permute-start(bf16[512,128]{1,0:T(8,128)(2,1)S(1)} %get-tuple-element.29.refs_0_), channel_id=1, source_target_pairs={{0,8},{4,12},{8,0},{12,4},{16,24},{20,28},{24,16},{28,20},{1,9},{5... | collective-permute-start | bytes 393224 | tf_op jit(solution)/shard_map/ppermute | solution.py:278
  4.7 2.6 %collective-permute-start.3 = (bf16[512,128]{1,0:T(8,128)(2,1)S(1)}, bf16[512,128]{1,0:T(8,128)(2,1)S(1)}, u32[]{:S(2)}, u32[]{:S(2)}) collective-permute-start(bf16[512,128]{1,0:T(8,128)(2,1)S(1)} %get-tuple-element.31), channel_id=1, source_target_pairs={{0,16},{4,20},{8,24},{12,28},{16,0},{20,4},{24,8},{28,12},{1,17},{... | collective-permute-start | bytes 393224 | tf_op jit(solution)/shard_map/ppermute | solution.py:278
  7.2 1.5 %collective-permute-start.2 = (bf16[512,128]{1,0:T(8,128)(2,1)S(1)}, bf16[512,128]{1,0:T(8,128)(2,1)S(1)}, u32[]{:S(2)}, u32[]{:S(2)}) collective-permute-start(bf16[512,128]{1,0:T(8,128)(2,1)S(1)} %get-tuple-element.29.refs_0_), channel_id=1, source_target_pairs={{0,4},{4,0},{8,12},{12,8},{16,20},{20,16},{24,28},{28,24},{1,5},{5... | collective-permute-start | bytes 393224 | tf_op jit(solution)/shard_map/ppermute | solution.py:278
  8.7 1.5 %collective-permute-start.12 = (bf16[256,2304]{1,0:T(8,128)(2,1)S(1)}, bf16[256,2304]{1,0:T(8,128)(2,1)S(1)}, u32[]{:S(2)}, u32[]{:S(2)}) collective-permute-start(bf16[256,2304]{1,0:T(8,128)(2,1)S(1)} %get-tuple-element.43.left), channel_id=1, source_target_pairs={{0,2},{1,3},{2,0},{3,1},{4,6},{5,7},{6,4},{7,5},{8,10},{9,11},{10,... | collective-permute-start | bytes 3538952 | tf_op jit(solution)/shard_map/ppermute | solution.py:295
  10.3 1.2 %collective-permute-done.refs_3_ = bf16[512,128]{1,0:T(8,128)(2,1)S(1)} collective-permute-done((bf16[512,128]{1,0:T(8,128)(2,1)S(1)}, bf16[512,128]{1,0:T(8,128)(2,1)S(1)}, u32[]{:S(2)}, u32[]{:S(2)}) %collective-permute-start) | collective-permute-done | bytes 131104 | tf_op jit(solution)/shard_map/ppermute | solution.py:278
  11.4 1.8 %collective-permute-start.1 = (bf16[512,128]{1,0:T(8,128)(2,1)S(1)}, bf16[512,128]{1,0:T(8,128)(2,1)S(1)}, u32[]{:S(2)}, u32[]{:S(2)}) collective-permute-start(bf16[512,128]{1,0:T(8,128)(2,1)S(1)} %collective-permute-done.refs_3_), channel_id=1, source_target_pairs={{0,4},{4,0},{8,12},{12,8},{16,20},{20,16},{24,28},{28,24},{1,5},{5... | collective-permute-start | bytes 393224 | tf_op jit(solution)/shard_map/ppermute | solution.py:278
  13.2 0.9 %collective-permute-done.3.refs_0_.refs_4_ = bf16[512,128]{1,0:T(8,128)(2,1)S(1)} collective-permute-done((bf16[512,128]{1,0:T(8,128)(2,1)S(1)}, bf16[512,128]{1,0:T(8,128)(2,1)S(1)}, u32[]{:S(2)}, u32[]{:S(2)}) %collective-permute-start.3) | collective-permute-done | bytes 131104 | tf_op jit(solution)/shard_map/ppermute | solution.py:278
  14.0 0.0 collective-permute-done.4.refs_2_.core_weight
  14.0 0.4 collective-permute-start.7
  14.5 1.5 %collective-permute-start.6 = (bf16[512,128]{1,0:T(8,128)(2,1)S(1)}, bf16[512,128]{1,0:T(8,128)(2,1)S(1)}, u32[]{:S(2)}, u32[]{:S(2)}) collective-permute-start(bf16[512,128]{1,0:T(8,128)(2,1)S(1)} %collective-permute-done.3.refs_0_.refs_4_), channel_id=1, source_target_pairs={{0,4},{4,0},{8,12},{12,8},{16,20},{20,16},{24,28},{28,24},{1,5},{5... | collective-permute-start | bytes 393224 | tf_op jit(solution)/shard_map/ppermute | solution.py:278
  16.0 0.0 collective-permute-done.2.refs_2_
  16.0 1.6 %collective-permute-start.5 = (bf16[512,128]{1,0:T(8,128)(2,1)S(1)}, bf16[512,128]{1,0:T(8,128)(2,1)S(1)}, u32[]{:S(2)}, u32[]{:S(2)}) collective-permute-start(bf16[512,128]{1,0:T(8,128)(2,1)S(1)} %collective-permute-done.3.refs_0_.refs_4_), channel_id=1, source_target_pairs={{0,12},{4,8},{8,4},{12,0},{16,28},{20,24},{24,20},{28,16},{1,13},{... | collective-permute-start | bytes 393224 | tf_op jit(solution)/shard_map/ppermute | solution.py:278
  17.5 0.0 collective-permute-done.1.refs_1_
  17.5 1.1 %collective-permute-start.8 = (bf16[256,128]{1,0:T(8,128)(2,1)S(1)}, bf16[256,128]{1,0:T(8,128)(2,1)S(1)}, u32[]{:S(2)}, u32[]{:S(2)}) collective-permute-start(bf16[256,128]{1,0:T(8,128)(2,1)S(1)} %get-tuple-element.38), channel_id=1, source_target_pairs={{0,16},{4,20},{8,24},{12,28},{16,0},{20,4},{24,8},{28,12},{1,17},{... | collective-permute-start | bytes 196616 | tf_op jit(solution)/shard_map/ppermute | solution.py:278
  18.6 0.0 copy-done.2
  18.6 1.3 %attend_near.1 = (f32[64,128]{1,0:T(8,128)S(1)}, f32[256,128]{1,0:T(8,128)S(1)}, f32[256,128]{1,0:T(8,128)S(1)}, f32[256,128]{1,0:T(8,128)S(1)}) custom-call(s32[16,16]{1,0:T(8,128)S(1)} %copy-done.2, bf16[256,128]{1,0:T(8,128)(2,1)S(1)} %get-tuple-element.28.queries, bf16[512,128]{1,0:T(8,128)(2,1)S(1)} %get-tuple-element.29.refs_0_, ...), custom_call_target="tpu_custom_call" | custom-call | flops 1300000000 | tf_op jit(solution)/shard_map/attend_near/pallas_call | solution.py:358
  20.0 2.8 %collective-permute-done.8.queries = bf16[256,128]{1,0:T(8,128)(2,1)S(1)} collective-permute-done((bf16[256,128]{1,0:T(8,128)(2,1)S(1)}, bf16[256,128]{1,0:T(8,128)(2,1)S(1)}, u32[]{:S(2)}, u32[]{:S(2)}) %collective-permute-start.8) | collective-permute-done | bytes 65568 | tf_op jit(solution)/shard_map/ppermute | solution.py:278
  22.8 0.0 collective-permute-done.7.refs_3_.refs_7_
  22.8 0.0 collective-permute-done.6.refs_2_.refs_6_
  22.8 1.3 %collective-permute-done.5.refs_1_.refs_5_ = bf16[512,128]{1,0:T(8,128)(2,1)S(1)} collective-permute-done((bf16[512,128]{1,0:T(8,128)(2,1)S(1)}, bf16[512,128]{1,0:T(8,128)(2,1)S(1)}, u32[]{:S(2)}, u32[]{:S(2)}) %collective-permute-start.5) | collective-permute-done | bytes 131104 | tf_op jit(solution)/shard_map/ppermute | solution.py:278
  24.1 1.1 %attend_far.1 = (bf16[128,128]{1,0:T(8,128)(2,1)S(1)}, bf16[128,128]{1,0:T(8,128)(2,1)S(1)}) custom-call(f32[64,128]{1,0:T(8,128)S(1)} %get-tuple-element.30.bias, bf16[256,128]{1,0:T(8,128)(2,1)S(1)} %collective-permute-done.8.queries, bf16[512,128]{1,0:T(8,128)(2,1)S(1)} %get-tuple-element.29.refs_0_, bf16[512,128]{1,0:T(8,128)(2,1)S(1)} %collective-permute-done.1.refs_1_, ...), custom_call_target="tpu_custom_call" | custom-call | flops 5000000000 | tf_op jit(solution)/shard_map/attend_far/pallas_call | solution.py:347
  25.2 0.1 collective-permute-start.9
  25.3 0.8 %collective-permute-start.11 = (bf16[128,128]{1,0:T(8,128)(2,1)S(1)}, bf16[128,128]{1,0:T(8,128)(2,1)S(1)}, u32[]{:S(2)}, u32[]{:S(2)}) collective-permute-start(bf16[128,128]{1,0:T(8,128)(2,1)S(1)} %get-tuple-element.41), channel_id=1, source_target_pairs={{0,16},{1,17},{2,18},{3,19},{4,20},{5,21},{6,22},{7,23},{8,24},{9,... | collective-permute-start | bytes 98312 | tf_op jit(solution)/shard_map/ppermute | solution.py:281
  26.1 0.8 %attend_own.1 = (bf16[128,128]{1,0:T(8,128)(2,1)S(1)}, bf16[128,128]{1,0:T(8,128)(2,1)S(1)}) custom-call(f32[64,128]{1,0:T(8,128)S(1)} %get-tuple-element.30.bias, bf16[256,128]{1,0:T(8,128)(2,1)S(1)} %get-tuple-element.28.queries, bf16[512,128]{1,0:T(8,128)(2,1)S(1)} %collective-permute-done.3.refs_0_.refs_4_, ...), custom_call_target="tpu_custom_call" | custom-call | flops 1000000000 | tf_op jit(solution)/shard_map/attend_own/pallas_call | solution.py:347
  26.9 2.0 %collective-permute-start.10 = (bf16[128,128]{1,0:T(8,128)(2,1)S(1)}, bf16[128,128]{1,0:T(8,128)(2,1)S(1)}, u32[]{:S(2)}, u32[]{:S(2)}) collective-permute-start(bf16[128,128]{1,0:T(8,128)(2,1)S(1)} %get-tuple-element.40), channel_id=1, source_target_pairs={{0,1},{1,0},{2,3},{3,2},{4,5},{5,4},{6,7},{7,6},{8,9},{9,8},{10,11... | collective-permute-start | bytes 98312 | tf_op jit(solution)/shard_map/ppermute | solution.py:281
  29.0 1.4 %stage.1.refs_1_.right = bf16[256,2816]{1,0:T(8,128)(2,1)S(1)} custom-call(bf16[256,5120]{1,0:T(8,128)(2,1)} %weight.2), custom_call_target="tpu_custom_call" | custom-call | flops 1300000000 | tf_op jit(solution)/shard_map/stage/pallas_call | solution.py:326
  30.3 0.0 collective-permute-done.9.far_other
  30.4 0.3 collective-permute-done.11.far
  30.6 0.0 collective-permute-done.10.other
  30.7 0.3 project_heads.1
  31.0 1.6 %collective-permute-start.14 = (bf16[64,1664]{1,0:T(8,128)(2,1)S(1)}, bf16[64,1664]{1,0:T(8,128)(2,1)S(1)}, u32[]{:S(2)}, u32[]{:S(2)}) collective-permute-start(bf16[64,1664]{1,0:T(8,128)(2,1)S(1)} %project_heads.1), channel_id=1, source_target_pairs={{0,2},{1,3},{2,0},{3,1},{4,6},{5,7},{6,4},{7,5},{8,10},{9,11},{10,... | collective-permute-start | bytes 638984 | tf_op jit(solution)/shard_map/ppermute | solution.py:295
  32.6 0.4 project_tails.1
  32.9 0.6 %collective-permute-start.13 = (bf16[64,1664]{1,0:T(8,128)(2,1)S(1)}, bf16[64,1664]{1,0:T(8,128)(2,1)S(1)}, u32[]{:S(2)}, u32[]{:S(2)}) collective-permute-start(bf16[64,1664]{1,0:T(8,128)(2,1)S(1)} %project_tails.1), channel_id=1, source_target_pairs={{0,2},{1,3},{2,0},{3,1},{4,6},{5,7},{6,4},{7,5},{8,10},{9,11},{10,... | collective-permute-start | bytes 638984 | tf_op jit(solution)/shard_map/ppermute | solution.py:295
  33.5 4.1 %collective-permute-done.12.refs_1_ = bf16[256,2304]{1,0:T(8,128)(2,1)S(1)} collective-permute-done((bf16[256,2304]{1,0:T(8,128)(2,1)S(1)}, bf16[256,2304]{1,0:T(8,128)(2,1)S(1)}, u32[]{:S(2)}, u32[]{:S(2)}) %collective-permute-start.12) | collective-permute-done | bytes 1179680 | tf_op jit(solution)/shard_map/ppermute | solution.py:295
  37.6 0.0 copy-start
  37.6 0.0 collective-permute-start.15
  37.6 1.0 %project_own.1 = (f32[64,2304]{1,0:T(8,128)S(1)}, f32[64,2816]{1,0:T(8,128)S(1)}) custom-call(bf16[64,512]{1,0:T(8,128)(2,1)S(1)} %get-tuple-element.47.attended, bf16[256,2304]{1,0:T(8,128)(2,1)S(1)} %get-tuple-element.43.left, bf16[256,2816]{1,0:T(8,128)(2,1)S(1)} %stage.1.refs_1_.right, bf16[256,5120]{1,0:T(8,128)(2,1)S(1)} %collective-permute-done.4.refs_2_.core_weight), custom_call_target="tpu_custom_call" | custom-call | flops 100000000 | tf_op jit(solution)/shard_map/project_own/pallas_call | solution.py:404
  38.7 3.5 %collective-permute-done.14.refs_0_ = bf16[64,1664]{1,0:T(8,128)(2,1)S(1)} collective-permute-done((bf16[64,1664]{1,0:T(8,128)(2,1)S(1)}, bf16[64,1664]{1,0:T(8,128)(2,1)S(1)}, u32[]{:S(2)}, u32[]{:S(2)}) %collective-permute-start.14) | collective-permute-done | bytes 213024 | tf_op jit(solution)/shard_map/ppermute | solution.py:295
  42.2 0.0 copy-done
  42.2 0.0 copy-done.1
  42.2 0.7 %finish_head.1.refs_3_ = bf16[64,5120]{1,0:T(8,128)(2,1)} custom-call(bf16[64,5120]{1,0:T(8,128)(2,1)S(1)} %copy-done, f32[1,5120]{1,0:T(1,128)S(1)} %bitcast.1, f32[64,2816]{1,0:T(8,128)S(1)} %get-tuple-element.48.own_right.own, bf16[64,1664]{1,0:T(8,128)(2,1)S(1)} %collective-permute-done.14.refs_0_), custom_call_target="tpu_custom_call" | custom-call | flops 20000000000 | tf_op jit(solution)/shard_map/finish_head/pallas_call | solution.py:418
  42.9 0.0 collective-permute-done.15.refs_2_
  42.9 1.3 %finish_left.1.refs_1_ = bf16[64,5120]{1,0:T(8,128)(2,1)} custom-call(bf16[64,5120]{1,0:T(8,128)(2,1)S(1)} %copy-done, f32[1,5120]{1,0:T(1,128)S(1)} %bitcast.2, f32[64,2304]{1,0:T(8,128)S(1)} %get-tuple-element.49.own, bf16[64,1664]{1,0:T(8,128)(2,1)S(1)} %collective-permute-done.14.refs_0_, ...), custom_call_target="tpu_custom_call", output_to_operand_aliasing={{}: (6, {})} | custom-call | flops 1500000000 | tf_op jit(solution)/shard_map/finish_left/pallas_call | solution.py:428
  44.2 1.2 %collective-permute-done.13.refs_0_ = bf16[64,1664]{1,0:T(8,128)(2,1)S(1)} collective-permute-done((bf16[64,1664]{1,0:T(8,128)(2,1)S(1)}, bf16[64,1664]{1,0:T(8,128)(2,1)S(1)}, u32[]{:S(2)}, u32[]{:S(2)}) %collective-permute-start.13) | collective-permute-done | bytes 213024 | tf_op jit(solution)/shard_map/ppermute | solution.py:295
  45.4 0.8 %finish_right.1 = bf16[64,5120]{1,0:T(8,128)(2,1)} custom-call(bf16[64,5120]{1,0:T(8,128)(2,1)S(1)} %copy-done, f32[1,5120]{1,0:T(1,128)S(1)} %bitcast.3, f32[64,2816]{1,0:T(8,128)S(1)} %get-tuple-element.48.own_right.own, bf16[64,1664]{1,0:T(8,128)(2,1)S(1)} %collective-permute-done.13.refs_0_, ...), custom_call_target="tpu_custom_call", output_to_operand_aliasing={{}: (4, {})} | custom-call | flops 700000000 | tf_op jit(solution)/shard_map/finish_right/pallas_call | solution.py:439
  (2 shorter events, 0.0 us)
Async XLA Ops:
  0.0 18.6 %copy-start.2 = (s32[16,16]{1,0:T(8,128)S(1)}, s32[16,16]{1,0:T(8,128)}, u32[]{:S(2)}) copy-start(s32[16,16]{1,0:T(8,128)} %mask.1) | copy-start | bytes 3076
  0.0 14.0 %collective-permute-start.4 = (bf16[256,5120]{1,0:T(8,128)(2,1)}, bf16[256,5120]{1,0:T(8,128)(2,1)S(1)}, u32[]{:S(2)}, u32[]{:S(2)}) collective-permute-start(bf16[256,5120]{1,0:T(8,128)(2,1)} %weight.2), channel_id=1, source_target_pairs={{0,1},{1,0},{2,3},{3,2},{4,5},{5,4},{6,7},{7,6},{8,9},{9,8},{10,11... | collective-permute-start | bytes 7864328 | tf_op jit(solution)/shard_map/ppermute | solution.py:292
  2.0 9.4 %collective-permute-start = (bf16[512,128]{1,0:T(8,128)(2,1)S(1)}, bf16[512,128]{1,0:T(8,128)(2,1)S(1)}, u32[]{:S(2)}, u32[]{:S(2)}) collective-permute-start(bf16[512,128]{1,0:T(8,128)(2,1)S(1)} %get-tuple-element.29.refs_0_), channel_id=1, source_target_pairs={{0,8},{4,12},{8,0},{12,4},{16,24},{20,28},{24,16},{28,20},{1,9},{5... | collective-permute-start | bytes 393224 | tf_op jit(solution)/shard_map/ppermute | solution.py:278
  4.7 9.4 %collective-permute-start.3 = (bf16[512,128]{1,0:T(8,128)(2,1)S(1)}, bf16[512,128]{1,0:T(8,128)(2,1)S(1)}, u32[]{:S(2)}, u32[]{:S(2)}) collective-permute-start(bf16[512,128]{1,0:T(8,128)(2,1)S(1)} %get-tuple-element.31), channel_id=1, source_target_pairs={{0,16},{4,20},{8,24},{12,28},{16,0},{20,4},{24,8},{28,12},{1,17},{... | collective-permute-start | bytes 393224 | tf_op jit(solution)/shard_map/ppermute | solution.py:278
  7.2 8.7 %collective-permute-start.2 = (bf16[512,128]{1,0:T(8,128)(2,1)S(1)}, bf16[512,128]{1,0:T(8,128)(2,1)S(1)}, u32[]{:S(2)}, u32[]{:S(2)}) collective-permute-start(bf16[512,128]{1,0:T(8,128)(2,1)S(1)} %get-tuple-element.29.refs_0_), channel_id=1, source_target_pairs={{0,4},{4,0},{8,12},{12,8},{16,20},{20,16},{24,28},{28,24},{1,5},{5... | collective-permute-start | bytes 393224 | tf_op jit(solution)/shard_map/ppermute | solution.py:278
  8.7 28.9 %collective-permute-start.12 = (bf16[256,2304]{1,0:T(8,128)(2,1)S(1)}, bf16[256,2304]{1,0:T(8,128)(2,1)S(1)}, u32[]{:S(2)}, u32[]{:S(2)}) collective-permute-start(bf16[256,2304]{1,0:T(8,128)(2,1)S(1)} %get-tuple-element.43.left), channel_id=1, source_target_pairs={{0,2},{1,3},{2,0},{3,1},{4,6},{5,7},{6,4},{7,5},{8,10},{9,11},{10,... | collective-permute-start | bytes 3538952 | tf_op jit(solution)/shard_map/ppermute | solution.py:295
  11.4 6.1 %collective-permute-start.1 = (bf16[512,128]{1,0:T(8,128)(2,1)S(1)}, bf16[512,128]{1,0:T(8,128)(2,1)S(1)}, u32[]{:S(2)}, u32[]{:S(2)}) collective-permute-start(bf16[512,128]{1,0:T(8,128)(2,1)S(1)} %collective-permute-done.refs_3_), channel_id=1, source_target_pairs={{0,4},{4,0},{8,12},{12,8},{16,20},{20,16},{24,28},{28,24},{1,5},{5... | collective-permute-start | bytes 393224 | tf_op jit(solution)/shard_map/ppermute | solution.py:278
  14.0 8.8 %collective-permute-start.7 = (bf16[512,128]{1,0:T(8,128)(2,1)S(1)}, bf16[512,128]{1,0:T(8,128)(2,1)S(1)}, u32[]{:S(2)}, u32[]{:S(2)}) collective-permute-start(bf16[512,128]{1,0:T(8,128)(2,1)S(1)} %collective-permute-done.3.refs_0_.refs_4_), channel_id=1, source_target_pairs={{0,8},{4,12},{8,0},{12,4},{16,24},{20,28},{24,16},{28,20},{1,9},{5... | collective-permute-start | bytes 393224 | tf_op jit(solution)/shard_map/ppermute | solution.py:278
  14.5 8.3 %collective-permute-start.6 = (bf16[512,128]{1,0:T(8,128)(2,1)S(1)}, bf16[512,128]{1,0:T(8,128)(2,1)S(1)}, u32[]{:S(2)}, u32[]{:S(2)}) collective-permute-start(bf16[512,128]{1,0:T(8,128)(2,1)S(1)} %collective-permute-done.3.refs_0_.refs_4_), channel_id=1, source_target_pairs={{0,4},{4,0},{8,12},{12,8},{16,20},{20,16},{24,28},{28,24},{1,5},{5... | collective-permute-start | bytes 393224 | tf_op jit(solution)/shard_map/ppermute | solution.py:278
  16.0 8.2 %collective-permute-start.5 = (bf16[512,128]{1,0:T(8,128)(2,1)S(1)}, bf16[512,128]{1,0:T(8,128)(2,1)S(1)}, u32[]{:S(2)}, u32[]{:S(2)}) collective-permute-start(bf16[512,128]{1,0:T(8,128)(2,1)S(1)} %collective-permute-done.3.refs_0_.refs_4_), channel_id=1, source_target_pairs={{0,12},{4,8},{8,4},{12,0},{16,28},{20,24},{24,20},{28,16},{1,13},{... | collective-permute-start | bytes 393224 | tf_op jit(solution)/shard_map/ppermute | solution.py:278
  17.5 5.3 %collective-permute-start.8 = (bf16[256,128]{1,0:T(8,128)(2,1)S(1)}, bf16[256,128]{1,0:T(8,128)(2,1)S(1)}, u32[]{:S(2)}, u32[]{:S(2)}) collective-permute-start(bf16[256,128]{1,0:T(8,128)(2,1)S(1)} %get-tuple-element.38), channel_id=1, source_target_pairs={{0,16},{4,20},{8,24},{12,28},{16,0},{20,4},{24,8},{28,12},{1,17},{... | collective-permute-start | bytes 196616 | tf_op jit(solution)/shard_map/ppermute | solution.py:278
  25.2 5.1 %collective-permute-start.9 = (bf16[128,128]{1,0:T(8,128)(2,1)S(1)}, bf16[128,128]{1,0:T(8,128)(2,1)S(1)}, u32[]{:S(2)}, u32[]{:S(2)}) collective-permute-start(bf16[128,128]{1,0:T(8,128)(2,1)S(1)} %get-tuple-element.39), channel_id=1, source_target_pairs={{0,17},{1,16},{2,19},{3,18},{4,21},{5,20},{6,23},{7,22},{8,25},{9,... | collective-permute-start | bytes 98312 | tf_op jit(solution)/shard_map/ppermute | solution.py:281
  25.3 5.3 %collective-permute-start.11 = (bf16[128,128]{1,0:T(8,128)(2,1)S(1)}, bf16[128,128]{1,0:T(8,128)(2,1)S(1)}, u32[]{:S(2)}, u32[]{:S(2)}) collective-permute-start(bf16[128,128]{1,0:T(8,128)(2,1)S(1)} %get-tuple-element.41), channel_id=1, source_target_pairs={{0,16},{1,17},{2,18},{3,19},{4,20},{5,21},{6,22},{7,23},{8,24},{9,... | collective-permute-start | bytes 98312 | tf_op jit(solution)/shard_map/ppermute | solution.py:281
  26.9 3.7 %collective-permute-start.10 = (bf16[128,128]{1,0:T(8,128)(2,1)S(1)}, bf16[128,128]{1,0:T(8,128)(2,1)S(1)}, u32[]{:S(2)}, u32[]{:S(2)}) collective-permute-start(bf16[128,128]{1,0:T(8,128)(2,1)S(1)} %get-tuple-element.40), channel_id=1, source_target_pairs={{0,1},{1,0},{2,3},{3,2},{4,5},{5,4},{6,7},{7,6},{8,9},{9,8},{10,11... | collective-permute-start | bytes 98312 | tf_op jit(solution)/shard_map/ppermute | solution.py:281
  31.0 11.2 %collective-permute-start.14 = (bf16[64,1664]{1,0:T(8,128)(2,1)S(1)}, bf16[64,1664]{1,0:T(8,128)(2,1)S(1)}, u32[]{:S(2)}, u32[]{:S(2)}) collective-permute-start(bf16[64,1664]{1,0:T(8,128)(2,1)S(1)} %project_heads.1), channel_id=1, source_target_pairs={{0,2},{1,3},{2,0},{3,1},{4,6},{5,7},{6,4},{7,5},{8,10},{9,11},{10,... | collective-permute-start | bytes 638984 | tf_op jit(solution)/shard_map/ppermute | solution.py:295
  32.9 12.5 %collective-permute-start.13 = (bf16[64,1664]{1,0:T(8,128)(2,1)S(1)}, bf16[64,1664]{1,0:T(8,128)(2,1)S(1)}, u32[]{:S(2)}, u32[]{:S(2)}) collective-permute-start(bf16[64,1664]{1,0:T(8,128)(2,1)S(1)} %project_tails.1), channel_id=1, source_target_pairs={{0,2},{1,3},{2,0},{3,1},{4,6},{5,7},{6,4},{7,5},{8,10},{9,11},{10,... | collective-permute-start | bytes 638984 | tf_op jit(solution)/shard_map/ppermute | solution.py:295
  37.6 4.6 %copy-start = (bf16[64,5120]{1,0:T(8,128)(2,1)S(1)}, bf16[64,5120]{1,0:T(8,128)(2,1)}, u32[]{:S(2)}) copy-start(bf16[64,5120]{1,0:T(8,128)(2,1)} %residual.5) | copy-start | bytes 1966084
  37.6 4.6 %copy-start.1 = (f32[5120]{0:T(1024)S(1)}, f32[5120]{0:T(1024)}, u32[]{:S(2)}) copy-start(f32[5120]{0:T(1024)} %param.12) | copy-start | bytes 61444
  37.6 5.3 %collective-permute-start.15 = (bf16[256,2304]{1,0:T(8,128)(2,1)S(1)}, bf16[256,2304]{1,0:T(8,128)(2,1)S(1)}, u32[]{:S(2)}, u32[]{:S(2)}) collective-permute-start(bf16[256,2304]{1,0:T(8,128)(2,1)S(1)} %collective-permute-done.12.refs_1_), channel_id=1, source_target_pairs={{0,1},{1,0},{2,3},{3,2},{4,5},{5,4},{6,7},{7,6},{8,9},{9,8},{10,11... | collective-permute-start | bytes 3538952 | tf_op jit(solution)/shard_map/ppermute | solution.py:292
